TPU v7x, 32 devices: a whole 2x2x4 slice. The times are simulated.
32 devices in a mesh: groups: 2 (over y), space: 4 (over z), tm: 2 (over x), chan: 2 (over core).
Axes of the slice: x: 2, y: 2, z: 4, core: 2. Of those that a mesh axis runs over, the one named last changes fastest.
Arguments:
- hidden_states: bfloat16 [8, 4, 64, 512], P(('groups', 'tm'), 'space', None, 'chan'), parts along dimension 0, may hold values from -25 to 25
- first_gain: float32 [512], P('chan'), may hold values from 0.1 to 1.9
- second_gain: float32 [512], P('chan'), may hold values from 0.1 to 1.9
- query_weight: bfloat16 [512, 512], replicated, may hold values from -0.4861359 to 0.4861359
- key_weight: bfloat16 [512, 512], replicated, may hold values from -0.4861359 to 0.4861359
- value_weight: bfloat16 [512, 512], replicated, may hold values from -0.25 to 0.25
- out_weight: bfloat16 [512, 512], replicated, may hold values from -0.25 to 0.25
- conv_kernel: bfloat16 [3, 3, 3, 512, 512], P(None, None, None, 'tm', 'chan'), may hold values from -0.0546875 to 0.0546875
Outputs:
- attended: bfloat16 [8, 4, 64, 512], P(('groups', 'tm'), 'space', None, 'chan'), parts along dimension 0
- convolved: bfloat16 [8, 4, 64, 512], P(('groups', 'tm'), 'space', None, 'chan'), parts along dimension 0
There are 2 independent parts, one for each index of `groups`. A program takes and returns all parts, laid end to end along the dimension named above; an argument that names none is the same for every part. Nothing has to cross between parts.
All inputs are finite; a program needn't handle non-finite values.
Results may differ from a plain program's by a relative error of at most 0.012.
The roundings to bfloat16 on the way count: a program that leaves them out, or rounds other values in their place, can miss the bound.
Values may be sent and summed in bfloat16 or wider, within the bound.
No kernel may reach another device: no remote copies, remote signals or barrier semaphores. Data moves between devices by JAX's collectives and lax.ppermute only.
A program may use at most 64 MiB of HBM per device.

v0:
```python
import jax
import jax.numpy as jnp
from jax import lax
from jax.sharding import PartitionSpec as P

D = 512
NGROUP = 32


EPSILON = 1e-06


def shifted_2(x, axis, by):
    peers = lax.axis_size(axis)
    pairs = [(i, i + by) for i in range(peers) if 0 <= i + by < peers]
    return lax.ppermute(x, axis, pairs)


def padded_2(cells, sides, width):
    for axis, dim in sides:
        count = lax.axis_size(axis)
        ends = count - 1
        head = lax.slice_in_dim(cells, 0, width, axis=dim)
        tail = lax.slice_in_dim(cells, cells.shape[dim] - width, cells.shape[dim], axis=dim)
        cells = jnp.concatenate(
            [
                lax.ppermute(tail, axis, [(i, (i + 1) % count) for i in range(ends)]),
                cells,
                lax.ppermute(head, axis, [((i + 1) % count, i) for i in range(ends)]),
            ],
            axis=dim,
        )
    return cells


def normalize(source, gain_vector):
    channels = source.shape[3]
    group_width = D // NGROUP
    grouped = source.reshape(-1, channels // group_width, group_width)
    population = grouped.shape[0] * group_width * lax.axis_size("space") * lax.axis_size("tm")
    group_sums, group_squares = lax.psum(
        (jnp.sum(grouped, axis=(0, 2)), jnp.sum(grouped * grouped, axis=(0, 2))), ("space", "tm")
    )
    centre = group_sums / population
    spread = jnp.maximum(group_squares / population - centre * centre, 0.0)
    shifted = grouped - centre[None, :, None]
    scaled = shifted * lax.rsqrt(spread + EPSILON)[None, :, None]
    return scaled.reshape(source.shape) * gain_vector


def attend(normed, query_weight, key_weight, value_weight, out_weight):
    frame_count, row_count, col_count, channels = normed.shape
    token_count = frame_count * row_count * col_count
    tokens = normed.reshape(token_count, channels)
    halves = lax.all_to_all(tokens, "chan", split_axis=0, concat_axis=1, tiled=True)
    half_rows = halves.shape[0]
    queries = jnp.dot(halves, query_weight, preferred_element_type=jnp.float32).astype(jnp.bfloat16)
    keyed = jnp.dot(halves, key_weight, preferred_element_type=jnp.float32).astype(jnp.bfloat16)
    valued = jnp.dot(halves, value_weight, preferred_element_type=jnp.float32).astype(jnp.bfloat16)
    score_scale = D ** (-0.5)
    running_max = jnp.full((half_rows,), -1e30, jnp.float32)
    key_piece = lax.all_gather(keyed, "space", axis=0, tiled=True)
    value_piece = lax.all_gather(valued, "space", axis=0, tiled=True)
    scores = jnp.dot(queries, key_piece.T, preferred_element_type=jnp.float32) * score_scale
    newest_max = jnp.maximum(running_max, jnp.max(scores, axis=1))
    weights = jnp.exp(scores - newest_max[:, None])
    running_sum = jnp.sum(weights, axis=1)
    accumulated = jnp.dot(
        weights.astype(jnp.bfloat16), value_piece, preferred_element_type=jnp.float32
    )
    mixed = (accumulated / running_sum[:, None]).astype(jnp.bfloat16)
    projected = jnp.dot(mixed, out_weight, preferred_element_type=jnp.float32).astype(jnp.bfloat16)
    returned = lax.all_to_all(projected, "chan", split_axis=1, concat_axis=0, tiled=True)
    return returned.reshape(frame_count, row_count, col_count, channels)


def join_channels(activated):
    return lax.all_gather(activated, "chan", axis=3, tiled=True)


def extend(frames_in):
    earlier = shifted_2(frames_in, "tm", 1)
    timed = jnp.concatenate([earlier, frames_in], axis=0)
    rimmed = padded_2(timed, (("space", 1),), 1)
    return jnp.pad(rimmed, ((0, 0), (0, 0), (1, 1), (0, 0)))


def convolve(activated, conv_kernel):
    frame_count, row_count, col_count = (activated.shape[0], activated.shape[1], activated.shape[2])
    padded = extend(join_channels(activated))
    out_width = conv_kernel.shape[4]
    initial = jnp.zeros((frame_count * row_count * col_count, out_width), jnp.float32)
    running_total = initial
    piece = lax.all_gather(conv_kernel, "tm", axis=3, tiled=True)
    for time_tap in range(3):
        for row_tap in range(3):
            for col_tap in range(3):
                window = padded[
                    time_tap : time_tap + frame_count,
                    row_tap : row_tap + row_count,
                    col_tap : col_tap + col_count,
                ]
                window = window.reshape(frame_count * row_count * col_count, piece.shape[3])
                running_total = running_total + jnp.dot(
                    window, piece[time_tap, row_tap, col_tap], preferred_element_type=jnp.float32
                )
    return running_total.reshape(frame_count, row_count, col_count, out_width).astype(jnp.bfloat16)


def on_device(
    hidden_states,
    first_gain,
    second_gain,
    query_weight,
    key_weight,
    value_weight,
    out_weight,
    conv_kernel,
):
    source = hidden_states.astype(jnp.float32)
    normed = normalize(source, first_gain).astype(jnp.bfloat16)
    attended = attend(normed, query_weight, key_weight, value_weight, out_weight)
    resid = source + attended.astype(jnp.float32)
    activated = jax.nn.silu(normalize(resid, second_gain)).astype(jnp.bfloat16)
    convolved = convolve(activated, conv_kernel)
    return (attended, convolved)


def solution(mesh):
    placed = (
        P(("groups", "tm"), "space", None, "chan"),
        P("chan"),
        P("chan"),
        P(),
        P(),
        P(),
        P(),
        P(None, None, None, "tm", "chan"),
    )
    return jax.shard_map(
        on_device,
        mesh=mesh,
        in_specs=placed,
        out_specs=(
            P(("groups", "tm"), "space", None, "chan"),
            P(("groups", "tm"), "space", None, "chan"),
        ),
        check_vma=False,
    )
```

profile of v0, /device:TPU:0, one launch (start us, length us, event | category | flops | bytes accessed | tf_op | source)
XLA Modules:
  0.0 143.2 jit_solution(14035605134556565551)
XLA Ops:
  7.2 0.7 all-gather.2.cloned.1.call-update
  7.9 0.9 convert_reduce_fusion
  9.2 23.3 %all-reduce.2 = (f32[16]{0:T(128)S(1)}, f32[16]{0:T(128)S(1)}) all-reduce(f32[16]{0:T(128)S(1)} %reduce_sum.62, f32[16]{0:T(128)S(1)} %reduce_sum.59), channel_id=1, replica_groups=mesh['groups'=2,'space'=4,'tm'=2,'chan'=2] {'space','tm'}, use_global_device_ids=true, to_apply=%region_5.0 | all-reduce | flops 32 | bytes 256 | tf_op jit(solution)/shard_map/psum | solution.py:41
  32.8 0.9 fusion.26
  33.7 3.8 %all_to_all.35 = bf16[2,64,256]{2,1,0:T(8,128)(2,1)S(1)} all-to-all(bf16[2,64,256]{2,1,0:T(8,128)(2,1)S(1)} %fusion.26), channel_id=1, replica_groups=mesh['groups'=2,'space'=4,'tm'=2,'chan'=2] {'chan'}, dimensions={0} | all-to-all | bytes 131072 | tf_op jit(solution)/shard_map/all_to_all | solution.py:55
  37.5 0.2 convolution_convert_fusion.2
  37.7 14.3 %all_gather.12 = bf16[256,512]{1,0:T(8,128)(2,1)S(1)} all-gather(bf16[64,512]{1,0:T(8,128)(2,1)S(1)} %convolution_convert_fusion.2), channel_id=1, replica_groups=mesh['groups'=2,'space'=4,'tm'=2,'chan'=2] {'space'}, dimensions={0}, use_global_device_ids=true | all-gather | bytes 327680 | tf_op jit(solution)/shard_map/all_gather | solution.py:62
  52.0 1.2 convolution_convert_fusion.1
  53.3 13.9 %all_gather.13 = bf16[256,512]{1,0:T(8,128)(2,1)S(1)} all-gather(bf16[64,512]{1,0:T(8,128)(2,1)S(1)} %convolution_convert_fusion.1), channel_id=1, replica_groups=mesh['groups'=2,'space'=4,'tm'=2,'chan'=2] {'space'}, dimensions={0}, use_global_device_ids=true | all-gather | bytes 327680 | tf_op jit(solution)/shard_map/all_gather | solution.py:63
  67.2 1.5 %fusion.37 = (f32[64]{0:T(128)S(1)}, f32[64,256]{1,0:T(8,128)S(1)}) fusion(bf16[256,512]{1,0:T(8,128)(2,1)S(1)} %all_gather.12, bf16[64,512]{1,0:T(8,128)(2,1)S(1)} %bitcast.164, bf16[512,512]{1,0:T(8,128)(2,1)} %param.11), kind=kOutput, calls=%fused_computation.104 | convolution fusion | flops 50397120 | bytes 917760 | tf_op jit(solution)/shard_map/dot_general | solution.py:64
  68.9 1.4 convolution_convert_fusion
  70.3 3.8 %all_to_all.36 = bf16[64,2,256]{2,0,1:T(8,128)(2,1)S(1)} all-to-all(bf16[64,2,256]{2,0,1:T(8,128)(2,1)S(1)} %bitcast.193), channel_id=1, replica_groups=mesh['groups'=2,'space'=4,'tm'=2,'chan'=2] {'chan'}, dimensions={1} | all-to-all | bytes 131072 | tf_op jit(solution)/shard_map/all_to_all | solution.py:73
  74.5 17.4 %all-reduce.1 = (f32[16]{0:T(128)S(1)}, f32[16]{0:T(128)S(1)}) all-reduce(f32[16]{0:T(128)S(1)} %reduce_sum.85, f32[16]{0:T(128)S(1)} %reduce_sum.82), channel_id=1, replica_groups=mesh['groups'=2,'space'=4,'tm'=2,'chan'=2] {'space','tm'}, use_global_device_ids=true, to_apply=%region_13.14 | all-reduce | flops 32 | bytes 256 | tf_op jit(solution)/shard_map/psum | solution.py:41
  92.4 1.9 %all_gather.14 = bf16[2,1,64,512]{3,2,1,0:T(8,128)(2,1)S(1)} all-gather(bf16[2,1,64,256]{3,2,1,0:T(8,128)(2,1)S(1)} %multiply_convert_fusion), channel_id=1, replica_groups=mesh['groups'=2,'space'=4,'tm'=2,'chan'=2] {'chan'}, dimensions={3}, use_global_device_ids=true | all-gather | bytes 196608 | tf_op jit(solution)/shard_map/all_gather | solution.py:78
  94.3 4.0 %collective-permute-start = (bf16[2,1,64,512]{3,2,1,0:T(8,128)(2,1)S(1)}, bf16[2,1,64,512]{3,2,1,0:T(8,128)(2,1)S(1)}, u32[]{:S(2)}, u32[]{:S(2)}) collective-permute-start(bf16[2,1,64,512]{3,2,1,0:T(8,128)(2,1)S(1)} %all_gather.14), channel_id=1, source_target_pairs={{0,2},{1,3},{4,6},{5,7},{8,10},{9,11},{12,14},{13,15},{16,18},{17,... | collective-permute-start | bytes 393224 | tf_op jit(solution)/shard_map/ppermute | solution.py:16
  98.3 4.5 %collective-permute-done = bf16[2,1,64,512]{3,2,1,0:T(8,128)(2,1)S(1)} collective-permute-done((bf16[2,1,64,512]{3,2,1,0:T(8,128)(2,1)S(1)}, bf16[2,1,64,512]{3,2,1,0:T(8,128)(2,1)S(1)}, u32[]{:S(2)}, u32[]{:S(2)}) %collective-permute-start) | collective-permute-done | bytes 131104 | tf_op jit(solution)/shard_map/ppermute | solution.py:16
  102.8 2.5 %collective-permute-start.1 = (bf16[4,1,64,512]{3,2,1,0:T(8,128)(2,1)S(1)}, bf16[4,1,64,512]{3,2,1,0:T(8,128)(2,1)S(1)}, u32[]{:S(2)}, u32[]{:S(2)}) collective-permute-start(bf16[4,1,64,512]{3,2,1,0:T(8,128)(2,1)S(1)} %constant_dynamic-update-slice_fusion), channel_id=1, source_target_pairs={{0,4},{4,8},{8,12},{1,5},{5,9},{9,13},{2,6},{6,10},{10,14},{3,7},{... | collective-permute-start | bytes 786440 | tf_op jit(solution)/shard_map/ppermute | solution.py:27
  105.3 1.3 collective-permute-start.2
  106.6 3.7 %collective-permute-done.1 = bf16[4,1,64,512]{3,2,1,0:T(8,128)(2,1)S(1)} collective-permute-done((bf16[4,1,64,512]{3,2,1,0:T(8,128)(2,1)S(1)}, bf16[4,1,64,512]{3,2,1,0:T(8,128)(2,1)S(1)}, u32[]{:S(2)}, u32[]{:S(2)}) %collective-permute-start.1) | collective-permute-done | bytes 262176 | tf_op jit(solution)/shard_map/ppermute | solution.py:27
  110.3 4.1 %collective-permute-done.2 = bf16[4,1,64,512]{3,2,1,0:T(8,128)(2,1)S(1)} collective-permute-done((bf16[4,1,64,512]{3,2,1,0:T(8,128)(2,1)S(1)}, bf16[4,1,64,512]{3,2,1,0:T(8,128)(2,1)S(1)}, u32[]{:S(2)}, u32[]{:S(2)}) %collective-permute-start.2) | collective-permute-done | bytes 262176 | tf_op jit(solution)/shard_map/ppermute | solution.py:29
  114.4 0.2 fusion.13
  114.7 0.7 fusion.36
  115.4 0.8 fusion.35
  116.2 0.4 fusion.34
  116.6 1.3 fusion.20
  117.9 1.7 %fusion.19 = f32[128,256]{1,0:T(8,128)S(1)} fusion(bf16[128,512]{1,0:T(8,128)(2,1)S(1)} %bitcast.184, bf16[3,3,3,512,256]{4,3,2,1,0:T(8,128)(2,1)} %all-gather.2.cloned.1.call-done), kind=kOutput, calls=%fused_computation.69 | convolution fusion | flops 33554432 | bytes 524288 | tf_op jit(solution)/shard_map/dot_general | solution.py:104
  119.6 1.1 fusion.18
  120.8 1.1 fusion.17
  121.9 1.1 fusion.16
  123.1 1.2 fusion.15
  124.3 1.1 fusion.14
  125.4 1.1 convolution_add_fusion.19
  126.6 1.1 convolution_add_fusion.18
  127.7 1.1 convolution_add_fusion.17
  128.8 1.1 fusion.6
  130.0 1.1 convolution_add_fusion.15
  131.2 1.1 fusion.5
  132.5 0.2 fusion.4
  132.7 0.2 convolution_add_fusion.11
  132.9 0.2 convolution_add_fusion.10
  133.1 0.2 convolution_add_fusion.9
  133.3 0.2 convolution_add_fusion.8
  133.5 0.2 fusion.3
  133.7 0.2 convolution_add_fusion.6
  134.1 0.2 convolution_add_fusion.4
  134.5 0.2 convolution_add_fusion.2
  134.9 0.8 fusion.8
  135.7 0.6 copy.24
  (49 shorter events, 2.6 us)
Async XLA Ops:
  7.2 30.3 %copy-start = (bf16[512,512]{1,0:T(8,128)(2,1)S(1)}, bf16[512,512]{1,0:T(8,128)(2,1)}, u32[]{:S(2)}) copy-start(bf16[512,512]{1,0:T(8,128)(2,1)} %param.12) | copy-start | bytes 1572868
  7.2 66.9 %copy-start.2 = (bf16[2,1,64,256]{3,2,1,0:T(8,128)(2,1)S(1)}, bf16[2,1,64,256]{3,2,1,0:T(8,128)(2,1)}, u32[]{:S(2)}) copy-start(bf16[2,1,64,256]{3,2,1,0:T(8,128)(2,1)} %param.8) | copy-start | bytes 196612
  7.2 85.1 %copy-start.7 = (f32[256]{0:T(256)S(1)}, f32[256]{0:T(256)}, u32[]{:S(2)}) copy-start(f32[256]{0:T(256)} %param.10) | copy-start | bytes 3076
  7.2 109.4 %all-gather.2.cloned.1.call-start = ((), (), s32[]{:S(2)}) async-start(), calls=%async_computation.2 | async-start | bytes 10616832 | tf_op jit(solution)/shard_map/all_gather | solution.py:94
  94.3 8.5 %collective-permute-start = (bf16[2,1,64,512]{3,2,1,0:T(8,128)(2,1)S(1)}, bf16[2,1,64,512]{3,2,1,0:T(8,128)(2,1)S(1)}, u32[]{:S(2)}, u32[]{:S(2)}) collective-permute-start(bf16[2,1,64,512]{3,2,1,0:T(8,128)(2,1)S(1)} %all_gather.14), channel_id=1, source_target_pairs={{0,2},{1,3},{4,6},{5,7},{8,10},{9,11},{12,14},{13,15},{16,18},{17,... | collective-permute-start | bytes 393224 | tf_op jit(solution)/shard_map/ppermute | solution.py:16
  102.8 7.5 %collective-permute-start.1 = (bf16[4,1,64,512]{3,2,1,0:T(8,128)(2,1)S(1)}, bf16[4,1,64,512]{3,2,1,0:T(8,128)(2,1)S(1)}, u32[]{:S(2)}, u32[]{:S(2)}) collective-permute-start(bf16[4,1,64,512]{3,2,1,0:T(8,128)(2,1)S(1)} %constant_dynamic-update-slice_fusion), channel_id=1, source_target_pairs={{0,4},{4,8},{8,12},{1,5},{5,9},{9,13},{2,6},{6,10},{10,14},{3,7},{... | collective-permute-start | bytes 786440 | tf_op jit(solution)/shard_map/ppermute | solution.py:27
  105.3 9.1 %collective-permute-start.2 = (bf16[4,1,64,512]{3,2,1,0:T(8,128)(2,1)S(1)}, bf16[4,1,64,512]{3,2,1,0:T(8,128)(2,1)S(1)}, u32[]{:S(2)}, u32[]{:S(2)}) collective-permute-start(bf16[4,1,64,512]{3,2,1,0:T(8,128)(2,1)S(1)} %constant_dynamic-update-slice_fusion), channel_id=1, source_target_pairs={{4,0},{8,4},{12,8},{5,1},{9,5},{13,9},{6,2},{10,6},{14,10},{7,3},{... | collective-permute-start | bytes 786440 | tf_op jit(solution)/shard_map/ppermute | solution.py:29
  116.6 14.5 %copy-start.1 = (bf16[3,3,3,512,256]{4,3,2,1,0:T(8,128)(2,1)S(1)}, bf16[3,3,3,512,256]{4,3,2,1,0:T(8,128)(2,1)}, u32[]{:S(2)}) copy-start(bf16[3,3,3,512,256]{4,3,2,1,0:T(8,128)(2,1)} %all-gather.2.cloned.1.call-done) | copy-start | bytes 21233668
  116.6 15.8 %copy-start.6 = (bf16[2,1,64,512]{3,2,1,0:T(8,128)(2,1)S(1)}, bf16[2,1,64,512]{3,2,1,0:T(8,128)(2,1)}, u32[]{:S(2)}) copy-start(bf16[2,1,64,512]{3,2,1,0:T(8,128)(2,1)} %get-tuple-element.38) | copy-start | bytes 393220
  116.6 16.8 %copy-start.5 = (bf16[2,1,64,512]{3,2,1,0:T(8,128)(2,1)S(1)}, bf16[2,1,64,512]{3,2,1,0:T(8,128)(2,1)}, u32[]{:S(2)}) copy-start(bf16[2,1,64,512]{3,2,1,0:T(8,128)(2,1)} %get-tuple-element.35) | copy-start | bytes 393220
  116.6 17.2 %copy-start.4 = (bf16[2,1,64,512]{3,2,1,0:T(8,128)(2,1)S(1)}, bf16[2,1,64,512]{3,2,1,0:T(8,128)(2,1)}, u32[]{:S(2)}) copy-start(bf16[2,1,64,512]{3,2,1,0:T(8,128)(2,1)} %get-tuple-element.37) | copy-start | bytes 393220
  123.1 11.8 %copy-start.3 = (bf16[2,1,64,512]{3,2,1,0:T(8,128)(2,1)S(1)}, bf16[2,1,64,512]{3,2,1,0:T(8,128)(2,1)}, u32[]{:S(2)}) copy-start(bf16[2,1,64,512]{3,2,1,0:T(8,128)(2,1)} %get-tuple-element.34) | copy-start | bytes 393220
Sparse Core Ops, SparseCore 0:
  9.6 92.6 all-gather.1
where the time goes:
time: 144 us; the launch traced here: 143 us
  blocking collectives  78.4 us (54%)
  matrix products  23.1 us (16%)
  between operations  14.5 us (10%)
  waiting for transfers between devices  13 us (9%)
  starting transfers between devices  7.81 us (5%)
  local copies, waits for them, and re-layouts  3.52 us (2%)
  other arithmetic  2.8 us (2%)
    psum x2, blocking collectives, normalize(): lax.psum((jnp.sum(grouped, axis=(0, 2)), jnp.sum(grouped * grouped, axis=...  40.8 us
    dot_general x27, matrix products, convolve(): jnp.dot(window, piece[time_tap, row_tap, col_tap], preferred_element_type...  18.8 us
    all_gather x1, blocking collectives, attend(): key_piece = lax.all_gather(keyed, 'space', axis=0, tiled=True)  14.3 us
    all_gather x1, blocking collectives, attend(): value_piece = lax.all_gather(valued, 'space', axis=0, tiled=True)  13.9 us
    ppermute x1, waiting for transfers between devices, shifted_2(): return lax.ppermute(x, axis, pairs)  4.48 us
    ppermute x1, waiting for transfers between devices, padded_2(): lax.ppermute(head, axis, [((i + 1) % count, i) for i in range(ends)])  4.13 us
    ppermute x1, starting transfers between devices, shifted_2(): return lax.ppermute(x, axis, pairs)  3.96 us
    all_to_all x1, blocking collectives, attend(): lax.all_to_all(projected, 'chan', split_axis=1, concat_axis=0, tiled=True)  3.79 us
  transfers between devices with their start and end apart: 4, of which 3 were waited for; matrix products, arithmetic and copies ran while one was open for 7% of the time, Pallas kernels for 0%

commit v1 on v0

--- a/solution.py
+++ b/solution.py
@@ -1,6 +1,10 @@
+import functools
+
 import jax
 import jax.numpy as jnp
 from jax import lax
+from jax.experimental import pallas as pl
+from jax.experimental.pallas import tpu as pltpu
 from jax.sharding import PartitionSpec as P
 
 D = 512
@@ -107,7 +111,7 @@
     return running_total.reshape(frame_count, row_count, col_count, out_width).astype(jnp.bfloat16)
 
 
-def on_device(
+def split_plan(
     hidden_states,
     first_gain,
     second_gain,
@@ -124,6 +128,194 @@
     activated = jax.nn.silu(normalize(resid, second_gain)).astype(jnp.bfloat16)
     convolved = convolve(activated, conv_kernel)
     return (attended, convolved)
+
+
+def exchange(x, axes, step):
+    peers = lax.axis_size(axes)
+    return lax.ppermute(x, axes, [(i, i ^ step) for i in range(peers)])
+
+
+def pack_kernel(*refs):
+    piece_refs, out_ref = refs[:-1], refs[-1]
+    frames, cols, channels = piece_refs[0].shape
+    blocks = out_ref.shape[0] // frames
+    rows = len(piece_refs) // blocks
+    for block in range(blocks):
+        for row in range(rows):
+            for frame in range(frames):
+                out_ref[block * frames + frame, row] = piece_refs[row * blocks + block][frame]
+
+
+def group_means(sums, count):
+    channels = sums.shape[1]
+    width = D // NGROUP
+    left = lax.broadcasted_iota(jnp.int32, (channels, channels), 0) // width
+    right = lax.broadcasted_iota(jnp.int32, (channels, channels), 1) // width
+    member = (left == right).astype(jnp.float32)
+    return jnp.dot(sums, member, precision=lax.Precision.HIGHEST, preferred_element_type=jnp.float32) / count
+
+
+def moments(values, count):
+    tokens, channels = values.shape
+    parts = values.reshape(tokens // 8, 8, channels)
+    sums = jnp.sum(jnp.sum(parts, axis=0), axis=0, keepdims=True)
+    squares = jnp.sum(jnp.sum(parts * parts, axis=0), axis=0, keepdims=True)
+    stacked = jnp.concatenate([sums, squares, jnp.zeros((6, channels), jnp.float32)], axis=0)
+    means = group_means(stacked, count)
+    centre = means[0:1]
+    spread = jnp.maximum(means[1:2] - centre * centre, 0.0)
+    return centre, lax.rsqrt(spread + EPSILON)
+
+
+def main_kernel(
+    mine_ref, other_ref, gains_ref, other_gains_ref, query_ref, key_ref, value_ref, out_weight_ref, kernel_ref,
+    attended_ref, keep_ref, send_ref,
+    normed, queries, keyed, valued, resid, activated,
+):
+    frames, rows, cols, channels = mine_ref.shape
+    tokens = frames * rows * cols
+    frame_tokens = rows * cols
+    own_frames = attended_ref.shape[0]
+    space = lax.axis_index("space")
+    block = lax.axis_index("tm")
+    half = lax.axis_index("chan")
+    width = D // NGROUP
+    count = tokens * width
+    own_rows = pl.ds(pl.multiple_of(half * channels, channels), channels)
+    other_rows = pl.ds(pl.multiple_of((1 - half) * channels, channels), channels)
+
+    for side, (ref, gain_ref) in enumerate(((mine_ref, gains_ref), (other_ref, other_gains_ref))):
+        values = ref[...].reshape(tokens, channels).astype(jnp.float32)
+        centre, scale = moments(values, count)
+        normed[side] = ((values - centre) * scale * gain_ref[0:1, :]).astype(jnp.bfloat16)
+
+    for weight_ref, target in ((query_ref, queries), (key_ref, keyed), (value_ref, valued)):
+        target[...] = (
+            jnp.dot(normed[0], weight_ref[own_rows, :], preferred_element_type=jnp.float32)
+            + jnp.dot(normed[1], weight_ref[other_rows, :], preferred_element_type=jnp.float32)
+        ).astype(jnp.bfloat16)
+
+    in_channels = kernel_ref.shape[3]
+    in_cols = pl.ds(pl.multiple_of(block * in_channels, in_channels), in_channels)
+    own_cols = pl.ds(pl.multiple_of(half * channels, channels), channels)
+    mine_in = block == half
+    for frame in range(frames):
+        at = slice(frame * frame_tokens, (frame + 1) * frame_tokens)
+        scores = lax.dot_general(
+            queries[at, :], keyed[at, :], (((1,), (1,)), ((), ())), preferred_element_type=jnp.float32
+        ) * (D ** (-0.5))
+        weights = jnp.exp(scores - jnp.max(scores, axis=1, keepdims=True))
+        mass = jnp.sum(weights, axis=1, keepdims=True)
+        mixed = jnp.dot(weights.astype(jnp.bfloat16), valued[at, :], preferred_element_type=jnp.float32)
+        mixed = (mixed / mass).astype(jnp.bfloat16)
+        if frame < own_frames:
+            attended_ref[frame, 0] = jnp.dot(
+                mixed[:cols], out_weight_ref[:, own_cols], preferred_element_type=jnp.float32
+            ).astype(jnp.bfloat16)
+        projected = jnp.dot(
+            mixed, out_weight_ref[:, in_cols], preferred_element_type=jnp.float32
+        ).astype(jnp.bfloat16)
+        source = jnp.where(mine_in, mine_ref[frame].astype(jnp.float32), other_ref[frame].astype(jnp.float32))
+        resid[frame] = source + projected.astype(jnp.float32).reshape(rows, cols, in_channels)
+
+    centre, scale = moments(resid[...].reshape(tokens, in_channels), count)
+    gain = jnp.where(mine_in, gains_ref[1:2, :], other_gains_ref[1:2, :])
+    for tap in range(3):
+        row = space + (tap - 1)
+        inside = jnp.logical_and(row >= 0, row < rows)
+        place = jnp.where(inside, space ^ row, 0)
+        for frame in range(frames):
+            relative = ((frame // own_frames) ^ block) * own_frames + frame % own_frames
+            values = (resid[relative, place] - centre) * scale * gain
+            values = values / (1.0 + jnp.exp(-values))
+            activated[tap, frame] = jnp.where(inside, values, 0.0).astype(jnp.bfloat16)
+
+    out_channels = kernel_ref.shape[4]
+    columns = [None] * 3
+    for col_tap in range(3):
+        total = None
+        for time_tap in (2, 1, 0):
+            late = 2 - time_tap
+            shorter = None
+            for row_tap in range(3):
+                window = activated[row_tap, 0 : frames - late].reshape((frames - late) * cols, in_channels)
+                term = jnp.dot(window, kernel_ref[time_tap, row_tap, col_tap], preferred_element_type=jnp.float32)
+                shorter = term if shorter is None else shorter + term
+            if late:
+                shorter = jnp.concatenate([jnp.zeros((late * cols, out_channels), jnp.float32), shorter], axis=0)
+            total = shorter if total is None else total + shorter
+        columns[col_tap] = total
+    place = lax.broadcasted_iota(jnp.int32, (frames * cols, out_channels), 0) % cols
+    left = jnp.where(place == 0, 0.0, pltpu.roll(columns[0], 1, 0))
+    right = jnp.where(place == cols - 1, 0.0, pltpu.roll(columns[2], frames * cols - 1, 0))
+    summed = (columns[1] + left + right).reshape(frames, cols, out_channels)
+    blocks = frames // own_frames
+    for index in range(blocks):
+        piece = summed[index * own_frames : (index + 1) * own_frames]
+
+        @pl.when(index == block)
+        def _():
+            keep_ref[...] = piece
+
+        @pl.when(index != block)
+        def _():
+            send_ref[(index ^ block) - 1] = piece.astype(jnp.bfloat16)
+
+
+def gathered_plan(
+    hidden_states, first_gain, second_gain, query_weight, key_weight, value_weight, out_weight, conv_kernel
+):
+    frames, _, cols, channels = hidden_states.shape
+    rows, blocks = lax.axis_size("space"), lax.axis_size("tm")
+    own = hidden_states.reshape(frames, cols, channels)
+    gains = jnp.stack([first_gain, second_gain])
+    other_gains = exchange(gains, "chan", 1)
+    pieces = [own] + [exchange(own, ("space", "tm"), step) for step in range(1, rows * blocks)]
+    mine = pl.pallas_call(
+        pack_kernel,
+        out_shape=jax.ShapeDtypeStruct((blocks * frames, rows, cols, channels), jnp.bfloat16),
+        name="pack",
+    )(*pieces)
+    other = exchange(mine, "chan", 1)
+    out_channels = conv_kernel.shape[4]
+    in_channels = conv_kernel.shape[3]
+    tokens = blocks * frames * rows * cols
+    attended, keep, send = pl.pallas_call(
+        main_kernel,
+        out_shape=(
+            jax.ShapeDtypeStruct((frames, 1, cols, channels), jnp.bfloat16),
+            jax.ShapeDtypeStruct((frames, cols, out_channels), jnp.float32),
+            jax.ShapeDtypeStruct((blocks - 1, frames, cols, out_channels), jnp.bfloat16),
+        ),
+        scratch_shapes=[
+            pltpu.VMEM((2, tokens, channels), jnp.bfloat16),
+            pltpu.VMEM((tokens, D), jnp.bfloat16),
+            pltpu.VMEM((tokens, D), jnp.bfloat16),
+            pltpu.VMEM((tokens, D), jnp.bfloat16),
+            pltpu.VMEM((blocks * frames, rows, cols, in_channels), jnp.float32),
+            pltpu.VMEM((3, blocks * frames, cols, in_channels), jnp.bfloat16),
+        ],
+        compiler_params=pltpu.CompilerParams(vmem_limit_bytes=40 * 1024 * 1024),
+        name="block",
+    )(mine, other, gains, other_gains, query_weight, key_weight, value_weight, out_weight, conv_kernel)
+    total = keep
+    for step in range(1, blocks):
+        total = total + exchange(send[step - 1], "tm", step).astype(jnp.float32)
+    return attended, total.astype(jnp.bfloat16).reshape(frames, 1, cols, out_channels)
+
+
+def power_of_two(count):
+    return count & (count - 1) == 0
+
+
+def on_device(hidden_states, *others):
+    frames, rows, cols, channels = hidden_states.shape
+    spaces, blocks = lax.axis_size("space"), lax.axis_size("tm")
+    tokens = frames * blocks * spaces * rows * cols
+    fits = tokens * D <= 2 ** 20 and rows == 1 and lax.axis_size("chan") == 2 and blocks == 2
+    if fits and power_of_two(spaces):
+        return gathered_plan(hidden_states, *others)
+    return split_plan(hidden_states, *others)
 
 
 def solution(mesh):

time: 144 us -> 43.2 us (0.30)
  blocking collectives: 78.4 us -> 0 us
  matrix products: 23.1 us -> 0 us
  between operations: 14.5 us -> 0.67 us
  Pallas kernels: 0 us -> 8.73 us
  starting transfers between devices: 7.81 us -> 13.8 us
  local copies, waits for them, and re-layouts: 3.52 us -> 8.45 us
  waiting for transfers between devices: 13 us -> 9.7 us
  other arithmetic: 2.8 us -> 1.35 us
    psum x2 -> x0, blocking collectives: 40.8 us -> none  [normalize(): lax.psum((jnp.sum(grouped, axis=(0, 2)), jnp.sum(grouped * grouped, axis=...]
    all_gather x3 -> x0, blocking collectives: 30.1 us -> none  [the longest x1 14.3 us: attend(): key_piece = lax.all_gather(keyed, 'space', axis=0, tiled=True)]
    dot_general x31 -> x0, matrix products: 23.1 us -> none  [the longest x27 18.8 us: convolve(): jnp.dot(window, piece[time_tap, row_tap, col_tap], preferred_element_type...]
    pallas_call x0 -> x2, Pallas kernels: none -> 8.73 us  [the longest x1 6.83 us: gathered_plan(): pl.pallas_call(main_kernel, out_shape=(jax.ShapeDtypeStruct((frames, 1, c...]
    unnamed x18 -> x26, local copies, waits for them, and re-layouts: 0.68 us -> 8.45 us
    all_to_all x2 -> x0, blocking collectives: 7.58 us -> none  [the longest x1 3.79 us: attend(): lax.all_to_all(projected, 'chan', split_axis=1, concat_axis=0, tiled=True)]
    ppermute x3 -> x10, starting transfers between devices: 7.77 us -> 13.8 us  [exchange(): return lax.ppermute(x, axes, [(i, i ^ step) for i in range(peers)])]
    ppermute x3 -> x10, waiting for transfers between devices: 12.3 us -> 9.7 us  [exchange(): return lax.ppermute(x, axes, [(i, i ^ step) for i in range(peers)])]
  transfers between devices with their start and end apart: 4 -> 10, of which waited for: 3 -> 7; matrix products, arithmetic and copies ran while one was open for 7% -> 2% of each run, Pallas kernels for 0% -> 0%
where the time goes in v1:
time: 43.2 us; the launch traced here: 42.7 us
  starting transfers between devices  13.8 us (32%)
  waiting for transfers between devices  9.7 us (22%)
  Pallas kernels  8.73 us (20%)
  local copies, waits for them, and re-layouts  8.45 us (20%)
  other arithmetic  1.35 us (3%)
  between operations  0.67 us (2%)
    ppermute x10, starting transfers between devices, exchange(): return lax.ppermute(x, axes, [(i, i ^ step) for i in range(peers)])  13.8 us
    ppermute x10, waiting for transfers between devices, exchange(): return lax.ppermute(x, axes, [(i, i ^ step) for i in range(peers)])  9.7 us
    unnamed x26, local copies, waits for them, and re-layouts  8.45 us
    pallas_call x1, Pallas kernels, gathered_plan(): pl.pallas_call(main_kernel, out_shape=(jax.ShapeDtypeStruct((frames, 1, c...  6.83 us
    pallas_call x1, Pallas kernels, gathered_plan(): pl.pallas_call(pack_kernel, out_shape=jax.ShapeDtypeStruct((blocks * fram...  1.9 us
  transfers between devices with their start and end apart: 10, of which 7 were waited for; matrix products, arithmetic and copies ran while one was open for 2% of the time, Pallas kernels for 0%

profile of v1, /device:TPU:0, one launch (start us, length us, event | category | flops | bytes accessed | tf_op | source)
XLA Modules:
  0.0 42.7 jit_solution(18223849676041470717)
XLA Ops:
  0.6 6.0 %collective-permute-start.6 = (bf16[2,64,256]{2,1,0:T(8,128)(2,1)}, bf16[2,64,256]{2,1,0:T(8,128)(2,1)S(1)}, u32[]{:S(2)}, u32[]{:S(2)}) collective-permute-start(bf16[2,64,256]{2,1,0:T(8,128)(2,1)} %bitcast.9), channel_id=1, source_target_pairs={{0,14},{2,12},{4,10},{6,8},{8,6},{10,4},{12,2},{14,0},{1,15},{3,13... | collective-permute-start | bytes 196616 | tf_op jit(solution)/shard_map/ppermute | solution.py:135
  6.7 0.2 collective-permute-start.5
  6.9 0.8 %collective-permute-start.4 = (bf16[2,64,256]{2,1,0:T(8,128)(2,1)}, bf16[2,64,256]{2,1,0:T(8,128)(2,1)S(1)}, u32[]{:S(2)}, u32[]{:S(2)}) collective-permute-start(bf16[2,64,256]{2,1,0:T(8,128)(2,1)} %bitcast.11), channel_id=1, source_target_pairs={{0,10},{2,8},{4,14},{6,12},{8,2},{10,0},{12,6},{14,4},{1,11},{3,9}... | collective-permute-start | bytes 196616 | tf_op jit(solution)/shard_map/ppermute | solution.py:135
  7.7 2.0 %collective-permute-start.3 = (bf16[2,64,256]{2,1,0:T(8,128)(2,1)}, bf16[2,64,256]{2,1,0:T(8,128)(2,1)S(1)}, u32[]{:S(2)}, u32[]{:S(2)}) collective-permute-start(bf16[2,64,256]{2,1,0:T(8,128)(2,1)} %bitcast.12), channel_id=1, source_target_pairs={{0,8},{2,10},{4,12},{6,14},{8,0},{10,2},{12,4},{14,6},{1,9},{3,11}... | collective-permute-start | bytes 196616 | tf_op jit(solution)/shard_map/ppermute | solution.py:135
  9.7 2.3 %collective-permute-start.2 = (bf16[2,64,256]{2,1,0:T(8,128)(2,1)}, bf16[2,64,256]{2,1,0:T(8,128)(2,1)S(1)}, u32[]{:S(2)}, u32[]{:S(2)}) collective-permute-start(bf16[2,64,256]{2,1,0:T(8,128)(2,1)} %bitcast.13), channel_id=1, source_target_pairs={{0,6},{2,4},{4,2},{6,0},{8,14},{10,12},{12,10},{14,8},{1,7},{3,5},... | collective-permute-start | bytes 196616 | tf_op jit(solution)/shard_map/ppermute | solution.py:135
  12.0 0.0 collective-permute-done.6.refs_7_
  12.0 0.0 copy-start.6
  12.0 0.8 %collective-permute-start.1 = (bf16[2,64,256]{2,1,0:T(8,128)(2,1)}, bf16[2,64,256]{2,1,0:T(8,128)(2,1)S(1)}, u32[]{:S(2)}, u32[]{:S(2)}) collective-permute-start(bf16[2,64,256]{2,1,0:T(8,128)(2,1)} %bitcast.14), channel_id=1, source_target_pairs={{0,4},{2,6},{4,0},{6,2},{8,12},{10,14},{12,8},{14,10},{1,5},{3,7},... | collective-permute-start | bytes 196616 | tf_op jit(solution)/shard_map/ppermute | solution.py:135
  12.8 0.4 collective-permute-done.5.refs_6_
  13.1 0.0 copy-start.7
  13.1 0.5 %collective-permute-start = (bf16[2,64,256]{2,1,0:T(8,128)(2,1)}, bf16[2,64,256]{2,1,0:T(8,128)(2,1)S(1)}, u32[]{:S(2)}, u32[]{:S(2)}) collective-permute-start(bf16[2,64,256]{2,1,0:T(8,128)(2,1)} %bitcast.15), channel_id=1, source_target_pairs={{0,2},{2,0},{4,6},{6,4},{8,10},{10,8},{12,14},{14,12},{1,3},{3,1},... | collective-permute-start | bytes 196616 | tf_op jit(solution)/shard_map/ppermute | solution.py:135
  13.6 2.8 %collective-permute-done.4.refs_5_ = bf16[2,64,256]{2,1,0:T(8,128)(2,1)S(1)} collective-permute-done((bf16[2,64,256]{2,1,0:T(8,128)(2,1)}, bf16[2,64,256]{2,1,0:T(8,128)(2,1)S(1)}, u32[]{:S(2)}, u32[]{:S(2)}) %collective-permute-start.4) | collective-permute-done | bytes 65568 | tf_op jit(solution)/shard_map/ppermute | solution.py:135
  16.5 0.0 copy-start.8
  16.5 1.6 %collective-permute-done.3.refs_4_ = bf16[2,64,256]{2,1,0:T(8,128)(2,1)S(1)} collective-permute-done((bf16[2,64,256]{2,1,0:T(8,128)(2,1)}, bf16[2,64,256]{2,1,0:T(8,128)(2,1)S(1)}, u32[]{:S(2)}, u32[]{:S(2)}) %collective-permute-start.3) | collective-permute-done | bytes 65568 | tf_op jit(solution)/shard_map/ppermute | solution.py:135
  18.1 0.0 copy-start.9
  18.1 0.0 collective-permute-done.2.refs_3_
  18.1 0.0 copy-start.10
  18.1 0.4 collective-permute-done.1.refs_2_
  18.5 0.0 copy-start.11
  18.5 0.0 collective-permute-done.refs_1_
  18.5 0.0 copy-done.6
  18.5 0.0 copy-done.7
  18.5 0.0 copy-done.8
  18.5 0.2 copy-done.9
  18.7 0.0 copy-done.10
  18.8 0.4 copy-done.11
  19.1 0.6 %copy-done.12 = bf16[2,64,256]{2,1,0:T(8,128)(2,1)} copy-done((bf16[2,64,256]{2,1,0:T(8,128)(2,1)}, bf16[2,64,256]{2,1,0:T(8,128)(2,1)S(1)}, u32[]{:S(2)}) %copy-start.12) | copy-done | bytes 65560
  19.8 1.9 %pack.1.mine_ref = bf16[4,4,64,256]{3,2,1,0:T(8,128)(2,1)} custom-call(bf16[2,64,256]{2,1,0:T(8,128)(2,1)} %bitcast.16, bf16[2,64,256]{2,1,0:T(8,128)(2,1)} %copy-done.12, bf16[2,64,256]{2,1,0:T(8,128)(2,1)} %copy-done.11, bf16[2,64,256]{2,1,0:T(8,128)(2,1)} %copy-done.10, bf16[2,64,256]{2,1,0:T(8,128)(2,1)} %copy-done.9, bf16[2,64,256]{2,1,0:T(8,128)(2,1)} %copy-done.8, ...), custom_call_target="tpu_custom_call" | custom-call | tf_op jit(solution)/shard_map/pack/pallas_call | solution.py:274
  21.7 0.0 collective-permute-start.7
  21.7 0.7 %pad_maximum_fusion.gains_ref = f32[2,256]{1,0:T(2,128)S(1)} fusion(f32[1,256]{1,0:T(1,128)} %bitcast.17, f32[1,256]{1,0:T(1,128)} %bitcast.18), kind=kLoop, calls=%fused_computation.2 | loop fusion | flops 512 | bytes 4096 | tf_op jit(solution)/shard_map/stack | solution.py:271
  22.4 0.5 %collective-permute-start.8 = (f32[2,256]{1,0:T(2,128)S(1)}, f32[2,256]{1,0:T(2,128)S(1)}, u32[]{:S(2)}, u32[]{:S(2)}) collective-permute-start(f32[2,256]{1,0:T(2,128)S(1)} %pad_maximum_fusion.gains_ref), channel_id=1, source_target_pairs={{0,1},{1,0},{2,3},{3,2},{4,5},{5,4},{6,7},{7,6},{8,9},{9,8},{10,11... | collective-permute-start | bytes 6152 | tf_op jit(solution)/shard_map/ppermute | solution.py:135
  22.9 0.8 %collective-permute-done.8.other_gains_ref = f32[2,256]{1,0:T(2,128)S(1)} collective-permute-done((f32[2,256]{1,0:T(2,128)S(1)}, f32[2,256]{1,0:T(2,128)S(1)}, u32[]{:S(2)}, u32[]{:S(2)}) %collective-permute-start.8) | collective-permute-done | bytes 2080 | tf_op jit(solution)/shard_map/ppermute | solution.py:135
  23.7 0.1 collective-permute-done.7.other_ref
  23.8 0.0 copy-start
  23.8 2.0 %copy-done = bf16[3,3,3,256,256]{4,3,2,1,0:T(8,128)(2,1)S(1)} copy-done((bf16[3,3,3,256,256]{4,3,2,1,0:T(8,128)(2,1)S(1)}, bf16[3,3,3,256,256]{4,3,2,1,0:T(8,128)(2,1)}, u32[]{:S(2)}) %copy-start) | copy-done | bytes 3538968
  25.8 1.0 %copy-done.1 = bf16[4,4,64,256]{3,2,1,0:T(8,128)(2,1)S(1)} copy-done((bf16[4,4,64,256]{3,2,1,0:T(8,128)(2,1)S(1)}, bf16[4,4,64,256]{3,2,1,0:T(8,128)(2,1)}, u32[]{:S(2)}) %copy-start.1) | copy-done | bytes 524312
  26.8 0.0 copy-start.2
  26.8 1.0 %copy-done.2 = bf16[512,512]{1,0:T(8,128)(2,1)S(1)} copy-done((bf16[512,512]{1,0:T(8,128)(2,1)S(1)}, bf16[512,512]{1,0:T(8,128)(2,1)}, u32[]{:S(2)}) %copy-start.2) | copy-done | bytes 524312
  27.9 0.0 copy-start.3
  27.9 1.0 %copy-done.3 = bf16[512,512]{1,0:T(8,128)(2,1)S(1)} copy-done((bf16[512,512]{1,0:T(8,128)(2,1)S(1)}, bf16[512,512]{1,0:T(8,128)(2,1)}, u32[]{:S(2)}) %copy-start.3) | copy-done | bytes 524312
  28.9 0.0 copy-start.4
  28.9 1.0 %copy-done.4 = bf16[512,512]{1,0:T(8,128)(2,1)S(1)} copy-done((bf16[512,512]{1,0:T(8,128)(2,1)S(1)}, bf16[512,512]{1,0:T(8,128)(2,1)}, u32[]{:S(2)}) %copy-start.4) | copy-done | bytes 524312
  30.0 0.0 copy-start.5
  30.0 1.0 %copy-done.5 = bf16[512,512]{1,0:T(8,128)(2,1)S(1)} copy-done((bf16[512,512]{1,0:T(8,128)(2,1)S(1)}, bf16[512,512]{1,0:T(8,128)(2,1)}, u32[]{:S(2)}) %copy-start.5) | copy-done | bytes 524312
  31.0 6.8 %block.1 = (bf16[2,1,64,256]{3,2,1,0:T(8,128)(2,1)}, f32[2,64,256]{2,1,0:T(8,128)S(1)}, bf16[1,2,64,256]{3,2,1,0:T(8,128)(2,1)S(1)}) custom-call(bf16[4,4,64,256]{3,2,1,0:T(8,128)(2,1)S(1)} %copy-done.1, bf16[4,4,64,256]{3,2,1,0:T(8,128)(2,1)S(1)} %collective-permute-done.7.other_ref, f32[2,256]{1,0:T(2,128)S(1)} %pad_maximum_fusion.gains_ref, ...), custom_call_target="tpu_custom_call" | custom-call | tf_op jit(solution)/shard_map/block/pallas_call | solution.py:283
  37.8 0.7 %collective-permute-start.9 = (bf16[2,64,256]{2,1,0:T(8,128)(2,1)S(1)}, bf16[2,64,256]{2,1,0:T(8,128)(2,1)S(1)}, u32[]{:S(2)}, u32[]{:S(2)}) collective-permute-start(bf16[2,64,256]{2,1,0:T(8,128)(2,1)S(1)} %bitcast.8), channel_id=1, source_target_pairs={{0,2},{2,0},{1,3},{3,1},{4,6},{6,4},{5,7},{7,5},{8,10},{10,8},{9,1... | collective-permute-start | bytes 196616 | tf_op jit(solution)/shard_map/ppermute | solution.py:135
  38.6 3.5 %collective-permute-done.9 = bf16[2,64,256]{2,1,0:T(8,128)(2,1)S(1)} collective-permute-done((bf16[2,64,256]{2,1,0:T(8,128)(2,1)S(1)}, bf16[2,64,256]{2,1,0:T(8,128)(2,1)S(1)}, u32[]{:S(2)}, u32[]{:S(2)}) %collective-permute-start.9) | collective-permute-done | bytes 65568 | tf_op jit(solution)/shard_map/ppermute | solution.py:135
  42.1 0.6 %fusion = bf16[2,1,64,256]{3,2,1,0:T(8,128)(2,1)} fusion(f32[2,64,256]{2,1,0:T(8,128)S(1)} %get-tuple-element.6, bf16[2,64,256]{2,1,0:T(8,128)(2,1)S(1)} %collective-permute-done.9), kind=kLoop, calls=%fused_computation.1 | loop fusion | flops 98304 | bytes 262144
  (2 shorter events, 0.0 us)
Async XLA Ops:
  0.6 11.3 %collective-permute-start.6 = (bf16[2,64,256]{2,1,0:T(8,128)(2,1)}, bf16[2,64,256]{2,1,0:T(8,128)(2,1)S(1)}, u32[]{:S(2)}, u32[]{:S(2)}) collective-permute-start(bf16[2,64,256]{2,1,0:T(8,128)(2,1)} %bitcast.9), channel_id=1, source_target_pairs={{0,14},{2,12},{4,10},{6,8},{8,6},{10,4},{12,2},{14,0},{1,15},{3,13... | collective-permute-start | bytes 196616 | tf_op jit(solution)/shard_map/ppermute | solution.py:135
  6.7 6.5 %collective-permute-start.5 = (bf16[2,64,256]{2,1,0:T(8,128)(2,1)}, bf16[2,64,256]{2,1,0:T(8,128)(2,1)S(1)}, u32[]{:S(2)}, u32[]{:S(2)}) collective-permute-start(bf16[2,64,256]{2,1,0:T(8,128)(2,1)} %bitcast.10), channel_id=1, source_target_pairs={{0,12},{2,14},{4,8},{6,10},{8,4},{10,6},{12,0},{14,2},{1,13},{3,15... | collective-permute-start | bytes 196616 | tf_op jit(solution)/shard_map/ppermute | solution.py:135
  6.9 9.6 %collective-permute-start.4 = (bf16[2,64,256]{2,1,0:T(8,128)(2,1)}, bf16[2,64,256]{2,1,0:T(8,128)(2,1)S(1)}, u32[]{:S(2)}, u32[]{:S(2)}) collective-permute-start(bf16[2,64,256]{2,1,0:T(8,128)(2,1)} %bitcast.11), channel_id=1, source_target_pairs={{0,10},{2,8},{4,14},{6,12},{8,2},{10,0},{12,6},{14,4},{1,11},{3,9}... | collective-permute-start | bytes 196616 | tf_op jit(solution)/shard_map/ppermute | solution.py:135
  7.7 10.4 %collective-permute-start.3 = (bf16[2,64,256]{2,1,0:T(8,128)(2,1)}, bf16[2,64,256]{2,1,0:T(8,128)(2,1)S(1)}, u32[]{:S(2)}, u32[]{:S(2)}) collective-permute-start(bf16[2,64,256]{2,1,0:T(8,128)(2,1)} %bitcast.12), channel_id=1, source_target_pairs={{0,8},{2,10},{4,12},{6,14},{8,0},{10,2},{12,4},{14,6},{1,9},{3,11}... | collective-permute-start | bytes 196616 | tf_op jit(solution)/shard_map/ppermute | solution.py:135
  9.7 8.4 %collective-permute-start.2 = (bf16[2,64,256]{2,1,0:T(8,128)(2,1)}, bf16[2,64,256]{2,1,0:T(8,128)(2,1)S(1)}, u32[]{:S(2)}, u32[]{:S(2)}) collective-permute-start(bf16[2,64,256]{2,1,0:T(8,128)(2,1)} %bitcast.13), channel_id=1, source_target_pairs={{0,6},{2,4},{4,2},{6,0},{8,14},{10,12},{12,10},{14,8},{1,7},{3,5},... | collective-permute-start | bytes 196616 | tf_op jit(solution)/shard_map/ppermute | solution.py:135
  12.0 6.6 %copy-start.6 = (bf16[2,64,256]{2,1,0:T(8,128)(2,1)}, bf16[2,64,256]{2,1,0:T(8,128)(2,1)S(1)}, u32[]{:S(2)}) copy-start(bf16[2,64,256]{2,1,0:T(8,128)(2,1)S(1)} %collective-permute-done.6.refs_7_) | copy-start | bytes 196612
  12.0 6.5 %collective-permute-start.1 = (bf16[2,64,256]{2,1,0:T(8,128)(2,1)}, bf16[2,64,256]{2,1,0:T(8,128)(2,1)S(1)}, u32[]{:S(2)}, u32[]{:S(2)}) collective-permute-start(bf16[2,64,256]{2,1,0:T(8,128)(2,1)} %bitcast.14), channel_id=1, source_target_pairs={{0,4},{2,6},{4,0},{6,2},{8,12},{10,14},{12,8},{14,10},{1,5},{3,7},... | collective-permute-start | bytes 196616 | tf_op jit(solution)/shard_map/ppermute | solution.py:135
  13.1 5.4 %copy-start.7 = (bf16[2,64,256]{2,1,0:T(8,128)(2,1)}, bf16[2,64,256]{2,1,0:T(8,128)(2,1)S(1)}, u32[]{:S(2)}) copy-start(bf16[2,64,256]{2,1,0:T(8,128)(2,1)S(1)} %collective-permute-done.5.refs_6_) | copy-start | bytes 196612
  13.1 5.4 %collective-permute-start = (bf16[2,64,256]{2,1,0:T(8,128)(2,1)}, bf16[2,64,256]{2,1,0:T(8,128)(2,1)S(1)}, u32[]{:S(2)}, u32[]{:S(2)}) collective-permute-start(bf16[2,64,256]{2,1,0:T(8,128)(2,1)} %bitcast.15), channel_id=1, source_target_pairs={{0,2},{2,0},{4,6},{6,4},{8,10},{10,8},{12,14},{14,12},{1,3},{3,1},... | collective-permute-start | bytes 196616 | tf_op jit(solution)/shard_map/ppermute | solution.py:135
  16.5 2.1 %copy-start.8 = (bf16[2,64,256]{2,1,0:T(8,128)(2,1)}, bf16[2,64,256]{2,1,0:T(8,128)(2,1)S(1)}, u32[]{:S(2)}) copy-start(bf16[2,64,256]{2,1,0:T(8,128)(2,1)S(1)} %collective-permute-done.4.refs_5_) | copy-start | bytes 196612
  18.1 0.6 %copy-start.9 = (bf16[2,64,256]{2,1,0:T(8,128)(2,1)}, bf16[2,64,256]{2,1,0:T(8,128)(2,1)S(1)}, u32[]{:S(2)}) copy-start(bf16[2,64,256]{2,1,0:T(8,128)(2,1)S(1)} %collective-permute-done.3.refs_4_) | copy-start | bytes 196612
  18.1 0.6 %copy-start.10 = (bf16[2,64,256]{2,1,0:T(8,128)(2,1)}, bf16[2,64,256]{2,1,0:T(8,128)(2,1)S(1)}, u32[]{:S(2)}) copy-start(bf16[2,64,256]{2,1,0:T(8,128)(2,1)S(1)} %collective-permute-done.2.refs_3_) | copy-start | bytes 196612
  18.5 0.6 %copy-start.11 = (bf16[2,64,256]{2,1,0:T(8,128)(2,1)}, bf16[2,64,256]{2,1,0:T(8,128)(2,1)S(1)}, u32[]{:S(2)}) copy-start(bf16[2,64,256]{2,1,0:T(8,128)(2,1)S(1)} %collective-permute-done.1.refs_2_) | copy-start | bytes 196612
  19.1 0.6 %copy-start.12 = (bf16[2,64,256]{2,1,0:T(8,128)(2,1)}, bf16[2,64,256]{2,1,0:T(8,128)(2,1)S(1)}, u32[]{:S(2)}) copy-start(bf16[2,64,256]{2,1,0:T(8,128)(2,1)S(1)} %collective-permute-done.refs_1_) | copy-start | bytes 196612
  21.7 2.1 %collective-permute-start.7 = (bf16[4,4,64,256]{3,2,1,0:T(8,128)(2,1)}, bf16[4,4,64,256]{3,2,1,0:T(8,128)(2,1)S(1)}, u32[]{:S(2)}, u32[]{:S(2)}) collective-permute-start(bf16[4,4,64,256]{3,2,1,0:T(8,128)(2,1)} %pack.1.mine_ref), channel_id=1, source_target_pairs={{0,1},{1,0},{2,3},{3,2},{4,5},{5,4},{6,7},{7,6},{8,9},{9,8},{10,11... | collective-permute-start | bytes 1572872 | tf_op jit(solution)/shard_map/ppermute | solution.py:135
  22.4 1.3 %collective-permute-start.8 = (f32[2,256]{1,0:T(2,128)S(1)}, f32[2,256]{1,0:T(2,128)S(1)}, u32[]{:S(2)}, u32[]{:S(2)}) collective-permute-start(f32[2,256]{1,0:T(2,128)S(1)} %pad_maximum_fusion.gains_ref), channel_id=1, source_target_pairs={{0,1},{1,0},{2,3},{3,2},{4,5},{5,4},{6,7},{7,6},{8,9},{9,8},{10,11... | collective-permute-start | bytes 6152 | tf_op jit(solution)/shard_map/ppermute | solution.py:135
  23.8 2.0 %copy-start = (bf16[3,3,3,256,256]{4,3,2,1,0:T(8,128)(2,1)S(1)}, bf16[3,3,3,256,256]{4,3,2,1,0:T(8,128)(2,1)}, u32[]{:S(2)}) copy-start(bf16[3,3,3,256,256]{4,3,2,1,0:T(8,128)(2,1)} %kernel_ref.1) | copy-start | bytes 10616836
  25.8 1.0 %copy-start.1 = (bf16[4,4,64,256]{3,2,1,0:T(8,128)(2,1)S(1)}, bf16[4,4,64,256]{3,2,1,0:T(8,128)(2,1)}, u32[]{:S(2)}) copy-start(bf16[4,4,64,256]{3,2,1,0:T(8,128)(2,1)} %pack.1.mine_ref) | copy-start | bytes 1572868
  26.8 1.0 %copy-start.2 = (bf16[512,512]{1,0:T(8,128)(2,1)S(1)}, bf16[512,512]{1,0:T(8,128)(2,1)}, u32[]{:S(2)}) copy-start(bf16[512,512]{1,0:T(8,128)(2,1)} %query_ref.1) | copy-start | bytes 1572868
  27.9 1.0 %copy-start.3 = (bf16[512,512]{1,0:T(8,128)(2,1)S(1)}, bf16[512,512]{1,0:T(8,128)(2,1)}, u32[]{:S(2)}) copy-start(bf16[512,512]{1,0:T(8,128)(2,1)} %key_ref.1) | copy-start | bytes 1572868
  28.9 1.0 %copy-start.4 = (bf16[512,512]{1,0:T(8,128)(2,1)S(1)}, bf16[512,512]{1,0:T(8,128)(2,1)}, u32[]{:S(2)}) copy-start(bf16[512,512]{1,0:T(8,128)(2,1)} %value_ref.1) | copy-start | bytes 1572868
  30.0 1.0 %copy-start.5 = (bf16[512,512]{1,0:T(8,128)(2,1)S(1)}, bf16[512,512]{1,0:T(8,128)(2,1)}, u32[]{:S(2)}) copy-start(bf16[512,512]{1,0:T(8,128)(2,1)} %out_weight_ref.1) | copy-start | bytes 1572868
  37.8 4.3 %collective-permute-start.9 = (bf16[2,64,256]{2,1,0:T(8,128)(2,1)S(1)}, bf16[2,64,256]{2,1,0:T(8,128)(2,1)S(1)}, u32[]{:S(2)}, u32[]{:S(2)}) collective-permute-start(bf16[2,64,256]{2,1,0:T(8,128)(2,1)S(1)} %bitcast.8), channel_id=1, source_target_pairs={{0,2},{2,0},{1,3},{3,1},{4,6},{6,4},{5,7},{7,5},{8,10},{10,8},{9,1... | collective-permute-start | bytes 196616 | tf_op jit(solution)/shard_map/ppermute | solution.py:135

commit v2 on v1

--- a/solution.py
+++ b/solution.py
@@ -130,20 +130,98 @@
     return (attended, convolved)
 
 
+GAIN_ROWS = 16
+
+
 def exchange(x, axes, step):
     peers = lax.axis_size(axes)
     return lax.ppermute(x, axes, [(i, i ^ step) for i in range(peers)])
 
 
-def pack_kernel(*refs):
-    piece_refs, out_ref = refs[:-1], refs[-1]
-    frames, cols, channels = piece_refs[0].shape
-    blocks = out_ref.shape[0] // frames
-    rows = len(piece_refs) // blocks
-    for block in range(blocks):
-        for row in range(rows):
-            for frame in range(frames):
-                out_ref[block * frames + frame, row] = piece_refs[row * blocks + block][frame]
+def stage_kernel(*refs):
+    count = len(refs) // 2
+    copies = [pltpu.make_async_copy(refs[i], refs[count + i], refs[-1].at[i]) for i in range(count)]
+    for copy in copies:
+        copy.start()
+    for copy in copies:
+        copy.wait()
+
+
+def stage(arrays):
+    size = sum(array.size * array.dtype.itemsize for array in arrays)
+    return pl.pallas_call(
+        stage_kernel,
+        out_shape=tuple(jax.ShapeDtypeStruct(array.shape, array.dtype) for array in arrays),
+        in_specs=[pl.BlockSpec(memory_space=pltpu.HBM)] * len(arrays),
+        out_specs=tuple(pl.BlockSpec(memory_space=pltpu.VMEM) for _ in arrays),
+        scratch_shapes=[pltpu.SemaphoreType.DMA((len(arrays),))],
+        compiler_params=pltpu.CompilerParams(vmem_limit_bytes=1 << 20),
+        cost_estimate=pl.CostEstimate(flops=0, bytes_accessed=2 * size, transcendentals=0),
+        name="stage",
+    )(*(in_hbm(array) for array in arrays))
+
+
+def near_kernel(*refs):
+    count = len(refs) - 8
+    piece_refs, own_hbm, first_hbm, second_hbm, out_ref, own_ref, first_ref, second_ref, arrived = (
+        refs[:count], *refs[count:]
+    )
+    copies = [
+        pltpu.make_async_copy(own_hbm, own_ref, arrived.at[0]),
+        pltpu.make_async_copy(first_hbm, first_ref, arrived.at[1]),
+        pltpu.make_async_copy(second_hbm, second_ref, arrived.at[2]),
+    ]
+    for copy in copies:
+        copy.start()
+    size = own_ref.shape[0]
+    for index, piece_ref in enumerate(piece_refs):
+        out_ref[(index + 1) * size : (index + 2) * size, :] = piece_ref[...]
+    for copy in copies:
+        copy.wait()
+    out_ref[:size, :] = own_ref[...]
+    parts = []
+    for gain_ref in (first_ref, second_ref):
+        rest = gain_ref[...]
+        for _ in range(3):
+            rounded = rest.astype(jnp.bfloat16).astype(jnp.float32)
+            parts.append(rounded)
+            rest = rest - rounded
+    parts.append(jnp.zeros((GAIN_ROWS - len(parts), out_ref.shape[1]), jnp.float32))
+    end = out_ref.shape[0]
+    out_ref[end - GAIN_ROWS : end, :] = jnp.concatenate(parts, axis=0).astype(jnp.bfloat16)
+
+
+def pack_near(pieces, own, gains):
+    size, channels = own.shape
+    return pl.pallas_call(
+        near_kernel,
+        out_shape=jax.ShapeDtypeStruct(((len(pieces) + 1) * size + GAIN_ROWS, channels), own.dtype),
+        in_specs=[pl.BlockSpec(memory_space=pltpu.VMEM)] * len(pieces) + [pl.BlockSpec(memory_space=pltpu.HBM)] * 3,
+        scratch_shapes=[pltpu.VMEM(array.shape, array.dtype) for array in (own, *gains)]
+        + [pltpu.SemaphoreType.DMA((3,))],
+        compiler_params=pltpu.CompilerParams(vmem_limit_bytes=2 * 1024 * 1024),
+        name="near",
+    )(*pieces, *(in_hbm(array) for array in (own, *gains)))
+
+
+def far_kernel(*refs):
+    size = refs[0].shape[0]
+    for index, piece_ref in enumerate(refs[:-1]):
+        refs[-1][index * size : (index + 1) * size, :] = piece_ref[...]
+
+
+def pack_far(pieces):
+    size, channels = pieces[0].shape
+    return pl.pallas_call(
+        far_kernel,
+        out_shape=jax.ShapeDtypeStruct((len(pieces) * size, channels), pieces[0].dtype),
+        compiler_params=pltpu.CompilerParams(vmem_limit_bytes=2 * 1024 * 1024),
+        name="far",
+    )(*pieces)
+
+
+def in_hbm(array):
+    return pltpu.with_memory_space_constraint(array, pltpu.HBM)
 
 
 def group_means(sums, count):
@@ -168,14 +246,16 @@
 
 
 def main_kernel(
-    mine_ref, other_ref, gains_ref, other_gains_ref, query_ref, key_ref, value_ref, out_weight_ref, kernel_ref,
+    near_ref, far_ref, other_near_ref, other_far_ref, query_ref, key_ref, value_ref, out_weight_ref, kernel_hbm,
     attended_ref, keep_ref, send_ref,
-    normed, queries, keyed, valued, resid, activated,
+    normed, queries, keyed, valued, resid, activated, kernel_ref, arrived,
 ):
-    frames, rows, cols, channels = mine_ref.shape
+    kernel_copy = pltpu.make_async_copy(kernel_hbm, kernel_ref, arrived)
+    kernel_copy.start()
+    own_frames, _, cols, channels = attended_ref.shape
+    frames, rows = resid.shape[:2]
     tokens = frames * rows * cols
     frame_tokens = rows * cols
-    own_frames = attended_ref.shape[0]
     space = lax.axis_index("space")
     block = lax.axis_index("tm")
     half = lax.axis_index("chan")
@@ -184,12 +264,28 @@
     own_rows = pl.ds(pl.multiple_of(half * channels, channels), channels)
     other_rows = pl.ds(pl.multiple_of((1 - half) * channels, channels), channels)
 
-    for side, (ref, gain_ref) in enumerate(((mine_ref, gains_ref), (other_ref, other_gains_ref))):
-        values = ref[...].reshape(tokens, channels).astype(jnp.float32)
+    blocks = frames // own_frames
+
+    def side_parts(near, far):
+        pieces = []
+        for ref in (near, far):
+            pieces += [ref[at : at + own_frames * cols, :] for at in range(0, rows // 2 * frames * cols, own_frames * cols)]
+        laid = []
+        for index in range(blocks):
+            for frame in range(own_frames):
+                at = slice(frame * cols, (frame + 1) * cols)
+                laid += [pieces[row * blocks + index][at] for row in range(rows)]
+        parts = near[near.shape[0] - GAIN_ROWS : near.shape[0], :].astype(jnp.float32)
+        gains = [parts[at : at + 1] + parts[at + 1 : at + 2] + parts[at + 2 : at + 3] for at in (0, 3)]
+        return jnp.concatenate(laid, axis=0), *gains
+
+    sides, first_gains, second_gains = zip(side_parts(near_ref, far_ref), side_parts(other_near_ref, other_far_ref))
+    for side, gain in enumerate(first_gains):
+        values = sides[side].astype(jnp.float32)
         centre, scale = moments(values, count)
-        normed[side] = ((values - centre) * scale * gain_ref[0:1, :]).astype(jnp.bfloat16)
-
-    for weight_ref, target in ((query_ref, queries), (key_ref, keyed), (value_ref, valued)):
+        normed[side] = ((values - centre) * scale * gain).astype(jnp.bfloat16)
+
+    for weight_ref, target in zip((query_ref, key_ref, value_ref), (queries, keyed, valued)):
         target[...] = (
             jnp.dot(normed[0], weight_ref[own_rows, :], preferred_element_type=jnp.float32)
             + jnp.dot(normed[1], weight_ref[other_rows, :], preferred_element_type=jnp.float32)
@@ -215,11 +311,11 @@
         projected = jnp.dot(
             mixed, out_weight_ref[:, in_cols], preferred_element_type=jnp.float32
         ).astype(jnp.bfloat16)
-        source = jnp.where(mine_in, mine_ref[frame].astype(jnp.float32), other_ref[frame].astype(jnp.float32))
-        resid[frame] = source + projected.astype(jnp.float32).reshape(rows, cols, in_channels)
+        source = jnp.where(mine_in, sides[0][at].astype(jnp.float32), sides[1][at].astype(jnp.float32))
+        resid[frame] = (source + projected.astype(jnp.float32)).reshape(rows, cols, in_channels)
 
     centre, scale = moments(resid[...].reshape(tokens, in_channels), count)
-    gain = jnp.where(mine_in, gains_ref[1:2, :], other_gains_ref[1:2, :])
+    gain = jnp.where(mine_in, *second_gains)
     for tap in range(3):
         row = space + (tap - 1)
         inside = jnp.logical_and(row >= 0, row < rows)
@@ -232,6 +328,7 @@
 
     out_channels = kernel_ref.shape[4]
     columns = [None] * 3
+    kernel_copy.wait()
     for col_tap in range(3):
         total = None
         for time_tap in (2, 1, 0):
@@ -249,7 +346,6 @@
     left = jnp.where(place == 0, 0.0, pltpu.roll(columns[0], 1, 0))
     right = jnp.where(place == cols - 1, 0.0, pltpu.roll(columns[2], frames * cols - 1, 0))
     summed = (columns[1] + left + right).reshape(frames, cols, out_channels)
-    blocks = frames // own_frames
     for index in range(blocks):
         piece = summed[index * own_frames : (index + 1) * own_frames]
 
@@ -267,19 +363,21 @@
 ):
     frames, _, cols, channels = hidden_states.shape
     rows, blocks = lax.axis_size("space"), lax.axis_size("tm")
-    own = hidden_states.reshape(frames, cols, channels)
-    gains = jnp.stack([first_gain, second_gain])
-    other_gains = exchange(gains, "chan", 1)
-    pieces = [own] + [exchange(own, ("space", "tm"), step) for step in range(1, rows * blocks)]
-    mine = pl.pallas_call(
-        pack_kernel,
-        out_shape=jax.ShapeDtypeStruct((blocks * frames, rows, cols, channels), jnp.bfloat16),
-        name="pack",
-    )(*pieces)
-    other = exchange(mine, "chan", 1)
+    own = hidden_states.reshape(frames * cols, channels)
+    gains = (first_gain.reshape(1, channels), second_gain.reshape(1, channels))
+    far_own = {row: exchange(own, "space", row) for row in range(rows - 1, rows // 2 - 1, -1)}
+    near = [exchange(own, ("space", "tm"), step) for step in range(1, rows // 2 * blocks)]
+    far = []
+    for row in range(rows // 2, rows):
+        far += [far_own[row]] + [exchange(far_own[row], "tm", step) for step in range(1, blocks)]
+    near_mine = pack_near(near, own, gains)
+    near_other = exchange(near_mine, "chan", 1)
+    far_mine = pack_far(far)
+    far_other = exchange(far_mine, "chan", 1)
     out_channels = conv_kernel.shape[4]
     in_channels = conv_kernel.shape[3]
     tokens = blocks * frames * rows * cols
+    weights = stage((query_weight, key_weight, value_weight, out_weight))
     attended, keep, send = pl.pallas_call(
         main_kernel,
         out_shape=(
@@ -294,10 +392,13 @@
             pltpu.VMEM((tokens, D), jnp.bfloat16),
             pltpu.VMEM((blocks * frames, rows, cols, in_channels), jnp.float32),
             pltpu.VMEM((3, blocks * frames, cols, in_channels), jnp.bfloat16),
+            pltpu.VMEM(conv_kernel.shape, conv_kernel.dtype),
+            pltpu.SemaphoreType.DMA,
         ],
-        compiler_params=pltpu.CompilerParams(vmem_limit_bytes=40 * 1024 * 1024),
+        in_specs=[pl.BlockSpec(memory_space=pltpu.VMEM)] * 8 + [pl.BlockSpec(memory_space=pltpu.HBM)],
+        compiler_params=pltpu.CompilerParams(vmem_limit_bytes=24 * 1024 * 1024),
         name="block",
-    )(mine, other, gains, other_gains, query_weight, key_weight, value_weight, out_weight, conv_kernel)
+    )(near_mine, far_mine, near_other, far_other, *weights, in_hbm(conv_kernel))
     total = keep
     for step in range(1, blocks):
         total = total + exchange(send[step - 1], "tm", step).astype(jnp.float32)

time: 43.2 us -> 30 us (0.69)
  local copies, waits for them, and re-layouts: 8.45 us -> 0 us
  waiting for transfers between devices: 9.7 us -> 5.7 us
  other arithmetic: 1.35 us -> 0.65 us
  Pallas kernels: 8.73 us -> 9.43 us
  starting transfers between devices: 13.8 us -> 13.3 us
    unnamed x26 -> x0, local copies, waits for them, and re-layouts: 8.45 us -> none
    ppermute x10, waiting for transfers between devices: 9.7 us -> 5.7 us  [exchange(): return lax.ppermute(x, axes, [(i, i ^ step) for i in range(peers)])]
    another operation x1 -> x0, other arithmetic: 0.7 us -> none  [gathered_plan(): gains = jnp.stack([first_gain, second_gain])]
    pallas_call x1 -> x3, Pallas kernels: 1.9 us -> 2.47 us  [the longest x1 1.55 us: stage(): pl.pallas_call(stage_kernel, out_shape=tuple((jax.ShapeDtypeStruct(array....]
    ppermute x10, starting transfers between devices: 13.8 us -> 13.3 us  [exchange(): return lax.ppermute(x, axes, [(i, i ^ step) for i in range(peers)])]
  transfers between devices with their start and end apart: 10 -> 10, of which waited for: 7 -> 5; matrix products, arithmetic and copies ran while one was open for 2% -> 0% of each run, Pallas kernels for 0% -> 8%
where the time goes in v2:
time: 30 us; the launch traced here: 29.8 us
  starting transfers between devices  13.3 us (44%)
  Pallas kernels  9.43 us (31%)
  waiting for transfers between devices  5.7 us (19%)
  between operations  0.7 us (2%)
  other arithmetic  0.65 us (2%)
    ppermute x10, starting transfers between devices, exchange(): return lax.ppermute(x, axes, [(i, i ^ step) for i in range(peers)])  13.3 us
    pallas_call x1, Pallas kernels, gathered_plan(): pl.pallas_call(main_kernel, out_shape=(jax.ShapeDtypeStruct((frames, 1, c...  6.96 us
    ppermute x10, waiting for transfers between devices, exchange(): return lax.ppermute(x, axes, [(i, i ^ step) for i in range(peers)])  5.7 us
    pallas_call x1, Pallas kernels, stage(): pl.pallas_call(stage_kernel, out_shape=tuple((jax.ShapeDtypeStruct(array....  1.55 us
    pallas_call x1, Pallas kernels, pack_near(): pl.pallas_call(near_kernel, out_shape=jax.ShapeDtypeStruct(((len(pieces)...  0.9 us
    unnamed x1, other arithmetic  0.65 us
  transfers between devices with their start and end apart: 10, of which 5 were waited for; matrix products, arithmetic and copies ran while one was open for 0% of the time, Pallas kernels for 8%

profile of v2, /device:TPU:0, one launch (start us, length us, event | category | flops | bytes accessed | tf_op | source)
XLA Modules:
  0.0 29.8 jit_solution(2987839093094610594)
XLA Ops:
  0.6 5.1 %collective-permute-start.5 = (bf16[128,256]{1,0:T(8,128)(2,1)}, bf16[128,256]{1,0:T(8,128)(2,1)S(1)}, u32[]{:S(2)}, u32[]{:S(2)}) collective-permute-start(bf16[128,256]{1,0:T(8,128)(2,1)} %bitcast.9), channel_id=1, source_target_pairs={{0,12},{4,8},{8,4},{12,0},{1,13},{5,9},{9,5},{13,1},{2,14},{6,10},... | collective-permute-start | bytes 196616 | tf_op jit(solution)/shard_map/ppermute | solution.py:138
  5.7 0.0 collective-permute-start.3
  5.7 1.7 %collective-permute-start.2 = (bf16[128,256]{1,0:T(8,128)(2,1)}, bf16[128,256]{1,0:T(8,128)(2,1)S(1)}, u32[]{:S(2)}, u32[]{:S(2)}) collective-permute-start(bf16[128,256]{1,0:T(8,128)(2,1)} %bitcast.11), channel_id=1, source_target_pairs={{0,6},{2,4},{4,2},{6,0},{8,14},{10,12},{12,10},{14,8},{1,7},{3,5},... | collective-permute-start | bytes 196616 | tf_op jit(solution)/shard_map/ppermute | solution.py:138
  7.5 1.2 %collective-permute-start.1 = (bf16[128,256]{1,0:T(8,128)(2,1)}, bf16[128,256]{1,0:T(8,128)(2,1)S(1)}, u32[]{:S(2)}, u32[]{:S(2)}) collective-permute-start(bf16[128,256]{1,0:T(8,128)(2,1)} %bitcast.12), channel_id=1, source_target_pairs={{0,4},{2,6},{4,0},{6,2},{8,12},{10,14},{12,8},{14,10},{1,5},{3,7},... | collective-permute-start | bytes 196616 | tf_op jit(solution)/shard_map/ppermute | solution.py:138
  8.7 0.5 %collective-permute-start = (bf16[128,256]{1,0:T(8,128)(2,1)}, bf16[128,256]{1,0:T(8,128)(2,1)S(1)}, u32[]{:S(2)}, u32[]{:S(2)}) collective-permute-start(bf16[128,256]{1,0:T(8,128)(2,1)} %bitcast.13), channel_id=1, source_target_pairs={{0,2},{2,0},{4,6},{6,4},{8,10},{10,8},{12,14},{14,12},{1,3},{3,1},... | collective-permute-start | bytes 196616 | tf_op jit(solution)/shard_map/ppermute | solution.py:138
  9.2 0.0 collective-permute-done.5.refs_2_
  9.2 1.5 %collective-permute-start.6 = (bf16[128,256]{1,0:T(8,128)(2,1)S(1)}, bf16[128,256]{1,0:T(8,128)(2,1)S(1)}, u32[]{:S(2)}, u32[]{:S(2)}) collective-permute-start(bf16[128,256]{1,0:T(8,128)(2,1)S(1)} %collective-permute-done.5.refs_2_), channel_id=1, source_target_pairs={{0,2},{2,0},{1,3},{3,1},{4,6},{6,4},{5,7},{7,5},{8,10},{10,8},{9,1... | collective-permute-start | bytes 196616 | tf_op jit(solution)/shard_map/ppermute | solution.py:138
  10.7 0.9 %collective-permute-done.3.refs_0_ = bf16[128,256]{1,0:T(8,128)(2,1)S(1)} collective-permute-done((bf16[128,256]{1,0:T(8,128)(2,1)}, bf16[128,256]{1,0:T(8,128)(2,1)S(1)}, u32[]{:S(2)}, u32[]{:S(2)}) %collective-permute-start.3) | collective-permute-done | bytes 65568 | tf_op jit(solution)/shard_map/ppermute | solution.py:138
  11.7 1.5 %collective-permute-start.4 = (bf16[128,256]{1,0:T(8,128)(2,1)S(1)}, bf16[128,256]{1,0:T(8,128)(2,1)S(1)}, u32[]{:S(2)}, u32[]{:S(2)}) collective-permute-start(bf16[128,256]{1,0:T(8,128)(2,1)S(1)} %collective-permute-done.3.refs_0_), channel_id=1, source_target_pairs={{0,2},{2,0},{1,3},{3,1},{4,6},{6,4},{5,7},{7,5},{8,10},{10,8},{9,1... | collective-permute-start | bytes 196616 | tf_op jit(solution)/shard_map/ppermute | solution.py:138
  13.2 0.0 collective-permute-done.2.refs_2_
  13.2 0.1 collective-permute-done.1.refs_1_
  13.2 0.2 collective-permute-done.refs_0_
  13.5 0.9 %near.1.near_ref = bf16[528,256]{1,0:T(8,128)(2,1)S(1)} custom-call(bf16[128,256]{1,0:T(8,128)(2,1)S(1)} %collective-permute-done.refs_0_, bf16[128,256]{1,0:T(8,128)(2,1)S(1)} %collective-permute-done.1.refs_1_, bf16[128,256]{1,0:T(8,128)(2,1)S(1)} %collective-permute-done.2.refs_2_, bf16[128,256]{1,0:T(8,128)(2,1)} %bitcast.14, f32[1,256]{1,0:T(1,128)} %bitcast.15, ...), custom_call_target="tpu_custom_call" | custom-call | tf_op jit(solution)/shard_map/near/pallas_call | solution.py:196
  14.4 0.1 collective-permute-start.7
  14.5 0.0 collective-permute-done.6.refs_3_
  14.5 1.4 %collective-permute-done.4.refs_1_ = bf16[128,256]{1,0:T(8,128)(2,1)S(1)} collective-permute-done((bf16[128,256]{1,0:T(8,128)(2,1)S(1)}, bf16[128,256]{1,0:T(8,128)(2,1)S(1)}, u32[]{:S(2)}, u32[]{:S(2)}) %collective-permute-start.4) | collective-permute-done | bytes 65568 | tf_op jit(solution)/shard_map/ppermute | solution.py:138
  15.9 0.1 collective-permute-start.8
  16.0 1.6 %stage.1 = (bf16[512,512]{1,0:T(8,128)(2,1)S(1)}, bf16[512,512]{1,0:T(8,128)(2,1)S(1)}, bf16[512,512]{1,0:T(8,128)(2,1)S(1)}, bf16[512,512]{1,0:T(8,128)(2,1)S(1)}) custom-call(bf16[512,512]{1,0:T(8,128)(2,1)} %refs_0_.1, bf16[512,512]{1,0:T(8,128)(2,1)} %refs_1_.1, bf16[512,512]{1,0:T(8,128)(2,1)} %refs_2_.1, bf16[512,512]{1,0:T(8,128)(2,1)} %refs_3_.1), custom_call_target="tpu_custom_call" | custom-call | bytes 4194304 | tf_op jit(solution)/shard_map/stage/pallas_call | solution.py:152
  17.6 0.0 collective-permute-done.7.other_near_ref
  17.6 0.0 collective-permute-done.8.other_far_ref
  17.6 7.0 %block.1 = (bf16[2,1,64,256]{3,2,1,0:T(8,128)(2,1)}, f32[2,64,256]{2,1,0:T(8,128)S(1)}, bf16[1,2,64,256]{3,2,1,0:T(8,128)(2,1)S(1)}) custom-call(bf16[528,256]{1,0:T(8,128)(2,1)S(1)} %near.1.near_ref, bf16[512,256]{1,0:T(8,128)(2,1)S(1)} %far.1.far_ref, bf16[528,256]{1,0:T(8,128)(2,1)S(1)} %collective-permute-done.7.other_near_ref, ...), custom_call_target="tpu_custom_call" | custom-call | tf_op jit(solution)/shard_map/block/pallas_call | solution.py:381
  24.6 1.6 %collective-permute-start.9 = (bf16[2,64,256]{2,1,0:T(8,128)(2,1)S(1)}, bf16[2,64,256]{2,1,0:T(8,128)(2,1)S(1)}, u32[]{:S(2)}, u32[]{:S(2)}) collective-permute-start(bf16[2,64,256]{2,1,0:T(8,128)(2,1)S(1)} %bitcast.8), channel_id=1, source_target_pairs={{0,2},{2,0},{1,3},{3,1},{4,6},{6,4},{5,7},{7,5},{8,10},{10,8},{9,1... | collective-permute-start | bytes 196616 | tf_op jit(solution)/shard_map/ppermute | solution.py:138
  26.2 3.0 %collective-permute-done.9 = bf16[2,64,256]{2,1,0:T(8,128)(2,1)S(1)} collective-permute-done((bf16[2,64,256]{2,1,0:T(8,128)(2,1)S(1)}, bf16[2,64,256]{2,1,0:T(8,128)(2,1)S(1)}, u32[]{:S(2)}, u32[]{:S(2)}) %collective-permute-start.9) | collective-permute-done | bytes 65568 | tf_op jit(solution)/shard_map/ppermute | solution.py:138
  29.1 0.6 %fusion = bf16[2,1,64,256]{3,2,1,0:T(8,128)(2,1)} fusion(f32[2,64,256]{2,1,0:T(8,128)S(1)} %get-tuple-element.14, bf16[2,64,256]{2,1,0:T(8,128)(2,1)S(1)} %collective-permute-done.9), kind=kLoop, calls=%fused_computation.1 | loop fusion | flops 98304 | bytes 262144
  (1 shorter events, 0.0 us)
Async XLA Ops:
  0.6 8.6 %collective-permute-start.5 = (bf16[128,256]{1,0:T(8,128)(2,1)}, bf16[128,256]{1,0:T(8,128)(2,1)S(1)}, u32[]{:S(2)}, u32[]{:S(2)}) collective-permute-start(bf16[128,256]{1,0:T(8,128)(2,1)} %bitcast.9), channel_id=1, source_target_pairs={{0,12},{4,8},{8,4},{12,0},{1,13},{5,9},{9,5},{13,1},{2,14},{6,10},... | collective-permute-start | bytes 196616 | tf_op jit(solution)/shard_map/ppermute | solution.py:138
  5.7 5.9 %collective-permute-start.3 = (bf16[128,256]{1,0:T(8,128)(2,1)}, bf16[128,256]{1,0:T(8,128)(2,1)S(1)}, u32[]{:S(2)}, u32[]{:S(2)}) collective-permute-start(bf16[128,256]{1,0:T(8,128)(2,1)} %bitcast.10), channel_id=1, source_target_pairs={{0,8},{4,12},{8,0},{12,4},{1,9},{5,13},{9,1},{13,5},{2,10},{6,14},... | collective-permute-start | bytes 196616 | tf_op jit(solution)/shard_map/ppermute | solution.py:138
  5.7 7.4 %collective-permute-start.2 = (bf16[128,256]{1,0:T(8,128)(2,1)}, bf16[128,256]{1,0:T(8,128)(2,1)S(1)}, u32[]{:S(2)}, u32[]{:S(2)}) collective-permute-start(bf16[128,256]{1,0:T(8,128)(2,1)} %bitcast.11), channel_id=1, source_target_pairs={{0,6},{2,4},{4,2},{6,0},{8,14},{10,12},{12,10},{14,8},{1,7},{3,5},... | collective-permute-start | bytes 196616 | tf_op jit(solution)/shard_map/ppermute | solution.py:138
  7.5 5.8 %collective-permute-start.1 = (bf16[128,256]{1,0:T(8,128)(2,1)}, bf16[128,256]{1,0:T(8,128)(2,1)S(1)}, u32[]{:S(2)}, u32[]{:S(2)}) collective-permute-start(bf16[128,256]{1,0:T(8,128)(2,1)} %bitcast.12), channel_id=1, source_target_pairs={{0,4},{2,6},{4,0},{6,2},{8,12},{10,14},{12,8},{14,10},{1,5},{3,7},... | collective-permute-start | bytes 196616 | tf_op jit(solution)/shard_map/ppermute | solution.py:138
  8.7 4.8 %collective-permute-start = (bf16[128,256]{1,0:T(8,128)(2,1)}, bf16[128,256]{1,0:T(8,128)(2,1)S(1)}, u32[]{:S(2)}, u32[]{:S(2)}) collective-permute-start(bf16[128,256]{1,0:T(8,128)(2,1)} %bitcast.13), channel_id=1, source_target_pairs={{0,2},{2,0},{4,6},{6,4},{8,10},{10,8},{12,14},{14,12},{1,3},{3,1},... | collective-permute-start | bytes 196616 | tf_op jit(solution)/shard_map/ppermute | solution.py:138
  9.2 5.3 %collective-permute-start.6 = (bf16[128,256]{1,0:T(8,128)(2,1)S(1)}, bf16[128,256]{1,0:T(8,128)(2,1)S(1)}, u32[]{:S(2)}, u32[]{:S(2)}) collective-permute-start(bf16[128,256]{1,0:T(8,128)(2,1)S(1)} %collective-permute-done.5.refs_2_), channel_id=1, source_target_pairs={{0,2},{2,0},{1,3},{3,1},{4,6},{6,4},{5,7},{7,5},{8,10},{10,8},{9,1... | collective-permute-start | bytes 196616 | tf_op jit(solution)/shard_map/ppermute | solution.py:138
  11.7 4.3 %collective-permute-start.4 = (bf16[128,256]{1,0:T(8,128)(2,1)S(1)}, bf16[128,256]{1,0:T(8,128)(2,1)S(1)}, u32[]{:S(2)}, u32[]{:S(2)}) collective-permute-start(bf16[128,256]{1,0:T(8,128)(2,1)S(1)} %collective-permute-done.3.refs_0_), channel_id=1, source_target_pairs={{0,2},{2,0},{1,3},{3,1},{4,6},{6,4},{5,7},{7,5},{8,10},{10,8},{9,1... | collective-permute-start | bytes 196616 | tf_op jit(solution)/shard_map/ppermute | solution.py:138
  14.4 3.2 %collective-permute-start.7 = (bf16[528,256]{1,0:T(8,128)(2,1)S(1)}, bf16[528,256]{1,0:T(8,128)(2,1)S(1)}, u32[]{:S(2)}, u32[]{:S(2)}) collective-permute-start(bf16[528,256]{1,0:T(8,128)(2,1)S(1)} %near.1.near_ref), channel_id=1, source_target_pairs={{0,1},{1,0},{2,3},{3,2},{4,5},{5,4},{6,7},{7,6},{8,9},{9,8},{10,11... | collective-permute-start | bytes 811016 | tf_op jit(solution)/shard_map/ppermute | solution.py:138
  15.9 1.7 %collective-permute-start.8 = (bf16[512,256]{1,0:T(8,128)(2,1)S(1)}, bf16[512,256]{1,0:T(8,128)(2,1)S(1)}, u32[]{:S(2)}, u32[]{:S(2)}) collective-permute-start(bf16[512,256]{1,0:T(8,128)(2,1)S(1)} %far.1.far_ref), channel_id=1, source_target_pairs={{0,1},{1,0},{2,3},{3,2},{4,5},{5,4},{6,7},{7,6},{8,9},{9,8},{10,11... | collective-permute-start | bytes 786440 | tf_op jit(solution)/shard_map/ppermute | solution.py:138
  24.6 4.6 %collective-permute-start.9 = (bf16[2,64,256]{2,1,0:T(8,128)(2,1)S(1)}, bf16[2,64,256]{2,1,0:T(8,128)(2,1)S(1)}, u32[]{:S(2)}, u32[]{:S(2)}) collective-permute-start(bf16[2,64,256]{2,1,0:T(8,128)(2,1)S(1)} %bitcast.8), channel_id=1, source_target_pairs={{0,2},{2,0},{1,3},{3,1},{4,6},{6,4},{5,7},{7,5},{8,10},{10,8},{9,1... | collective-permute-start | bytes 196616 | tf_op jit(solution)/shard_map/ppermute | solution.py:138

commit v3 on v0

--- a/solution.py
+++ b/solution.py
@@ -1,6 +1,10 @@
+import functools
+
 import jax
 import jax.numpy as jnp
 from jax import lax
+from jax.experimental import pallas as pl
+from jax.experimental.pallas import tpu as pltpu
 from jax.sharding import PartitionSpec as P
 
 D = 512
@@ -107,7 +111,7 @@
     return running_total.reshape(frame_count, row_count, col_count, out_width).astype(jnp.bfloat16)
 
 
-def on_device(
+def split_plan(
     hidden_states,
     first_gain,
     second_gain,
@@ -126,6 +130,288 @@
     return (attended, convolved)
 
 
+GAIN_ROWS = 16
+
+
+def exchange(x, axes, step):
+    peers = lax.axis_size(axes)
+    return lax.ppermute(x, axes, [(i, i ^ step) for i in range(peers)])
+
+
+def stage_kernel(*refs):
+    count = len(refs) // 2 - 1
+    copies = [pltpu.make_async_copy(refs[i], refs[count + 1 + i], refs[-1].at[i]) for i in range(count)]
+    for copy in copies:
+        copy.start()
+    for copy in copies:
+        copy.wait()
+
+
+def stage(arrays, after):
+    return pl.pallas_call(
+        stage_kernel,
+        out_shape=tuple(jax.ShapeDtypeStruct(array.shape, array.dtype) for array in arrays),
+        in_specs=[pl.BlockSpec(memory_space=pltpu.HBM)] * len(arrays) + [pl.BlockSpec(memory_space=pl.ANY)],
+        out_specs=tuple(pl.BlockSpec(memory_space=pltpu.VMEM) for _ in arrays),
+        scratch_shapes=[pltpu.SemaphoreType.DMA((len(arrays),))],
+        compiler_params=pltpu.CompilerParams(vmem_limit_bytes=1 << 20),
+        name="stage",
+    )(*(in_hbm(array) for array in arrays), after)
+
+
+def pack_kernel(*refs):
+    end = 0
+    for piece_ref in refs[:-1]:
+        start, end = end, end + piece_ref.shape[0]
+        refs[-1][start:end, :] = piece_ref[...]
+
+
+def near_kernel(first_ref, second_ref, *refs):
+    pack_kernel(*refs)
+    parts = split_parts(first_ref[...]) + split_parts(second_ref[...])
+    parts = [part.astype(jnp.float32) for part in parts]
+    parts.append(jnp.zeros((GAIN_ROWS - len(parts), first_ref.shape[1]), jnp.float32))
+    end = refs[-1].shape[0]
+    refs[-1][end - GAIN_ROWS : end, :] = jnp.concatenate(parts, axis=0).astype(jnp.bfloat16)
+
+
+def pack(kernel, pieces, name, gains=()):
+    size = sum(piece.shape[0] for piece in pieces) + (GAIN_ROWS if gains else 0)
+    return pl.pallas_call(
+        kernel,
+        out_shape=jax.ShapeDtypeStruct((size, pieces[0].shape[1]), pieces[0].dtype),
+        compiler_params=pltpu.CompilerParams(vmem_limit_bytes=2 * 1024 * 1024),
+        name=name,
+    )(*gains, *pieces)
+
+
+def in_hbm(array):
+    return pltpu.with_memory_space_constraint(array, pltpu.HBM)
+
+
+def split_parts(values):
+    parts = []
+    for _ in range(3):
+        rounded = values.astype(jnp.bfloat16)
+        parts.append(rounded)
+        values = values - rounded.astype(jnp.float32)
+    return parts
+
+
+def channel_sums(values):
+    tokens, channels = values.shape
+    parts = values.reshape(tokens // 8, 8, channels)
+    return [jnp.sum(jnp.sum(part, axis=0), axis=0, keepdims=True) for part in (parts, parts * parts)]
+
+
+def group_statistics(rows, count):
+    channels = rows[0].shape[1]
+    width = D // NGROUP
+    left = lax.broadcasted_iota(jnp.int32, (channels, channels), 0) // width
+    right = lax.broadcasted_iota(jnp.int32, (channels, channels), 1) // width
+    member = jnp.where(left == right, 1.0, 0.0).astype(jnp.bfloat16)
+    parts = [part for row in rows for part in split_parts(row)]
+    parts += [jnp.zeros((1, channels), jnp.bfloat16)] * (16 - len(parts))
+    totals = jnp.dot(jnp.concatenate(parts, axis=0), member, preferred_element_type=jnp.float32)
+    means = [
+        (totals[at : at + 1] + totals[at + 1 : at + 2] + totals[at + 2 : at + 3]) * (1.0 / count)
+        for at in range(0, 3 * len(rows), 3)
+    ]
+    found = []
+    for centre, square in zip(means[::2], means[1::2]):
+        spread = jnp.maximum(square - centre * centre, 0.0)
+        found.append((centre, lax.rsqrt(spread + EPSILON)))
+    return found
+
+
+def main_kernel(
+    near_ref, far_ref, other_near_ref, other_far_ref, query_ref, key_ref, value_ref, out_weight_ref, kernel_hbm,
+    attended_ref, activated, send_ref, kernel_ref,
+    normed, queries, keyed, valued, mixed, resid, arrived,
+):
+    kernel_copy = pltpu.make_async_copy(kernel_hbm, kernel_ref, arrived)
+    kernel_copy.start()
+    own_frames, _, cols, channels = attended_ref.shape
+    frames, rows = resid.shape[:2]
+    tokens = frames * rows * cols
+    frame_tokens = rows * cols
+    space = lax.axis_index("space")
+    block = lax.axis_index("tm")
+    half = lax.axis_index("chan")
+    width = D // NGROUP
+    count = tokens * width
+    own_rows = pl.ds(pl.multiple_of(half * channels, channels), channels)
+    other_rows = pl.ds(pl.multiple_of((1 - half) * channels, channels), channels)
+
+    blocks = frames // own_frames
+
+    def side_parts(near, far):
+        size = own_frames * cols
+        pieces = [ref[at : at + size, :] for ref in (near, far) for at in range(0, ref.shape[0] - size + 1, size)]
+        laid = []
+        for index in range(blocks):
+            for frame in range(own_frames):
+                at = slice(frame * cols, (frame + 1) * cols)
+                laid += [pieces[row * blocks + index][at] for row in range(rows)]
+        parts = near[near.shape[0] - GAIN_ROWS : near.shape[0], :].astype(jnp.float32)
+        gains = [parts[at : at + 1] + parts[at + 1 : at + 2] + parts[at + 2 : at + 3] for at in (0, 3)]
+        return jnp.concatenate(laid, axis=0), *gains
+
+    sides, first_gains, second_gains = zip(side_parts(near_ref, far_ref), side_parts(other_near_ref, other_far_ref))
+    statistics = group_statistics(
+        channel_sums(sides[0].astype(jnp.float32)) + channel_sums(sides[1].astype(jnp.float32)), count
+    )
+    for side, gain in enumerate(first_gains):
+        centre, scale = statistics[side]
+        normed[side] = ((sides[side].astype(jnp.float32) - centre) * (scale * gain)).astype(jnp.bfloat16)
+
+    for weight_ref, target in zip((query_ref, key_ref, value_ref), (queries, keyed, valued)):
+        target[...] = (
+            jnp.dot(normed[0], weight_ref[own_rows, :], preferred_element_type=jnp.float32)
+            + jnp.dot(normed[1], weight_ref[other_rows, :], preferred_element_type=jnp.float32)
+        ).astype(jnp.bfloat16)
+
+    in_channels = kernel_ref.shape[3]
+    in_cols = pl.ds(pl.multiple_of(block * in_channels, in_channels), in_channels)
+    own_cols = pl.ds(pl.multiple_of(half * channels, channels), channels)
+    mine_in = block == half
+    spans = [slice(frame * frame_tokens, (frame + 1) * frame_tokens) for frame in range(frames)]
+    scores = [
+        lax.dot_general(queries[at, :], keyed[at, :], (((1,), (1,)), ((), ())), preferred_element_type=jnp.float32)
+        for at in spans
+    ]
+    for at, score in zip(spans, scores):
+        peak = jnp.max(score, axis=1, keepdims=True)
+        weights = jnp.exp((score - peak) * (D ** (-0.5)))
+        mass = jnp.sum(weights, axis=1, keepdims=True)
+        blend = jnp.dot(weights.astype(jnp.bfloat16), valued[at, :], preferred_element_type=jnp.float32)
+        mixed[at, :] = (blend * (1.0 / mass)).astype(jnp.bfloat16)
+    projected = jnp.dot(
+        mixed[...], out_weight_ref[:, in_cols], preferred_element_type=jnp.float32
+    ).astype(jnp.bfloat16)
+    source = jnp.where(mine_in, sides[0].astype(jnp.float32), sides[1].astype(jnp.float32))
+    total = source + projected.astype(jnp.float32)
+    resid[...] = total.reshape(frames, rows, cols, in_channels)
+    own_mixed = jnp.concatenate([mixed[at.start : at.start + cols, :] for at in spans[:own_frames]], axis=0)
+    attended_ref[...] = jnp.dot(
+        own_mixed, out_weight_ref[:, own_cols], preferred_element_type=jnp.float32
+    ).astype(jnp.bfloat16).reshape(own_frames, 1, cols, channels)
+
+    kernel_copy.wait()
+    ((centre, scale),) = group_statistics(channel_sums(total), count)
+    scale = scale * jnp.where(mine_in, *second_gains)
+    activated[:, 0:2] = jnp.zeros((3, 2, cols, in_channels), jnp.bfloat16)
+    for tap in range(3):
+        row = space + (tap - 1)
+        inside = jnp.logical_and(row >= 0, row < rows)
+        place = jnp.where(inside, space ^ row, 0)
+        for frame in range(frames):
+            relative = ((frame // own_frames) ^ block) * own_frames + frame % own_frames
+            values = (resid[relative, place] - centre) * scale
+            values = 0.5 * values * (1.0 + jnp.tanh(0.5 * values))
+            activated[tap, frame + 2] = jnp.where(inside, values, 0.0).astype(jnp.bfloat16)
+
+    send_ref[...] = partial_conv(activated, kernel_ref, 1 - block, own_frames).astype(jnp.bfloat16)
+
+
+def partial_conv(activated, kernel_ref, block, frames):
+    cols, in_channels = activated.shape[2:]
+    tokens = frames * cols
+    columns = []
+    for col_tap in range(3):
+        total = None
+        for time_tap in range(3):
+            for row_tap in range(3):
+                window = activated[row_tap, pl.ds(block * frames + time_tap, frames)].reshape(tokens, in_channels)
+                term = jnp.dot(window, kernel_ref[time_tap, row_tap, col_tap], preferred_element_type=jnp.float32)
+                total = term if total is None else total + term
+        columns.append(total)
+    place = lax.broadcasted_iota(jnp.int32, columns[0].shape, 0) % cols
+    left = jnp.where(place == 0, 0.0, pltpu.roll(columns[0], 1, 0))
+    right = jnp.where(place == cols - 1, 0.0, pltpu.roll(columns[2], tokens - 1, 0))
+    return columns[1] + left + right
+
+
+def own_kernel(activated, kernel_ref, attended_ref, attended_hbm, keep_ref, sent):
+    copy = pltpu.make_async_copy(attended_ref, attended_hbm, sent)
+    copy.start()
+    keep_ref[...] = partial_conv(activated, kernel_ref, lax.axis_index("tm"), attended_ref.shape[0])
+    copy.wait()
+
+
+def gathered_plan(
+    hidden_states, first_gain, second_gain, query_weight, key_weight, value_weight, out_weight, conv_kernel
+):
+    frames, _, cols, channels = hidden_states.shape
+    rows, blocks = lax.axis_size("space"), lax.axis_size("tm")
+    own = hidden_states.reshape(frames * cols, channels)
+    gains = (first_gain.reshape(1, channels), second_gain.reshape(1, channels))
+    by_row = {row: exchange(own, "space", row) for row in range(rows - 1, 0, -1)}
+    first = exchange(own, "tm", 1)
+    onward = {row: exchange(piece, "tm", 1) for row, piece in by_row.items() if row >= rows // 2}
+    for row in range(1, rows // 2):
+        onward[row] = exchange(own, ("space", "tm"), row * blocks + 1)
+    *weights, own_staged, first_gain, second_gain = stage(
+        (query_weight, key_weight, value_weight, out_weight, own, *gains), by_row[rows // 2]
+    )
+    near = [own_staged, first]
+    for row in range(1, rows // 2):
+        near += [by_row[row], onward[row]]
+    far = [piece for row in range(rows // 2, rows) for piece in (by_row[row], onward[row])]
+    near_mine = pack(near_kernel, near, "near", (first_gain, second_gain))
+    near_other = exchange(near_mine, "chan", 1)
+    far_mine = pack(pack_kernel, far, "far")
+    far_other = exchange(far_mine, "chan", 1)
+    in_channels, out_channels = conv_kernel.shape[3:]
+    tokens = blocks * frames * rows * cols
+    in_vmem = pl.BlockSpec(memory_space=pltpu.VMEM)
+    attended, activated, send, kernel = pl.pallas_call(
+        main_kernel,
+        out_shape=(
+            jax.ShapeDtypeStruct((frames, 1, cols, channels), jnp.bfloat16),
+            jax.ShapeDtypeStruct((3, blocks * frames + 2, cols, in_channels), jnp.bfloat16),
+            jax.ShapeDtypeStruct((frames * cols, out_channels), jnp.bfloat16),
+            jax.ShapeDtypeStruct(conv_kernel.shape, conv_kernel.dtype),
+        ),
+        in_specs=[in_vmem] * 8 + [pl.BlockSpec(memory_space=pltpu.HBM)],
+        out_specs=(in_vmem,) * 4,
+        scratch_shapes=[pltpu.VMEM((2, tokens, channels), jnp.bfloat16)]
+        + [pltpu.VMEM((tokens, D), jnp.bfloat16)] * 4
+        + [pltpu.VMEM((blocks * frames, rows, cols, in_channels), jnp.float32), pltpu.SemaphoreType.DMA],
+        compiler_params=pltpu.CompilerParams(vmem_limit_bytes=24 * 1024 * 1024),
+        name="block",
+    )(near_mine, far_mine, near_other, far_other, *weights, in_hbm(conv_kernel))
+    received = exchange(send, "tm", 1)
+    attended, keep = pl.pallas_call(
+        own_kernel,
+        out_shape=(
+            jax.ShapeDtypeStruct(attended.shape, attended.dtype),
+            jax.ShapeDtypeStruct((frames * cols, out_channels), jnp.float32),
+        ),
+        in_specs=[in_vmem] * 3,
+        out_specs=(pl.BlockSpec(memory_space=pl.ANY), in_vmem),
+        scratch_shapes=[pltpu.SemaphoreType.DMA],
+        compiler_params=pltpu.CompilerParams(vmem_limit_bytes=4 * 1024 * 1024),
+        name="own",
+    )(activated, kernel, attended)
+    total = keep + received.astype(jnp.float32)
+    return attended, total.astype(jnp.bfloat16).reshape(frames, 1, cols, out_channels)
+
+
+def power_of_two(count):
+    return count & (count - 1) == 0
+
+
+def on_device(hidden_states, *others):
+    frames, rows, cols, channels = hidden_states.shape
+    spaces, blocks = lax.axis_size("space"), lax.axis_size("tm")
+    tokens = frames * blocks * spaces * rows * cols
+    fits = tokens * D <= 2 ** 20 and rows == 1 and lax.axis_size("chan") == 2 and blocks == 2
+    if fits and power_of_two(spaces):
+        return gathered_plan(hidden_states, *others)
+    return split_plan(hidden_states, *others)
+
+
 def solution(mesh):
     placed = (
         P(("groups", "tm"), "space", None, "chan"),

time: 144 us -> 27.3 us (0.19)
  blocking collectives: 78.4 us -> 0 us
  matrix products: 23.1 us -> 0 us
  between operations: 14.5 us -> 0.72 us
  waiting for transfers between devices: 13 us -> 5.57 us
  Pallas kernels: 0 us -> 6.87 us
  starting transfers between devices: 7.81 us -> 13.3 us
  local copies, waits for them, and re-layouts: 3.52 us -> 0 us
  other arithmetic: 2.8 us -> 0.65 us
    psum x2 -> x0, blocking collectives: 40.8 us -> none  [normalize(): lax.psum((jnp.sum(grouped, axis=(0, 2)), jnp.sum(grouped * grouped, axis=...]
    all_gather x3 -> x0, blocking collectives: 30.1 us -> none  [the longest x1 14.3 us: attend(): key_piece = lax.all_gather(keyed, 'space', axis=0, tiled=True)]
    dot_general x31 -> x0, matrix products: 23.1 us -> none  [the longest x27 18.8 us: convolve(): jnp.dot(window, piece[time_tap, row_tap, col_tap], preferred_element_type...]
    all_to_all x2 -> x0, blocking collectives: 7.58 us -> none  [the longest x1 3.79 us: attend(): lax.all_to_all(projected, 'chan', split_axis=1, concat_axis=0, tiled=True)]
    pallas_call x0 -> x5, Pallas kernels: none -> 6.87 us  [the longest x1 4.58 us: gathered_plan(): pl.pallas_call(main_kernel, out_shape=(jax.ShapeDtypeStruct((frames, 1, c...]
    ppermute x3 -> x10, waiting for transfers between devices: 12.3 us -> 5.57 us  [exchange(): return lax.ppermute(x, axes, [(i, i ^ step) for i in range(peers)])]
    ppermute x3 -> x10, starting transfers between devices: 7.77 us -> 13.3 us  [exchange(): return lax.ppermute(x, axes, [(i, i ^ step) for i in range(peers)])]
    slice x4 -> x0, local copies, waits for them, and re-layouts: 1.89 us -> none  [convolve(): padded[time_tap:time_tap + frame_count, row_tap:row_tap + row_count, col_...]
  transfers between devices with their start and end apart: 4 -> 10, of which waited for: 3 -> 5; matrix products, arithmetic and copies ran while one was open for 7% -> 0% of each run, Pallas kernels for 0% -> 8%
where the time goes in v3:
time: 27.3 us; the launch traced here: 27.1 us
  starting transfers between devices  13.3 us (49%)
  Pallas kernels  6.87 us (25%)
  waiting for transfers between devices  5.57 us (20%)
  between operations  0.72 us (3%)
  other arithmetic  0.65 us (2%)
    ppermute x10, starting transfers between devices, exchange(): return lax.ppermute(x, axes, [(i, i ^ step) for i in range(peers)])  13.3 us
    ppermute x10, waiting for transfers between devices, exchange(): return lax.ppermute(x, axes, [(i, i ^ step) for i in range(peers)])  5.57 us
    pallas_call x1, Pallas kernels, gathered_plan(): pl.pallas_call(main_kernel, out_shape=(jax.ShapeDtypeStruct((frames, 1, c...  4.58 us
    pallas_call x1, Pallas kernels, stage(): pl.pallas_call(stage_kernel, out_shape=tuple((jax.ShapeDtypeStruct(array....  1.58 us
    pallas_call x1, Pallas kernels, gathered_plan(): pl.pallas_call(own_kernel, out_shape=(jax.ShapeDtypeStruct(attended.shape...  0.66 us
    convert_element_type x1, other arithmetic, gathered_plan(): total.astype(jnp.bfloat16).reshape(frames, 1, cols, out_channels)  0.65 us
  transfers between devices with their start and end apart: 10, of which 5 were waited for; matrix products, arithmetic and copies ran while one was open for 0% of the time, Pallas kernels for 8%

profile of v3, /device:TPU:0, one launch (start us, length us, event | category | flops | bytes accessed | tf_op | source)
XLA Modules:
  0.0 27.1 jit_solution(17323887629785104027)
XLA Ops:
  0.6 5.1 %collective-permute-start.5 = (bf16[128,256]{1,0:T(8,128)(2,1)}, bf16[128,256]{1,0:T(8,128)(2,1)S(1)}, u32[]{:S(2)}, u32[]{:S(2)}) collective-permute-start(bf16[128,256]{1,0:T(8,128)(2,1)} %bitcast.6), channel_id=1, source_target_pairs={{0,12},{4,8},{8,4},{12,0},{1,13},{5,9},{9,5},{13,1},{2,14},{6,10},... | collective-permute-start | bytes 196616 | tf_op jit(solution)/shard_map/ppermute | solution.py:138
  5.7 0.0 collective-permute-start
  5.7 1.7 %collective-permute-start.3 = (bf16[128,256]{1,0:T(8,128)(2,1)}, bf16[128,256]{1,0:T(8,128)(2,1)S(1)}, u32[]{:S(2)}, u32[]{:S(2)}) collective-permute-start(bf16[128,256]{1,0:T(8,128)(2,1)} %bitcast.8), channel_id=1, source_target_pairs={{0,6},{2,4},{4,2},{6,0},{8,14},{10,12},{12,10},{14,8},{1,7},{3,5},... | collective-permute-start | bytes 196616 | tf_op jit(solution)/shard_map/ppermute | solution.py:138
  7.5 1.2 %collective-permute-start.2 = (bf16[128,256]{1,0:T(8,128)(2,1)}, bf16[128,256]{1,0:T(8,128)(2,1)S(1)}, u32[]{:S(2)}, u32[]{:S(2)}) collective-permute-start(bf16[128,256]{1,0:T(8,128)(2,1)} %bitcast.9), channel_id=1, source_target_pairs={{0,4},{4,0},{8,12},{12,8},{1,5},{5,1},{9,13},{13,9},{2,6},{6,2},{1... | collective-permute-start | bytes 196616 | tf_op jit(solution)/shard_map/ppermute | solution.py:138
  8.7 0.5 %collective-permute-start.1 = (bf16[128,256]{1,0:T(8,128)(2,1)}, bf16[128,256]{1,0:T(8,128)(2,1)S(1)}, u32[]{:S(2)}, u32[]{:S(2)}) collective-permute-start(bf16[128,256]{1,0:T(8,128)(2,1)} %bitcast.10), channel_id=1, source_target_pairs={{0,2},{2,0},{1,3},{3,1},{4,6},{6,4},{5,7},{7,5},{8,10},{10,8},{9,1... | collective-permute-start | bytes 196616 | tf_op jit(solution)/shard_map/ppermute | solution.py:138
  9.2 0.0 collective-permute-done.5.refs_2_
  9.2 1.5 %collective-permute-start.6 = (bf16[128,256]{1,0:T(8,128)(2,1)S(1)}, bf16[128,256]{1,0:T(8,128)(2,1)S(1)}, u32[]{:S(2)}, u32[]{:S(2)}) collective-permute-start(bf16[128,256]{1,0:T(8,128)(2,1)S(1)} %collective-permute-done.5.refs_2_), channel_id=1, source_target_pairs={{0,2},{2,0},{1,3},{3,1},{4,6},{6,4},{5,7},{7,5},{8,10},{10,8},{9,1... | collective-permute-start | bytes 196616 | tf_op jit(solution)/shard_map/ppermute | solution.py:138
  10.7 0.9 %collective-permute-done.refs_7_.refs_0_ = bf16[128,256]{1,0:T(8,128)(2,1)S(1)} collective-permute-done((bf16[128,256]{1,0:T(8,128)(2,1)}, bf16[128,256]{1,0:T(8,128)(2,1)S(1)}, u32[]{:S(2)}, u32[]{:S(2)}) %collective-permute-start) | collective-permute-done | bytes 65568 | tf_op jit(solution)/shard_map/ppermute | solution.py:138
  11.7 1.5 %collective-permute-start.4 = (bf16[128,256]{1,0:T(8,128)(2,1)S(1)}, bf16[128,256]{1,0:T(8,128)(2,1)S(1)}, u32[]{:S(2)}, u32[]{:S(2)}) collective-permute-start(bf16[128,256]{1,0:T(8,128)(2,1)S(1)} %collective-permute-done.refs_7_.refs_0_), channel_id=1, source_target_pairs={{0,2},{2,0},{1,3},{3,1},{4,6},{6,4},{5,7},{7,5},{8,10},{10,8},{9,1... | collective-permute-start | bytes 196616 | tf_op jit(solution)/shard_map/ppermute | solution.py:138
  13.2 1.6 %stage.1 = (bf16[512,512]{1,0:T(8,128)(2,1)S(1)}, bf16[512,512]{1,0:T(8,128)(2,1)S(1)}, bf16[512,512]{1,0:T(8,128)(2,1)S(1)}, bf16[512,512]{1,0:T(8,128)(2,1)S(1...) custom-call(bf16[512,512]{1,0:T(8,128)(2,1)} %refs_0_.1, bf16[512,512]{1,0:T(8,128)(2,1)} %refs_1_.1, ...), custom_call_target="tpu_custom_call" | custom-call | tf_op jit(solution)/shard_map/stage/pallas_call | solution.py:151
  14.7 0.0 collective-permute-done.3.refs_3_
  14.8 0.0 collective-permute-done.2.refs_2_
  14.8 0.0 collective-permute-done.1.refs_1_
  14.8 0.1 collective-permute-start.7
  14.9 0.0 collective-permute-done.6.refs_3_
  14.9 1.0 %collective-permute-done.4.refs_1_ = bf16[128,256]{1,0:T(8,128)(2,1)S(1)} collective-permute-done((bf16[128,256]{1,0:T(8,128)(2,1)S(1)}, bf16[128,256]{1,0:T(8,128)(2,1)S(1)}, u32[]{:S(2)}, u32[]{:S(2)}) %collective-permute-start.4) | collective-permute-done | bytes 65568 | tf_op jit(solution)/shard_map/ppermute | solution.py:138
  15.9 0.1 collective-permute-start.8
  16.0 0.4 %collective-permute-done.7.other_near_ref = bf16[528,256]{1,0:T(8,128)(2,1)S(1)} collective-permute-done((bf16[528,256]{1,0:T(8,128)(2,1)S(1)}, bf16[528,256]{1,0:T(8,128)(2,1)S(1)}, u32[]{:S(2)}, u32[]{:S(2)}) %collective-permute-start.7) | collective-permute-done | bytes 270368 | tf_op jit(solution)/shard_map/ppermute | solution.py:138
  16.4 1.1 %collective-permute-done.8.other_far_ref = bf16[512,256]{1,0:T(8,128)(2,1)S(1)} collective-permute-done((bf16[512,256]{1,0:T(8,128)(2,1)S(1)}, bf16[512,256]{1,0:T(8,128)(2,1)S(1)}, u32[]{:S(2)}, u32[]{:S(2)}) %collective-permute-start.8) | collective-permute-done | bytes 262176 | tf_op jit(solution)/shard_map/ppermute | solution.py:138
  17.5 4.6 %block.1 = (bf16[2,1,64,256]{3,2,1,0:T(8,128)(2,1)S(1)}, bf16[3,6,64,256]{3,2,1,0:T(8,128)(2,1)S(1)}, bf16[128,256]{1,0:T(8,128)(2,1)S(1)}, bf16[3,3,3,256,256]{4,3,2,1,0:T(8,128)(2,1)S(1)}) custom-call(bf16[528,256]{1,0:T(8,128)(2,1)S(1)} %near.1.near_ref, bf16[512,256]{1,0:T(8,128)(2,1)S(1)} %far.1.far_ref, ...), custom_call_target="tpu_custom_call" | custom-call | tf_op jit(solution)/shard_map/block/pallas_call | solution.py:368
  22.1 1.6 %collective-permute-start.9 = (bf16[128,256]{1,0:T(8,128)(2,1)S(1)}, bf16[128,256]{1,0:T(8,128)(2,1)S(1)}, u32[]{:S(2)}, u32[]{:S(2)}) collective-permute-start(bf16[128,256]{1,0:T(8,128)(2,1)S(1)} %get-tuple-element.27), channel_id=1, source_target_pairs={{0,2},{2,0},{1,3},{3,1},{4,6},{6,4},{5,7},{7,5},{8,10},{10,8},{9,1... | collective-permute-start | bytes 196616 | tf_op jit(solution)/shard_map/ppermute | solution.py:138
  23.7 0.7 %own.1 = (bf16[2,1,64,256]{3,2,1,0:T(8,128)(2,1)}, f32[128,256]{1,0:T(8,128)S(1)}) custom-call(bf16[3,6,64,256]{3,2,1,0:T(8,128)(2,1)S(1)} %get-tuple-element.22.activated, bf16[3,3,3,256,256]{4,3,2,1,0:T(8,128)(2,1)S(1)} %get-tuple-element.23.kernel_ref, bf16[2,1,64,256]{3,2,1,0:T(8,128)(2,1)S(1)} %get-tuple-element.24.attended_ref), custom_call_target="tpu_custom_call" | custom-call | tf_op jit(solution)/shard_map/own/pallas_call | solution.py:385
  24.4 2.1 %collective-permute-done.9 = bf16[128,256]{1,0:T(8,128)(2,1)S(1)} collective-permute-done((bf16[128,256]{1,0:T(8,128)(2,1)S(1)}, bf16[128,256]{1,0:T(8,128)(2,1)S(1)}, u32[]{:S(2)}, u32[]{:S(2)}) %collective-permute-start.9) | collective-permute-done | bytes 65568 | tf_op jit(solution)/shard_map/ppermute | solution.py:138
  26.5 0.6 %add_convert_fusion = bf16[128,256]{1,0:T(8,128)(2,1)} fusion(f32[128,256]{1,0:T(8,128)S(1)} %get-tuple-element.26, bf16[128,256]{1,0:T(8,128)(2,1)S(1)} %collective-permute-done.9), kind=kLoop, calls=%fused_computation | loop fusion | flops 98304 | bytes 262144 | tf_op jit(solution)/shard_map/convert_element_type | solution.py:398
  (2 shorter events, 0.1 us)
Async XLA Ops:
  0.6 8.6 %collective-permute-start.5 = (bf16[128,256]{1,0:T(8,128)(2,1)}, bf16[128,256]{1,0:T(8,128)(2,1)S(1)}, u32[]{:S(2)}, u32[]{:S(2)}) collective-permute-start(bf16[128,256]{1,0:T(8,128)(2,1)} %bitcast.6), channel_id=1, source_target_pairs={{0,12},{4,8},{8,4},{12,0},{1,13},{5,9},{9,5},{13,1},{2,14},{6,10},... | collective-permute-start | bytes 196616 | tf_op jit(solution)/shard_map/ppermute | solution.py:138
  5.7 5.9 %collective-permute-start = (bf16[128,256]{1,0:T(8,128)(2,1)}, bf16[128,256]{1,0:T(8,128)(2,1)S(1)}, u32[]{:S(2)}, u32[]{:S(2)}) collective-permute-start(bf16[128,256]{1,0:T(8,128)(2,1)} %bitcast.7), channel_id=1, source_target_pairs={{0,8},{4,12},{8,0},{12,4},{1,9},{5,13},{9,1},{13,5},{2,10},{6,14},... | collective-permute-start | bytes 196616 | tf_op jit(solution)/shard_map/ppermute | solution.py:138
  5.7 9.0 %collective-permute-start.3 = (bf16[128,256]{1,0:T(8,128)(2,1)}, bf16[128,256]{1,0:T(8,128)(2,1)S(1)}, u32[]{:S(2)}, u32[]{:S(2)}) collective-permute-start(bf16[128,256]{1,0:T(8,128)(2,1)} %bitcast.8), channel_id=1, source_target_pairs={{0,6},{2,4},{4,2},{6,0},{8,14},{10,12},{12,10},{14,8},{1,7},{3,5},... | collective-permute-start | bytes 196616 | tf_op jit(solution)/shard_map/ppermute | solution.py:138
  7.5 7.3 %collective-permute-start.2 = (bf16[128,256]{1,0:T(8,128)(2,1)}, bf16[128,256]{1,0:T(8,128)(2,1)S(1)}, u32[]{:S(2)}, u32[]{:S(2)}) collective-permute-start(bf16[128,256]{1,0:T(8,128)(2,1)} %bitcast.9), channel_id=1, source_target_pairs={{0,4},{4,0},{8,12},{12,8},{1,5},{5,1},{9,13},{13,9},{2,6},{6,2},{1... | collective-permute-start | bytes 196616 | tf_op jit(solution)/shard_map/ppermute | solution.py:138
  8.7 6.1 %collective-permute-start.1 = (bf16[128,256]{1,0:T(8,128)(2,1)}, bf16[128,256]{1,0:T(8,128)(2,1)S(1)}, u32[]{:S(2)}, u32[]{:S(2)}) collective-permute-start(bf16[128,256]{1,0:T(8,128)(2,1)} %bitcast.10), channel_id=1, source_target_pairs={{0,2},{2,0},{1,3},{3,1},{4,6},{6,4},{5,7},{7,5},{8,10},{10,8},{9,1... | collective-permute-start | bytes 196616 | tf_op jit(solution)/shard_map/ppermute | solution.py:138
  9.2 5.7 %collective-permute-start.6 = (bf16[128,256]{1,0:T(8,128)(2,1)S(1)}, bf16[128,256]{1,0:T(8,128)(2,1)S(1)}, u32[]{:S(2)}, u32[]{:S(2)}) collective-permute-start(bf16[128,256]{1,0:T(8,128)(2,1)S(1)} %collective-permute-done.5.refs_2_), channel_id=1, source_target_pairs={{0,2},{2,0},{1,3},{3,1},{4,6},{6,4},{5,7},{7,5},{8,10},{10,8},{9,1... | collective-permute-start | bytes 196616 | tf_op jit(solution)/shard_map/ppermute | solution.py:138
  11.7 4.3 %collective-permute-start.4 = (bf16[128,256]{1,0:T(8,128)(2,1)S(1)}, bf16[128,256]{1,0:T(8,128)(2,1)S(1)}, u32[]{:S(2)}, u32[]{:S(2)}) collective-permute-start(bf16[128,256]{1,0:T(8,128)(2,1)S(1)} %collective-permute-done.refs_7_.refs_0_), channel_id=1, source_target_pairs={{0,2},{2,0},{1,3},{3,1},{4,6},{6,4},{5,7},{7,5},{8,10},{10,8},{9,1... | collective-permute-start | bytes 196616 | tf_op jit(solution)/shard_map/ppermute | solution.py:138
  14.8 1.6 %collective-permute-start.7 = (bf16[528,256]{1,0:T(8,128)(2,1)S(1)}, bf16[528,256]{1,0:T(8,128)(2,1)S(1)}, u32[]{:S(2)}, u32[]{:S(2)}) collective-permute-start(bf16[528,256]{1,0:T(8,128)(2,1)S(1)} %near.1.near_ref), channel_id=1, source_target_pairs={{0,1},{1,0},{2,3},{3,2},{4,5},{5,4},{6,7},{7,6},{8,9},{9,8},{10,11... | collective-permute-start | bytes 811016 | tf_op jit(solution)/shard_map/ppermute | solution.py:138
  15.9 1.6 %collective-permute-start.8 = (bf16[512,256]{1,0:T(8,128)(2,1)S(1)}, bf16[512,256]{1,0:T(8,128)(2,1)S(1)}, u32[]{:S(2)}, u32[]{:S(2)}) collective-permute-start(bf16[512,256]{1,0:T(8,128)(2,1)S(1)} %far.1.far_ref), channel_id=1, source_target_pairs={{0,1},{1,0},{2,3},{3,2},{4,5},{5,4},{6,7},{7,6},{8,9},{9,8},{10,11... | collective-permute-start | bytes 786440 | tf_op jit(solution)/shard_map/ppermute | solution.py:138
  22.1 4.3 %collective-permute-start.9 = (bf16[128,256]{1,0:T(8,128)(2,1)S(1)}, bf16[128,256]{1,0:T(8,128)(2,1)S(1)}, u32[]{:S(2)}, u32[]{:S(2)}) collective-permute-start(bf16[128,256]{1,0:T(8,128)(2,1)S(1)} %get-tuple-element.27), channel_id=1, source_target_pairs={{0,2},{2,0},{1,3},{3,1},{4,6},{6,4},{5,7},{7,5},{8,10},{10,8},{9,1... | collective-permute-start | bytes 196616 | tf_op jit(solution)/shard_map/ppermute | solution.py:138

commit v4 on v3

--- a/solution.py
+++ b/solution.py
@@ -140,17 +140,23 @@
 
 def stage_kernel(*refs):
     count = len(refs) // 2 - 1
-    copies = [pltpu.make_async_copy(refs[i], refs[count + 1 + i], refs[-1].at[i]) for i in range(count)]
+    targets = refs[count + 1 : -1]
+    copies = [
+        pltpu.make_async_copy(source.at[pl.ds(0, target.shape[0])], target, refs[-1].at[i])
+        for i, (source, target) in enumerate(zip(refs, targets))
+    ]
     for copy in copies:
         copy.start()
     for copy in copies:
         copy.wait()
 
 
-def stage(arrays, after):
+def stage(arrays, sizes, after):
     return pl.pallas_call(
         stage_kernel,
-        out_shape=tuple(jax.ShapeDtypeStruct(array.shape, array.dtype) for array in arrays),
+        out_shape=tuple(
+            jax.ShapeDtypeStruct((size, *array.shape[1:]), array.dtype) for array, size in zip(arrays, sizes)
+        ),
         in_specs=[pl.BlockSpec(memory_space=pltpu.HBM)] * len(arrays) + [pl.BlockSpec(memory_space=pl.ANY)],
         out_specs=tuple(pl.BlockSpec(memory_space=pltpu.VMEM) for _ in arrays),
         scratch_shapes=[pltpu.SemaphoreType.DMA((len(arrays),))],
@@ -224,12 +230,48 @@
     return found
 
 
+def core_tokens(near, far, layout):
+    own_frames, cols, rows, blocks = layout
+    size = own_frames * cols
+    pieces = [ref[at : at + size, :] for ref in (near, far) for at in range(0, ref.shape[0] - size + 1, size)]
+    laid = []
+    for index in range(blocks):
+        for frame in range(own_frames):
+            at = slice(frame * cols, (frame + 1) * cols)
+            laid += [pieces[row * blocks + index][at] for row in range(rows)]
+    parts = near[near.shape[0] - GAIN_ROWS : near.shape[0], :].astype(jnp.float32)
+    gains = [parts[at : at + 1] + parts[at + 1 : at + 2] + parts[at + 2 : at + 3] for at in (0, 3)]
+    return jnp.concatenate(laid, axis=0), *gains
+
+
+def normed_tokens(tokens, gain):
+    values = tokens.astype(jnp.float32)
+    ((centre, scale),) = group_statistics(channel_sums(values), tokens.shape[0] * (D // NGROUP))
+    return ((values - centre) * (scale * gain)).astype(jnp.bfloat16)
+
+
+def mine_kernel(
+    near_ref, far_ref, query_ref, key_ref, value_ref, kernel_hbm,
+    begun_query, begun_key, begun_value, early_ref, normed, arrived, *, layout,
+):
+    copy = pltpu.make_async_copy(kernel_hbm.at[pl.ds(1, early_ref.shape[0])], early_ref, arrived)
+    copy.start()
+    tokens, gain, _ = core_tokens(near_ref, far_ref, layout)
+    normed[...] = normed_tokens(tokens, gain)
+    channels = normed.shape[1]
+    rows = pl.ds(pl.multiple_of(lax.axis_index("chan") * channels, channels), channels)
+    for weight_ref, target in zip((query_ref, key_ref, value_ref), (begun_query, begun_key, begun_value)):
+        target[...] = jnp.dot(normed[...], weight_ref[rows, :], preferred_element_type=jnp.float32)
+    copy.wait()
+
+
 def main_kernel(
-    near_ref, far_ref, other_near_ref, other_far_ref, query_ref, key_ref, value_ref, out_weight_ref, kernel_hbm,
-    attended_ref, activated, send_ref, kernel_ref,
+    near_ref, far_ref, other_near_ref, other_far_ref, query_ref, key_ref, value_ref, begun_query, begun_key, begun_value,
+    out_weight_ref, first_tap, second_tap, kernel_hbm,
+    attended_ref, activated, send_ref, last_tap,
     normed, queries, keyed, valued, mixed, resid, arrived,
 ):
-    kernel_copy = pltpu.make_async_copy(kernel_hbm, kernel_ref, arrived)
+    kernel_copy = pltpu.make_async_copy(kernel_hbm.at[pl.ds(2, 1)], last_tap, arrived)
     kernel_copy.start()
     own_frames, _, cols, channels = attended_ref.shape
     frames, rows = resid.shape[:2]
@@ -240,38 +282,22 @@
     half = lax.axis_index("chan")
     width = D // NGROUP
     count = tokens * width
-    own_rows = pl.ds(pl.multiple_of(half * channels, channels), channels)
     other_rows = pl.ds(pl.multiple_of((1 - half) * channels, channels), channels)
 
     blocks = frames // own_frames
 
-    def side_parts(near, far):
-        size = own_frames * cols
-        pieces = [ref[at : at + size, :] for ref in (near, far) for at in range(0, ref.shape[0] - size + 1, size)]
-        laid = []
-        for index in range(blocks):
-            for frame in range(own_frames):
-                at = slice(frame * cols, (frame + 1) * cols)
-                laid += [pieces[row * blocks + index][at] for row in range(rows)]
-        parts = near[near.shape[0] - GAIN_ROWS : near.shape[0], :].astype(jnp.float32)
-        gains = [parts[at : at + 1] + parts[at + 1 : at + 2] + parts[at + 2 : at + 3] for at in (0, 3)]
-        return jnp.concatenate(laid, axis=0), *gains
-
-    sides, first_gains, second_gains = zip(side_parts(near_ref, far_ref), side_parts(other_near_ref, other_far_ref))
-    statistics = group_statistics(
-        channel_sums(sides[0].astype(jnp.float32)) + channel_sums(sides[1].astype(jnp.float32)), count
-    )
-    for side, gain in enumerate(first_gains):
-        centre, scale = statistics[side]
-        normed[side] = ((sides[side].astype(jnp.float32) - centre) * (scale * gain)).astype(jnp.bfloat16)
-
-    for weight_ref, target in zip((query_ref, key_ref, value_ref), (queries, keyed, valued)):
-        target[...] = (
-            jnp.dot(normed[0], weight_ref[own_rows, :], preferred_element_type=jnp.float32)
-            + jnp.dot(normed[1], weight_ref[other_rows, :], preferred_element_type=jnp.float32)
-        ).astype(jnp.bfloat16)
-
-    in_channels = kernel_ref.shape[3]
+    layout = (own_frames, cols, rows, blocks)
+    sides, first_gains, second_gains = zip(
+        core_tokens(near_ref, far_ref, layout), core_tokens(other_near_ref, other_far_ref, layout)
+    )
+    normed[...] = normed_tokens(sides[1], first_gains[1])
+    for weight_ref, begun_ref, target in zip(
+        (query_ref, key_ref, value_ref), (begun_query, begun_key, begun_value), (queries, keyed, valued)
+    ):
+        term = jnp.dot(normed[...], weight_ref[other_rows, :], preferred_element_type=jnp.float32)
+        target[...] = (begun_ref[...] + term).astype(jnp.bfloat16)
+
+    in_channels = first_tap.shape[3]
     in_cols = pl.ds(pl.multiple_of(block * in_channels, in_channels), in_channels)
     own_cols = pl.ds(pl.multiple_of(half * channels, channels), channels)
     mine_in = block == half
@@ -289,8 +315,8 @@
     projected = jnp.dot(
         mixed[...], out_weight_ref[:, in_cols], preferred_element_type=jnp.float32
     ).astype(jnp.bfloat16)
-    source = jnp.where(mine_in, sides[0].astype(jnp.float32), sides[1].astype(jnp.float32))
-    total = source + projected.astype(jnp.float32)
+    source = jnp.where(mine_in, sides[0], sides[1])
+    total = source.astype(jnp.float32) + projected.astype(jnp.float32)
     resid[...] = total.reshape(frames, rows, cols, in_channels)
     own_mixed = jnp.concatenate([mixed[at.start : at.start + cols, :] for at in spans[:own_frames]], axis=0)
     attended_ref[...] = jnp.dot(
@@ -311,10 +337,10 @@
             values = 0.5 * values * (1.0 + jnp.tanh(0.5 * values))
             activated[tap, frame + 2] = jnp.where(inside, values, 0.0).astype(jnp.bfloat16)
 
-    send_ref[...] = partial_conv(activated, kernel_ref, 1 - block, own_frames).astype(jnp.bfloat16)
-
-
-def partial_conv(activated, kernel_ref, block, frames):
+    send_ref[...] = partial_conv(activated, (first_tap, second_tap, last_tap), 1 - block, own_frames).astype(jnp.bfloat16)
+
+
+def partial_conv(activated, taps, block, frames):
     cols, in_channels = activated.shape[2:]
     tokens = frames * cols
     columns = []
@@ -323,7 +349,7 @@
         for time_tap in range(3):
             for row_tap in range(3):
                 window = activated[row_tap, pl.ds(block * frames + time_tap, frames)].reshape(tokens, in_channels)
-                term = jnp.dot(window, kernel_ref[time_tap, row_tap, col_tap], preferred_element_type=jnp.float32)
+                term = jnp.dot(window, taps[time_tap][0, row_tap, col_tap], preferred_element_type=jnp.float32)
                 total = term if total is None else total + term
         columns.append(total)
     place = lax.broadcasted_iota(jnp.int32, columns[0].shape, 0) % cols
@@ -332,10 +358,10 @@
     return columns[1] + left + right
 
 
-def own_kernel(activated, kernel_ref, attended_ref, attended_hbm, keep_ref, sent):
+def own_kernel(activated, first_tap, second_tap, last_tap, attended_ref, attended_hbm, keep_ref, sent):
     copy = pltpu.make_async_copy(attended_ref, attended_hbm, sent)
     copy.start()
-    keep_ref[...] = partial_conv(activated, kernel_ref, lax.axis_index("tm"), attended_ref.shape[0])
+    keep_ref[...] = partial_conv(activated, (first_tap, second_tap, last_tap), lax.axis_index("tm"), attended_ref.shape[0])
     copy.wait()
 
 
@@ -351,8 +377,9 @@
     onward = {row: exchange(piece, "tm", 1) for row, piece in by_row.items() if row >= rows // 2}
     for row in range(1, rows // 2):
         onward[row] = exchange(own, ("space", "tm"), row * blocks + 1)
-    *weights, own_staged, first_gain, second_gain = stage(
-        (query_weight, key_weight, value_weight, out_weight, own, *gains), by_row[rows // 2]
+    staged = (query_weight, key_weight, value_weight, out_weight, own, *gains, conv_kernel)
+    *weights, own_staged, first_gain, second_gain, first_tap = stage(
+        staged, [array.shape[0] for array in staged[:-1]] + [1], by_row[rows // 2]
     )
     near = [own_staged, first]
     for row in range(1, rows // 2):
@@ -365,22 +392,32 @@
     in_channels, out_channels = conv_kernel.shape[3:]
     tokens = blocks * frames * rows * cols
     in_vmem = pl.BlockSpec(memory_space=pltpu.VMEM)
-    attended, activated, send, kernel = pl.pallas_call(
+    *begun, second_tap = pl.pallas_call(
+        functools.partial(mine_kernel, layout=(frames, cols, rows, blocks)),
+        out_shape=(jax.ShapeDtypeStruct((tokens, D), jnp.float32),) * 3
+        + (jax.ShapeDtypeStruct((1, *conv_kernel.shape[1:]), conv_kernel.dtype),),
+        in_specs=[in_vmem] * 5 + [pl.BlockSpec(memory_space=pltpu.HBM)],
+        out_specs=(in_vmem,) * 4,
+        scratch_shapes=[pltpu.VMEM((tokens, channels), jnp.bfloat16), pltpu.SemaphoreType.DMA],
+        compiler_params=pltpu.CompilerParams(vmem_limit_bytes=8 * 1024 * 1024),
+        name="mine",
+    )(near_mine, far_mine, *weights[:3], in_hbm(conv_kernel))
+    attended, activated, send, last_tap = pl.pallas_call(
         main_kernel,
         out_shape=(
             jax.ShapeDtypeStruct((frames, 1, cols, channels), jnp.bfloat16),
             jax.ShapeDtypeStruct((3, blocks * frames + 2, cols, in_channels), jnp.bfloat16),
             jax.ShapeDtypeStruct((frames * cols, out_channels), jnp.bfloat16),
-            jax.ShapeDtypeStruct(conv_kernel.shape, conv_kernel.dtype),
+            jax.ShapeDtypeStruct((1, *conv_kernel.shape[1:]), conv_kernel.dtype),
         ),
-        in_specs=[in_vmem] * 8 + [pl.BlockSpec(memory_space=pltpu.HBM)],
+        in_specs=[in_vmem] * 13 + [pl.BlockSpec(memory_space=pltpu.HBM)],
         out_specs=(in_vmem,) * 4,
-        scratch_shapes=[pltpu.VMEM((2, tokens, channels), jnp.bfloat16)]
+        scratch_shapes=[pltpu.VMEM((tokens, channels), jnp.bfloat16)]
         + [pltpu.VMEM((tokens, D), jnp.bfloat16)] * 4
         + [pltpu.VMEM((blocks * frames, rows, cols, in_channels), jnp.float32), pltpu.SemaphoreType.DMA],
         compiler_params=pltpu.CompilerParams(vmem_limit_bytes=24 * 1024 * 1024),
         name="block",
-    )(near_mine, far_mine, near_other, far_other, *weights, in_hbm(conv_kernel))
+    )(near_mine, far_mine, near_other, far_other, *weights[:3], *begun, weights[3], first_tap, second_tap, in_hbm(conv_kernel))
     received = exchange(send, "tm", 1)
     attended, keep = pl.pallas_call(
         own_kernel,
@@ -388,12 +425,12 @@
             jax.ShapeDtypeStruct(attended.shape, attended.dtype),
             jax.ShapeDtypeStruct((frames * cols, out_channels), jnp.float32),
         ),
-        in_specs=[in_vmem] * 3,
+        in_specs=[in_vmem] * 5,
         out_specs=(pl.BlockSpec(memory_space=pl.ANY), in_vmem),
         scratch_shapes=[pltpu.SemaphoreType.DMA],
         compiler_params=pltpu.CompilerParams(vmem_limit_bytes=4 * 1024 * 1024),
         name="own",
-    )(activated, kernel, attended)
+    )(activated, first_tap, second_tap, last_tap, attended)
     total = keep + received.astype(jnp.float32)
     return attended, total.astype(jnp.bfloat16).reshape(frames, 1, cols, out_channels)
 

time: 27.3 us -> 26.6 us (0.974)
  waiting for transfers between devices: 5.57 us -> 3.83 us
  Pallas kernels: 6.87 us -> 7.92 us
    pallas_call x1 -> x2, Pallas kernels: 1.58 us -> 3.55 us  [the longest x1 2.03 us: stage(): pl.pallas_call(stage_kernel, out_shape=tuple((jax.ShapeDtypeStruct((size,...]
    ppermute x10, waiting for transfers between devices: 5.57 us -> 3.83 us  [exchange(): return lax.ppermute(x, axes, [(i, i ^ step) for i in range(peers)])]
    pallas_call x1, Pallas kernels: 4.58 us -> 3.64 us  [gathered_plan(): pl.pallas_call(main_kernel, out_shape=(jax.ShapeDtypeStruct((frames, 1, c...]
  transfers between devices with their start and end apart: 10 -> 10, of which waited for: 5 -> 3; matrix products, arithmetic and copies ran while one was open for 0% -> 0% of each run, Pallas kernels for 8% -> 16%
where the time goes in v4:
time: 26.6 us; the launch traced here: 26.4 us
  starting transfers between devices  13.3 us (50%)
  Pallas kernels  7.92 us (30%)
  waiting for transfers between devices  3.83 us (14%)
  between operations  0.74 us (3%)
  other arithmetic  0.64 us (2%)
    ppermute x10, starting transfers between devices, exchange(): return lax.ppermute(x, axes, [(i, i ^ step) for i in range(peers)])  13.3 us
    ppermute x10, waiting for transfers between devices, exchange(): return lax.ppermute(x, axes, [(i, i ^ step) for i in range(peers)])  3.83 us
    pallas_call x1, Pallas kernels, gathered_plan(): pl.pallas_call(main_kernel, out_shape=(jax.ShapeDtypeStruct((frames, 1, c...  3.64 us
    pallas_call x1, Pallas kernels, stage(): pl.pallas_call(stage_kernel, out_shape=tuple((jax.ShapeDtypeStruct((size,...  2.03 us
    pallas_call x1, Pallas kernels, gathered_plan(): pl.pallas_call(functools.partial(mine_kernel, layout=(frames, cols, rows,...  1.52 us
    pallas_call x1, Pallas kernels, gathered_plan(): pl.pallas_call(own_kernel, out_shape=(jax.ShapeDtypeStruct(attended.shape...  0.67 us
    convert_element_type x1, other arithmetic, gathered_plan(): total.astype(jnp.bfloat16).reshape(frames, 1, cols, out_channels)  0.64 us
  transfers between devices with their start and end apart: 10, of which 3 were waited for; matrix products, arithmetic and copies ran while one was open for 0% of the time, Pallas kernels for 16%

profile of v4, /device:TPU:0, one launch (start us, length us, event | category | flops | bytes accessed | tf_op | source)
XLA Modules:
  0.0 26.4 jit_solution(17498662835256215316)
XLA Ops:
  0.6 5.1 %collective-permute-start.5 = (bf16[128,256]{1,0:T(8,128)(2,1)}, bf16[128,256]{1,0:T(8,128)(2,1)S(1)}, u32[]{:S(2)}, u32[]{:S(2)}) collective-permute-start(bf16[128,256]{1,0:T(8,128)(2,1)} %bitcast.6), channel_id=1, source_target_pairs={{0,12},{4,8},{8,4},{12,0},{1,13},{5,9},{9,5},{13,1},{2,14},{6,10},... | collective-permute-start | bytes 196616 | tf_op jit(solution)/shard_map/ppermute | solution.py:138
  5.7 0.0 collective-permute-start
  5.7 1.7 %collective-permute-start.3 = (bf16[128,256]{1,0:T(8,128)(2,1)}, bf16[128,256]{1,0:T(8,128)(2,1)S(1)}, u32[]{:S(2)}, u32[]{:S(2)}) collective-permute-start(bf16[128,256]{1,0:T(8,128)(2,1)} %bitcast.8), channel_id=1, source_target_pairs={{0,6},{2,4},{4,2},{6,0},{8,14},{10,12},{12,10},{14,8},{1,7},{3,5},... | collective-permute-start | bytes 196616 | tf_op jit(solution)/shard_map/ppermute | solution.py:138
  7.5 1.2 %collective-permute-start.2 = (bf16[128,256]{1,0:T(8,128)(2,1)}, bf16[128,256]{1,0:T(8,128)(2,1)S(1)}, u32[]{:S(2)}, u32[]{:S(2)}) collective-permute-start(bf16[128,256]{1,0:T(8,128)(2,1)} %bitcast.9), channel_id=1, source_target_pairs={{0,4},{4,0},{8,12},{12,8},{1,5},{5,1},{9,13},{13,9},{2,6},{6,2},{1... | collective-permute-start | bytes 196616 | tf_op jit(solution)/shard_map/ppermute | solution.py:138
  8.7 0.5 %collective-permute-start.1 = (bf16[128,256]{1,0:T(8,128)(2,1)}, bf16[128,256]{1,0:T(8,128)(2,1)S(1)}, u32[]{:S(2)}, u32[]{:S(2)}) collective-permute-start(bf16[128,256]{1,0:T(8,128)(2,1)} %bitcast.10), channel_id=1, source_target_pairs={{0,2},{2,0},{1,3},{3,1},{4,6},{6,4},{5,7},{7,5},{8,10},{10,8},{9,1... | collective-permute-start | bytes 196616 | tf_op jit(solution)/shard_map/ppermute | solution.py:138
  9.2 0.0 collective-permute-done.5.refs_2_
  9.2 1.5 %collective-permute-start.6 = (bf16[128,256]{1,0:T(8,128)(2,1)S(1)}, bf16[128,256]{1,0:T(8,128)(2,1)S(1)}, u32[]{:S(2)}, u32[]{:S(2)}) collective-permute-start(bf16[128,256]{1,0:T(8,128)(2,1)S(1)} %collective-permute-done.5.refs_2_), channel_id=1, source_target_pairs={{0,2},{2,0},{1,3},{3,1},{4,6},{6,4},{5,7},{7,5},{8,10},{10,8},{9,1... | collective-permute-start | bytes 196616 | tf_op jit(solution)/shard_map/ppermute | solution.py:138
  10.7 0.9 %collective-permute-done.refs_8_.refs_0_ = bf16[128,256]{1,0:T(8,128)(2,1)S(1)} collective-permute-done((bf16[128,256]{1,0:T(8,128)(2,1)}, bf16[128,256]{1,0:T(8,128)(2,1)S(1)}, u32[]{:S(2)}, u32[]{:S(2)}) %collective-permute-start) | collective-permute-done | bytes 65568 | tf_op jit(solution)/shard_map/ppermute | solution.py:138
  11.7 1.5 %collective-permute-start.4 = (bf16[128,256]{1,0:T(8,128)(2,1)S(1)}, bf16[128,256]{1,0:T(8,128)(2,1)S(1)}, u32[]{:S(2)}, u32[]{:S(2)}) collective-permute-start(bf16[128,256]{1,0:T(8,128)(2,1)S(1)} %collective-permute-done.refs_8_.refs_0_), channel_id=1, source_target_pairs={{0,2},{2,0},{1,3},{3,1},{4,6},{6,4},{5,7},{7,5},{8,10},{10,8},{9,1... | collective-permute-start | bytes 196616 | tf_op jit(solution)/shard_map/ppermute | solution.py:138
  13.2 2.0 %stage.1 = (bf16[512,512]{1,0:T(8,128)(2,1)S(1)}, bf16[512,512]{1,0:T(8,128)(2,1)S(1)}, bf16[512,512]{1,0:T(8,128)(2,1)S(1)}, bf16[512,512]{1,0:T(8,128)(2,1)S(1...) custom-call(bf16[512,512]{1,0:T(8,128)(2,1)} %refs_0_.1, ...), custom_call_target="tpu_custom_call" | custom-call | tf_op jit(solution)/shard_map/stage/pallas_call | solution.py:155
  15.2 0.0 collective-permute-done.3.refs_3_
  15.2 0.0 collective-permute-done.2.refs_2_
  15.2 0.0 collective-permute-done.1.refs_1_
  15.3 0.1 collective-permute-start.7
  15.4 0.0 collective-permute-done.6.refs_3_
  15.4 0.6 %collective-permute-done.4.refs_1_ = bf16[128,256]{1,0:T(8,128)(2,1)S(1)} collective-permute-done((bf16[128,256]{1,0:T(8,128)(2,1)S(1)}, bf16[128,256]{1,0:T(8,128)(2,1)S(1)}, u32[]{:S(2)}, u32[]{:S(2)}) %collective-permute-start.4) | collective-permute-done | bytes 65568 | tf_op jit(solution)/shard_map/ppermute | solution.py:138
  15.9 0.1 collective-permute-start.8
  16.0 1.5 %mine.1 = (f32[1024,512]{1,0:T(8,128)S(1)}, f32[1024,512]{1,0:T(8,128)S(1)}, f32[1024,512]{1,0:T(8,128)S(1)}, bf16[1,3,3,256,256]{4,3,2,1,0:T(8,128)(2,1)S(1)}) custom-call(bf16[528,256]{1,0:T(8,128)(2,1)S(1)} %near.1.near_ref, bf16[512,256]{1,0:T(8,128)(2,1)S(1)} %far.1.far_ref, bf16[512,512]{1,0:T(8,128)(2,1)S(1)} %get-tuple-element.23.query_ref, ...), custom_call_target="tpu_custom_call" | custom-call | tf_op jit(solution)/shard_map/mine/pallas_call | solution.py:395
  17.6 0.0 collective-permute-done.7.other_near_ref
  17.6 0.0 collective-permute-done.8.other_far_ref
  17.6 3.6 %block.1 = (bf16[2,1,64,256]{3,2,1,0:T(8,128)(2,1)S(1)}, bf16[3,6,64,256]{3,2,1,0:T(8,128)(2,1)S(1)}, bf16[128,256]{1,0:T(8,128)(2,1)S(1)}, bf16[1,3,3,256,256]{4,3,2,1,0:T(8,128)(2,1)S(1)}) custom-call(bf16[528,256]{1,0:T(8,128)(2,1)S(1)} %near.1.near_ref, bf16[512,256]{1,0:T(8,128)(2,1)S(1)} %far.1.far_ref, ...), custom_call_target="tpu_custom_call" | custom-call | tf_op jit(solution)/shard_map/block/pallas_call | solution.py:405
  21.2 1.6 %collective-permute-start.9 = (bf16[128,256]{1,0:T(8,128)(2,1)S(1)}, bf16[128,256]{1,0:T(8,128)(2,1)S(1)}, u32[]{:S(2)}, u32[]{:S(2)}) collective-permute-start(bf16[128,256]{1,0:T(8,128)(2,1)S(1)} %get-tuple-element.37), channel_id=1, source_target_pairs={{0,2},{2,0},{1,3},{3,1},{4,6},{6,4},{5,7},{7,5},{8,10},{10,8},{9,1... | collective-permute-start | bytes 196616 | tf_op jit(solution)/shard_map/ppermute | solution.py:138
  22.8 0.7 %own.1 = (bf16[2,1,64,256]{3,2,1,0:T(8,128)(2,1)}, f32[128,256]{1,0:T(8,128)S(1)}) custom-call(bf16[3,6,64,256]{3,2,1,0:T(8,128)(2,1)S(1)} %get-tuple-element.32.activated, bf16[1,3,3,256,256]{4,3,2,1,0:T(8,128)(2,1)S(1)} %get-tuple-element.30.first_tap, bf16[1,3,3,256,256]{4,3,2,1,0:T(8,128)(2,1)S(1)} %get-tuple-element.31.second_tap, ...), custom_call_target="tpu_custom_call" | custom-call | tf_op jit(solution)/shard_map/own/pallas_call | solution.py:422
  23.5 2.3 %collective-permute-done.9 = bf16[128,256]{1,0:T(8,128)(2,1)S(1)} collective-permute-done((bf16[128,256]{1,0:T(8,128)(2,1)S(1)}, bf16[128,256]{1,0:T(8,128)(2,1)S(1)}, u32[]{:S(2)}, u32[]{:S(2)}) %collective-permute-start.9) | collective-permute-done | bytes 65568 | tf_op jit(solution)/shard_map/ppermute | solution.py:138
  25.8 0.6 %add_convert_fusion = bf16[128,256]{1,0:T(8,128)(2,1)} fusion(f32[128,256]{1,0:T(8,128)S(1)} %get-tuple-element.36, bf16[128,256]{1,0:T(8,128)(2,1)S(1)} %collective-permute-done.9), kind=kLoop, calls=%fused_computation | loop fusion | flops 98304 | bytes 262144 | tf_op jit(solution)/shard_map/convert_element_type | solution.py:435
  (2 shorter events, 0.1 us)
Async XLA Ops:
  0.6 8.6 %collective-permute-start.5 = (bf16[128,256]{1,0:T(8,128)(2,1)}, bf16[128,256]{1,0:T(8,128)(2,1)S(1)}, u32[]{:S(2)}, u32[]{:S(2)}) collective-permute-start(bf16[128,256]{1,0:T(8,128)(2,1)} %bitcast.6), channel_id=1, source_target_pairs={{0,12},{4,8},{8,4},{12,0},{1,13},{5,9},{9,5},{13,1},{2,14},{6,10},... | collective-permute-start | bytes 196616 | tf_op jit(solution)/shard_map/ppermute | solution.py:138
  5.7 5.9 %collective-permute-start = (bf16[128,256]{1,0:T(8,128)(2,1)}, bf16[128,256]{1,0:T(8,128)(2,1)S(1)}, u32[]{:S(2)}, u32[]{:S(2)}) collective-permute-start(bf16[128,256]{1,0:T(8,128)(2,1)} %bitcast.7), channel_id=1, source_target_pairs={{0,8},{4,12},{8,0},{12,4},{1,9},{5,13},{9,1},{13,5},{2,10},{6,14},... | collective-permute-start | bytes 196616 | tf_op jit(solution)/shard_map/ppermute | solution.py:138
  5.7 9.4 %collective-permute-start.3 = (bf16[128,256]{1,0:T(8,128)(2,1)}, bf16[128,256]{1,0:T(8,128)(2,1)S(1)}, u32[]{:S(2)}, u32[]{:S(2)}) collective-permute-start(bf16[128,256]{1,0:T(8,128)(2,1)} %bitcast.8), channel_id=1, source_target_pairs={{0,6},{2,4},{4,2},{6,0},{8,14},{10,12},{12,10},{14,8},{1,7},{3,5},... | collective-permute-start | bytes 196616 | tf_op jit(solution)/shard_map/ppermute | solution.py:138
  7.5 7.7 %collective-permute-start.2 = (bf16[128,256]{1,0:T(8,128)(2,1)}, bf16[128,256]{1,0:T(8,128)(2,1)S(1)}, u32[]{:S(2)}, u32[]{:S(2)}) collective-permute-start(bf16[128,256]{1,0:T(8,128)(2,1)} %bitcast.9), channel_id=1, source_target_pairs={{0,4},{4,0},{8,12},{12,8},{1,5},{5,1},{9,13},{13,9},{2,6},{6,2},{1... | collective-permute-start | bytes 196616 | tf_op jit(solution)/shard_map/ppermute | solution.py:138
  8.7 6.5 %collective-permute-start.1 = (bf16[128,256]{1,0:T(8,128)(2,1)}, bf16[128,256]{1,0:T(8,128)(2,1)S(1)}, u32[]{:S(2)}, u32[]{:S(2)}) collective-permute-start(bf16[128,256]{1,0:T(8,128)(2,1)} %bitcast.10), channel_id=1, source_target_pairs={{0,2},{2,0},{1,3},{3,1},{4,6},{6,4},{5,7},{7,5},{8,10},{10,8},{9,1... | collective-permute-start | bytes 196616 | tf_op jit(solution)/shard_map/ppermute | solution.py:138
  9.2 6.1 %collective-permute-start.6 = (bf16[128,256]{1,0:T(8,128)(2,1)S(1)}, bf16[128,256]{1,0:T(8,128)(2,1)S(1)}, u32[]{:S(2)}, u32[]{:S(2)}) collective-permute-start(bf16[128,256]{1,0:T(8,128)(2,1)S(1)} %collective-permute-done.5.refs_2_), channel_id=1, source_target_pairs={{0,2},{2,0},{1,3},{3,1},{4,6},{6,4},{5,7},{7,5},{8,10},{10,8},{9,1... | collective-permute-start | bytes 196616 | tf_op jit(solution)/shard_map/ppermute | solution.py:138
  11.7 4.3 %collective-permute-start.4 = (bf16[128,256]{1,0:T(8,128)(2,1)S(1)}, bf16[128,256]{1,0:T(8,128)(2,1)S(1)}, u32[]{:S(2)}, u32[]{:S(2)}) collective-permute-start(bf16[128,256]{1,0:T(8,128)(2,1)S(1)} %collective-permute-done.refs_8_.refs_0_), channel_id=1, source_target_pairs={{0,2},{2,0},{1,3},{3,1},{4,6},{6,4},{5,7},{7,5},{8,10},{10,8},{9,1... | collective-permute-start | bytes 196616 | tf_op jit(solution)/shard_map/ppermute | solution.py:138
  15.3 2.3 %collective-permute-start.7 = (bf16[528,256]{1,0:T(8,128)(2,1)S(1)}, bf16[528,256]{1,0:T(8,128)(2,1)S(1)}, u32[]{:S(2)}, u32[]{:S(2)}) collective-permute-start(bf16[528,256]{1,0:T(8,128)(2,1)S(1)} %near.1.near_ref), channel_id=1, source_target_pairs={{0,1},{1,0},{2,3},{3,2},{4,5},{5,4},{6,7},{7,6},{8,9},{9,8},{10,11... | collective-permute-start | bytes 811016 | tf_op jit(solution)/shard_map/ppermute | solution.py:138
  15.9 1.6 %collective-permute-start.8 = (bf16[512,256]{1,0:T(8,128)(2,1)S(1)}, bf16[512,256]{1,0:T(8,128)(2,1)S(1)}, u32[]{:S(2)}, u32[]{:S(2)}) collective-permute-start(bf16[512,256]{1,0:T(8,128)(2,1)S(1)} %far.1.far_ref), channel_id=1, source_target_pairs={{0,1},{1,0},{2,3},{3,2},{4,5},{5,4},{6,7},{7,6},{8,9},{9,8},{10,11... | collective-permute-start | bytes 786440 | tf_op jit(solution)/shard_map/ppermute | solution.py:138
  21.2 4.6 %collective-permute-start.9 = (bf16[128,256]{1,0:T(8,128)(2,1)S(1)}, bf16[128,256]{1,0:T(8,128)(2,1)S(1)}, u32[]{:S(2)}, u32[]{:S(2)}) collective-permute-start(bf16[128,256]{1,0:T(8,128)(2,1)S(1)} %get-tuple-element.37), channel_id=1, source_target_pairs={{0,2},{2,0},{1,3},{3,1},{4,6},{6,4},{5,7},{7,5},{8,10},{10,8},{9,1... | collective-permute-start | bytes 196616 | tf_op jit(solution)/shard_map/ppermute | solution.py:138

commit v5 on v4

--- a/solution.py
+++ b/solution.py
@@ -138,28 +138,42 @@
     return lax.ppermute(x, axes, [(i, i ^ step) for i in range(peers)])
 
 
-def stage_kernel(*refs):
-    count = len(refs) // 2 - 1
-    targets = refs[count + 1 : -1]
-    copies = [
-        pltpu.make_async_copy(source.at[pl.ds(0, target.shape[0])], target, refs[-1].at[i])
-        for i, (source, target) in enumerate(zip(refs, targets))
+def stage_kernel(
+    query_hbm, key_hbm, value_hbm, out_weight_hbm, own_hbm, first_hbm, second_hbm, kernel_hbm, _,
+    query_ref, key_ref, value_ref, in_out_ref, own_out_ref, own_ref, first_ref, second_ref, tap_ref, arrived,
+):
+    channels, in_channels = own_out_ref.shape[1], in_out_ref.shape[1]
+    own_half = pl.ds(pl.multiple_of(lax.axis_index("chan") * channels, channels), channels)
+    in_half = pl.ds(pl.multiple_of(lax.axis_index("tm") * in_channels, in_channels), in_channels)
+    moves = []
+    other_half = pl.ds(pl.multiple_of((1 - lax.axis_index("chan")) * channels, channels), channels)
+    for source, target in ((query_hbm, query_ref), (key_hbm, key_ref), (value_hbm, value_ref)):
+        moves.append((source.at[own_half], target.at[pl.ds(0, channels)]))
+        moves.append((source.at[other_half], target.at[pl.ds(channels, channels)]))
+    moves += [
+        (out_weight_hbm.at[:, in_half], in_out_ref), (out_weight_hbm.at[:, own_half], own_out_ref),
+        (own_hbm, own_ref), (first_hbm, first_ref), (second_hbm, second_ref), (kernel_hbm.at[pl.ds(0, tap_ref.shape[0])], tap_ref),
     ]
+    copies = [pltpu.make_async_copy(*move, arrived.at[place]) for place, move in enumerate(moves)]
     for copy in copies:
         copy.start()
     for copy in copies:
         copy.wait()
 
 
-def stage(arrays, sizes, after):
+def stage(arrays, after):
+    query_weight, _, _, out_weight, own, first_gain, second_gain, conv_kernel = arrays
+    in_channels = conv_kernel.shape[3]
+    shapes = [query_weight.shape] * 3 + [(out_weight.shape[0], in_channels), (out_weight.shape[0], own.shape[1])]
+    shapes = [jax.ShapeDtypeStruct(shape, own.dtype) for shape in shapes + [own.shape, (conv_kernel.shape[0] - 1, *conv_kernel.shape[1:])]]
+    gains = [jax.ShapeDtypeStruct(gain.shape, gain.dtype) for gain in (first_gain, second_gain)]
+    shapes = shapes[:-1] + gains + shapes[-1:]
     return pl.pallas_call(
         stage_kernel,
-        out_shape=tuple(
-            jax.ShapeDtypeStruct((size, *array.shape[1:]), array.dtype) for array, size in zip(arrays, sizes)
-        ),
+        out_shape=tuple(shapes),
         in_specs=[pl.BlockSpec(memory_space=pltpu.HBM)] * len(arrays) + [pl.BlockSpec(memory_space=pl.ANY)],
-        out_specs=tuple(pl.BlockSpec(memory_space=pltpu.VMEM) for _ in arrays),
-        scratch_shapes=[pltpu.SemaphoreType.DMA((len(arrays),))],
+        out_specs=tuple(pl.BlockSpec(memory_space=pltpu.VMEM) for _ in shapes),
+        scratch_shapes=[pltpu.SemaphoreType.DMA((12,))],
         compiler_params=pltpu.CompilerParams(vmem_limit_bytes=1 << 20),
         name="stage",
     )(*(in_hbm(array) for array in arrays), after)
@@ -202,12 +216,6 @@
         parts.append(rounded)
         values = values - rounded.astype(jnp.float32)
     return parts
-
-
-def channel_sums(values):
-    tokens, channels = values.shape
-    parts = values.reshape(tokens // 8, 8, channels)
-    return [jnp.sum(jnp.sum(part, axis=0), axis=0, keepdims=True) for part in (parts, parts * parts)]
 
 
 def group_statistics(rows, count):
@@ -230,49 +238,68 @@
     return found
 
 
-def core_tokens(near, far, layout):
+def core_chunks(near, far, layout):
     own_frames, cols, rows, blocks = layout
     size = own_frames * cols
-    pieces = [ref[at : at + size, :] for ref in (near, far) for at in range(0, ref.shape[0] - size + 1, size)]
-    laid = []
+    places = [(ref, at) for ref in (near, far) for at in range(0, ref.shape[0] - size + 1, size)]
+    chunks = []
     for index in range(blocks):
         for frame in range(own_frames):
-            at = slice(frame * cols, (frame + 1) * cols)
-            laid += [pieces[row * blocks + index][at] for row in range(rows)]
-    parts = near[near.shape[0] - GAIN_ROWS : near.shape[0], :].astype(jnp.float32)
-    gains = [parts[at : at + 1] + parts[at + 1 : at + 2] + parts[at + 2 : at + 3] for at in (0, 3)]
-    return jnp.concatenate(laid, axis=0), *gains
-
-
-def normed_tokens(tokens, gain):
-    values = tokens.astype(jnp.float32)
-    ((centre, scale),) = group_statistics(channel_sums(values), tokens.shape[0] * (D // NGROUP))
-    return ((values - centre) * (scale * gain)).astype(jnp.bfloat16)
+            for row in range(rows):
+                ref, at = places[row * blocks + index]
+                chunks.append((ref, slice(at + frame * cols, at + (frame + 1) * cols)))
+    return chunks
+
+
+def core_gain(near, which):
+    end = near.shape[0]
+    parts = near[end - GAIN_ROWS : end, :].astype(jnp.float32)
+    at = 3 * which
+    return parts[at : at + 1] + parts[at + 1 : at + 2] + parts[at + 2 : at + 3]
+
+
+def add_chunk(totals, values):
+    parts = values.reshape(values.shape[0] // 8, 8, values.shape[1])
+    found = [jnp.sum(parts, axis=0), jnp.sum(parts * parts, axis=0)]
+    return found if totals is None else [total + part for total, part in zip(totals, found)]
+
+
+def chunk_statistics(totals, count):
+    ((centre, scale),) = group_statistics([jnp.sum(total, axis=0, keepdims=True) for total in totals], count)
+    return centre, scale
+
+
+def norm_chunks(chunks, gain, normed):
+    totals = None
+    for ref, at in chunks:
+        totals = add_chunk(totals, ref[at, :].astype(jnp.float32))
+    centre, scale = chunk_statistics(totals, normed.shape[0] * (D // NGROUP))
+    scale = scale * gain
+    end = 0
+    for ref, at in chunks:
+        start, end = end, end + at.stop - at.start
+        normed[start:end, :] = ((ref[at, :].astype(jnp.float32) - centre) * scale).astype(jnp.bfloat16)
 
 
 def mine_kernel(
     near_ref, far_ref, query_ref, key_ref, value_ref, kernel_hbm,
-    begun_query, begun_key, begun_value, early_ref, normed, arrived, *, layout,
+    begun_query, begun_key, begun_value, last_tap, normed, arrived, *, layout,
 ):
-    copy = pltpu.make_async_copy(kernel_hbm.at[pl.ds(1, early_ref.shape[0])], early_ref, arrived)
+    copy = pltpu.make_async_copy(kernel_hbm.at[pl.ds(kernel_hbm.shape[0] - 1, 1)], last_tap, arrived)
     copy.start()
-    tokens, gain, _ = core_tokens(near_ref, far_ref, layout)
-    normed[...] = normed_tokens(tokens, gain)
+    norm_chunks(core_chunks(near_ref, far_ref, layout), core_gain(near_ref, 0), normed)
     channels = normed.shape[1]
-    rows = pl.ds(pl.multiple_of(lax.axis_index("chan") * channels, channels), channels)
     for weight_ref, target in zip((query_ref, key_ref, value_ref), (begun_query, begun_key, begun_value)):
-        target[...] = jnp.dot(normed[...], weight_ref[rows, :], preferred_element_type=jnp.float32)
+        target[...] = jnp.dot(normed[...], weight_ref[:channels, :], preferred_element_type=jnp.float32)
     copy.wait()
 
 
 def main_kernel(
     near_ref, far_ref, other_near_ref, other_far_ref, query_ref, key_ref, value_ref, begun_query, begun_key, begun_value,
-    out_weight_ref, first_tap, second_tap, kernel_hbm,
-    attended_ref, activated, send_ref, last_tap,
-    normed, queries, keyed, valued, mixed, resid, arrived,
+    in_out_ref, own_out_ref, early_taps, last_tap,
+    attended_ref, activated, send_ref,
+    normed, queries, keyed, valued, mixed, resid, projected,
 ):
-    kernel_copy = pltpu.make_async_copy(kernel_hbm.at[pl.ds(2, 1)], last_tap, arrived)
-    kernel_copy.start()
     own_frames, _, cols, channels = attended_ref.shape
     frames, rows = resid.shape[:2]
     tokens = frames * rows * cols
@@ -282,24 +309,19 @@
     half = lax.axis_index("chan")
     width = D // NGROUP
     count = tokens * width
-    other_rows = pl.ds(pl.multiple_of((1 - half) * channels, channels), channels)
 
     blocks = frames // own_frames
 
     layout = (own_frames, cols, rows, blocks)
-    sides, first_gains, second_gains = zip(
-        core_tokens(near_ref, far_ref, layout), core_tokens(other_near_ref, other_far_ref, layout)
-    )
-    normed[...] = normed_tokens(sides[1], first_gains[1])
+    mine, other = core_chunks(near_ref, far_ref, layout), core_chunks(other_near_ref, other_far_ref, layout)
+    norm_chunks(other, core_gain(other_near_ref, 0), normed)
     for weight_ref, begun_ref, target in zip(
         (query_ref, key_ref, value_ref), (begun_query, begun_key, begun_value), (queries, keyed, valued)
     ):
-        term = jnp.dot(normed[...], weight_ref[other_rows, :], preferred_element_type=jnp.float32)
+        term = jnp.dot(normed[...], weight_ref[channels:, :], preferred_element_type=jnp.float32)
         target[...] = (begun_ref[...] + term).astype(jnp.bfloat16)
 
-    in_channels = first_tap.shape[3]
-    in_cols = pl.ds(pl.multiple_of(block * in_channels, in_channels), in_channels)
-    own_cols = pl.ds(pl.multiple_of(half * channels, channels), channels)
+    in_channels = early_taps.shape[3]
     mine_in = block == half
     spans = [slice(frame * frame_tokens, (frame + 1) * frame_tokens) for frame in range(frames)]
     scores = [
@@ -312,44 +334,45 @@
         mass = jnp.sum(weights, axis=1, keepdims=True)
         blend = jnp.dot(weights.astype(jnp.bfloat16), valued[at, :], preferred_element_type=jnp.float32)
         mixed[at, :] = (blend * (1.0 / mass)).astype(jnp.bfloat16)
-    projected = jnp.dot(
-        mixed[...], out_weight_ref[:, in_cols], preferred_element_type=jnp.float32
-    ).astype(jnp.bfloat16)
-    source = jnp.where(mine_in, sides[0], sides[1])
-    total = source.astype(jnp.float32) + projected.astype(jnp.float32)
-    resid[...] = total.reshape(frames, rows, cols, in_channels)
+    projected[...] = jnp.dot(mixed[...], in_out_ref[...], preferred_element_type=jnp.float32).astype(jnp.bfloat16)
+    totals = None
+    for chunk, ((ref, at), (other_ref, _)) in enumerate(zip(mine, other)):
+        source = jnp.where(mine_in, ref[at, :], other_ref[at, :]).astype(jnp.float32)
+        total = source + projected[chunk * cols : (chunk + 1) * cols, :].astype(jnp.float32)
+        resid[chunk // rows, chunk % rows] = total
+        totals = add_chunk(totals, total)
     own_mixed = jnp.concatenate([mixed[at.start : at.start + cols, :] for at in spans[:own_frames]], axis=0)
     attended_ref[...] = jnp.dot(
-        own_mixed, out_weight_ref[:, own_cols], preferred_element_type=jnp.float32
+        own_mixed, own_out_ref[...], preferred_element_type=jnp.float32
     ).astype(jnp.bfloat16).reshape(own_frames, 1, cols, channels)
 
-    kernel_copy.wait()
-    ((centre, scale),) = group_statistics(channel_sums(total), count)
-    scale = scale * jnp.where(mine_in, *second_gains)
+    centre, scale = chunk_statistics(totals, count)
+    scale = 0.5 * scale * jnp.where(mine_in, core_gain(near_ref, 1), core_gain(other_near_ref, 1))
     activated[:, 0:2] = jnp.zeros((3, 2, cols, in_channels), jnp.bfloat16)
     for tap in range(3):
         row = space + (tap - 1)
         inside = jnp.logical_and(row >= 0, row < rows)
         place = jnp.where(inside, space ^ row, 0)
+        row_scale = jnp.where(inside, scale, 0.0)
         for frame in range(frames):
             relative = ((frame // own_frames) ^ block) * own_frames + frame % own_frames
-            values = (resid[relative, place] - centre) * scale
-            values = 0.5 * values * (1.0 + jnp.tanh(0.5 * values))
-            activated[tap, frame + 2] = jnp.where(inside, values, 0.0).astype(jnp.bfloat16)
-
-    send_ref[...] = partial_conv(activated, (first_tap, second_tap, last_tap), 1 - block, own_frames).astype(jnp.bfloat16)
-
-
-def partial_conv(activated, taps, block, frames):
+            halved = (resid[relative, place] - centre) * row_scale
+            activated[tap, frame + 2] = (halved + halved * jnp.tanh(halved)).astype(jnp.bfloat16)
+
+    send_ref[...] = partial_conv(activated, early_taps, last_tap, 1 - block, own_frames).astype(jnp.bfloat16)
+
+
+def partial_conv(activated, early_taps, last_tap, block, frames):
     cols, in_channels = activated.shape[2:]
     tokens = frames * cols
+    taps = [ref.at[tap] for ref in (early_taps, last_tap) for tap in range(ref.shape[0])]
     columns = []
     for col_tap in range(3):
         total = None
         for time_tap in range(3):
             for row_tap in range(3):
                 window = activated[row_tap, pl.ds(block * frames + time_tap, frames)].reshape(tokens, in_channels)
-                term = jnp.dot(window, taps[time_tap][0, row_tap, col_tap], preferred_element_type=jnp.float32)
+                term = jnp.dot(window, taps[time_tap][row_tap, col_tap], preferred_element_type=jnp.float32)
                 total = term if total is None else total + term
         columns.append(total)
     place = lax.broadcasted_iota(jnp.int32, columns[0].shape, 0) % cols
@@ -358,10 +381,10 @@
     return columns[1] + left + right
 
 
-def own_kernel(activated, first_tap, second_tap, last_tap, attended_ref, attended_hbm, keep_ref, sent):
+def own_kernel(activated, early_taps, last_tap, attended_ref, attended_hbm, keep_ref, sent):
     copy = pltpu.make_async_copy(attended_ref, attended_hbm, sent)
     copy.start()
-    keep_ref[...] = partial_conv(activated, (first_tap, second_tap, last_tap), lax.axis_index("tm"), attended_ref.shape[0])
+    keep_ref[...] = partial_conv(activated, early_taps, last_tap, lax.axis_index("tm"), attended_ref.shape[0])
     copy.wait()
 
 
@@ -378,9 +401,7 @@
     for row in range(1, rows // 2):
         onward[row] = exchange(own, ("space", "tm"), row * blocks + 1)
     staged = (query_weight, key_weight, value_weight, out_weight, own, *gains, conv_kernel)
-    *weights, own_staged, first_gain, second_gain, first_tap = stage(
-        staged, [array.shape[0] for array in staged[:-1]] + [1], by_row[rows // 2]
-    )
+    *weights, in_out, own_out, own_staged, first_gain, second_gain, early_taps = stage(staged, by_row[rows // 2])
     near = [own_staged, first]
     for row in range(1, rows // 2):
         near += [by_row[row], onward[row]]
@@ -392,7 +413,7 @@
     in_channels, out_channels = conv_kernel.shape[3:]
     tokens = blocks * frames * rows * cols
     in_vmem = pl.BlockSpec(memory_space=pltpu.VMEM)
-    *begun, second_tap = pl.pallas_call(
+    *begun, last_tap = pl.pallas_call(
         functools.partial(mine_kernel, layout=(frames, cols, rows, blocks)),
         out_shape=(jax.ShapeDtypeStruct((tokens, D), jnp.float32),) * 3
         + (jax.ShapeDtypeStruct((1, *conv_kernel.shape[1:]), conv_kernel.dtype),),
@@ -401,23 +422,23 @@
         scratch_shapes=[pltpu.VMEM((tokens, channels), jnp.bfloat16), pltpu.SemaphoreType.DMA],
         compiler_params=pltpu.CompilerParams(vmem_limit_bytes=8 * 1024 * 1024),
         name="mine",
-    )(near_mine, far_mine, *weights[:3], in_hbm(conv_kernel))
-    attended, activated, send, last_tap = pl.pallas_call(
+    )(near_mine, far_mine, *weights, in_hbm(conv_kernel))
+    attended, activated, send = pl.pallas_call(
         main_kernel,
         out_shape=(
             jax.ShapeDtypeStruct((frames, 1, cols, channels), jnp.bfloat16),
             jax.ShapeDtypeStruct((3, blocks * frames + 2, cols, in_channels), jnp.bfloat16),
             jax.ShapeDtypeStruct((frames * cols, out_channels), jnp.bfloat16),
-            jax.ShapeDtypeStruct((1, *conv_kernel.shape[1:]), conv_kernel.dtype),
         ),
-        in_specs=[in_vmem] * 13 + [pl.BlockSpec(memory_space=pltpu.HBM)],
-        out_specs=(in_vmem,) * 4,
+        in_specs=[in_vmem] * 14,
+        out_specs=(in_vmem,) * 3,
         scratch_shapes=[pltpu.VMEM((tokens, channels), jnp.bfloat16)]
         + [pltpu.VMEM((tokens, D), jnp.bfloat16)] * 4
-        + [pltpu.VMEM((blocks * frames, rows, cols, in_channels), jnp.float32), pltpu.SemaphoreType.DMA],
+        + [pltpu.VMEM((blocks * frames, rows, cols, in_channels), jnp.float32)]
+        + [pltpu.VMEM((tokens, in_channels), jnp.bfloat16)],
         compiler_params=pltpu.CompilerParams(vmem_limit_bytes=24 * 1024 * 1024),
         name="block",
-    )(near_mine, far_mine, near_other, far_other, *weights[:3], *begun, weights[3], first_tap, second_tap, in_hbm(conv_kernel))
+    )(near_mine, far_mine, near_other, far_other, *weights, *begun, in_out, own_out, early_taps, last_tap)
     received = exchange(send, "tm", 1)
     attended, keep = pl.pallas_call(
         own_kernel,
@@ -425,12 +446,12 @@
             jax.ShapeDtypeStruct(attended.shape, attended.dtype),
             jax.ShapeDtypeStruct((frames * cols, out_channels), jnp.float32),
         ),
-        in_specs=[in_vmem] * 5,
+        in_specs=[in_vmem] * 4,
         out_specs=(pl.BlockSpec(memory_space=pl.ANY), in_vmem),
         scratch_shapes=[pltpu.SemaphoreType.DMA],
         compiler_params=pltpu.CompilerParams(vmem_limit_bytes=4 * 1024 * 1024),
         name="own",
-    )(activated, first_tap, second_tap, last_tap, attended)
+    )(activated, early_taps, last_tap, attended)
     total = keep + received.astype(jnp.float32)
     return attended, total.astype(jnp.bfloat16).reshape(frames, 1, cols, out_channels)
 

time: 26.6 us -> 26.2 us (0.985)
  waiting for transfers between devices: 3.83 us -> 3.34 us
    ppermute x10, waiting for transfers between devices: 3.83 us -> 3.34 us  [exchange(): return lax.ppermute(x, axes, [(i, i ^ step) for i in range(peers)])]
    pallas_call x1, Pallas kernels: 2.03 us -> 2.45 us  [stage(): pl.pallas_call(stage_kernel, out_shape=tuple(shapes), in_specs=[pl.BlockS...]
    pallas_call x1, Pallas kernels: 3.64 us -> 3.37 us  [gathered_plan(): pl.pallas_call(main_kernel, out_shape=(jax.ShapeDtypeStruct((frames, 1, c...]
  transfers between devices with their start and end apart: 10 -> 10, of which waited for: 3 -> 3; matrix products, arithmetic and copies ran while one was open for 0% -> 0% of each run, Pallas kernels for 16% -> 17%
where the time goes in v5:
time: 26.2 us; the launch traced here: 26 us
  starting transfers between devices  13.5 us (52%)
  Pallas kernels  7.82 us (30%)
  waiting for transfers between devices  3.34 us (13%)
  between operations  0.73 us (3%)
  other arithmetic  0.64 us (2%)
    ppermute x10, starting transfers between devices, exchange(): return lax.ppermute(x, axes, [(i, i ^ step) for i in range(peers)])  13.5 us
    pallas_call x1, Pallas kernels, gathered_plan(): pl.pallas_call(main_kernel, out_shape=(jax.ShapeDtypeStruct((frames, 1, c...  3.37 us
    ppermute x10, waiting for transfers between devices, exchange(): return lax.ppermute(x, axes, [(i, i ^ step) for i in range(peers)])  3.34 us
    pallas_call x1, Pallas kernels, stage(): pl.pallas_call(stage_kernel, out_shape=tuple(shapes), in_specs=[pl.BlockS...  2.45 us
    pallas_call x1, Pallas kernels, gathered_plan(): pl.pallas_call(functools.partial(mine_kernel, layout=(frames, cols, rows,...  1.28 us
    pallas_call x1, Pallas kernels, gathered_plan(): pl.pallas_call(own_kernel, out_shape=(jax.ShapeDtypeStruct(attended.shape...  0.66 us
    convert_element_type x1, other arithmetic, gathered_plan(): total.astype(jnp.bfloat16).reshape(frames, 1, cols, out_channels)  0.64 us
  transfers between devices with their start and end apart: 10, of which 3 were waited for; matrix products, arithmetic and copies ran while one was open for 0% of the time, Pallas kernels for 17%

profile of v5, /device:TPU:0, one launch (start us, length us, event | category | flops | bytes accessed | tf_op | source)
XLA Modules:
  0.0 26.0 jit_solution(928841552618325467)
XLA Ops:
  0.6 5.1 %collective-permute-start.5 = (bf16[128,256]{1,0:T(8,128)(2,1)}, bf16[128,256]{1,0:T(8,128)(2,1)S(1)}, u32[]{:S(2)}, u32[]{:S(2)}) collective-permute-start(bf16[128,256]{1,0:T(8,128)(2,1)} %bitcast.6), channel_id=1, source_target_pairs={{0,12},{4,8},{8,4},{12,0},{1,13},{5,9},{9,5},{13,1},{2,14},{6,10},... | collective-permute-start | bytes 196616 | tf_op jit(solution)/shard_map/ppermute | solution.py:138
  5.7 0.0 collective-permute-start
  5.8 1.7 %collective-permute-start.3 = (bf16[128,256]{1,0:T(8,128)(2,1)}, bf16[128,256]{1,0:T(8,128)(2,1)S(1)}, u32[]{:S(2)}, u32[]{:S(2)}) collective-permute-start(bf16[128,256]{1,0:T(8,128)(2,1)} %bitcast.8), channel_id=1, source_target_pairs={{0,6},{2,4},{4,2},{6,0},{8,14},{10,12},{12,10},{14,8},{1,7},{3,5},... | collective-permute-start | bytes 196616 | tf_op jit(solution)/shard_map/ppermute | solution.py:138
  7.5 1.2 %collective-permute-start.2 = (bf16[128,256]{1,0:T(8,128)(2,1)}, bf16[128,256]{1,0:T(8,128)(2,1)S(1)}, u32[]{:S(2)}, u32[]{:S(2)}) collective-permute-start(bf16[128,256]{1,0:T(8,128)(2,1)} %bitcast.9), channel_id=1, source_target_pairs={{0,4},{4,0},{8,12},{12,8},{1,5},{5,1},{9,13},{13,9},{2,6},{6,2},{1... | collective-permute-start | bytes 196616 | tf_op jit(solution)/shard_map/ppermute | solution.py:138
  8.7 0.5 %collective-permute-start.1 = (bf16[128,256]{1,0:T(8,128)(2,1)}, bf16[128,256]{1,0:T(8,128)(2,1)S(1)}, u32[]{:S(2)}, u32[]{:S(2)}) collective-permute-start(bf16[128,256]{1,0:T(8,128)(2,1)} %bitcast.10), channel_id=1, source_target_pairs={{0,2},{2,0},{1,3},{3,1},{4,6},{6,4},{5,7},{7,5},{8,10},{10,8},{9,1... | collective-permute-start | bytes 196616 | tf_op jit(solution)/shard_map/ppermute | solution.py:138
  9.2 0.0 collective-permute-done.5.refs_2_
  9.2 1.5 %collective-permute-start.6 = (bf16[128,256]{1,0:T(8,128)(2,1)S(1)}, bf16[128,256]{1,0:T(8,128)(2,1)S(1)}, u32[]{:S(2)}, u32[]{:S(2)}) collective-permute-start(bf16[128,256]{1,0:T(8,128)(2,1)S(1)} %collective-permute-done.5.refs_2_), channel_id=1, source_target_pairs={{0,2},{2,0},{1,3},{3,1},{4,6},{6,4},{5,7},{7,5},{8,10},{10,8},{9,1... | collective-permute-start | bytes 196616 | tf_op jit(solution)/shard_map/ppermute | solution.py:138
  10.7 0.9 %collective-permute-done._.refs_0_ = bf16[128,256]{1,0:T(8,128)(2,1)S(1)} collective-permute-done((bf16[128,256]{1,0:T(8,128)(2,1)}, bf16[128,256]{1,0:T(8,128)(2,1)S(1)}, u32[]{:S(2)}, u32[]{:S(2)}) %collective-permute-start) | collective-permute-done | bytes 65568 | tf_op jit(solution)/shard_map/ppermute | solution.py:138
  11.7 1.5 %collective-permute-start.4 = (bf16[128,256]{1,0:T(8,128)(2,1)S(1)}, bf16[128,256]{1,0:T(8,128)(2,1)S(1)}, u32[]{:S(2)}, u32[]{:S(2)}) collective-permute-start(bf16[128,256]{1,0:T(8,128)(2,1)S(1)} %collective-permute-done._.refs_0_), channel_id=1, source_target_pairs={{0,2},{2,0},{1,3},{3,1},{4,6},{6,4},{5,7},{7,5},{8,10},{10,8},{9,1... | collective-permute-start | bytes 196616 | tf_op jit(solution)/shard_map/ppermute | solution.py:138
  13.2 2.4 %stage.1 = (bf16[512,512]{1,0:T(8,128)(2,1)S(1)}, bf16[512,512]{1,0:T(8,128)(2,1)S(1)}, bf16[512,512]{1,0:T(8,128)(2,1)S(1)}, bf16[512,256]{1,0:T(8,128)(2,1)S(1...) custom-call(bf16[512,512]{1,0:T(8,128)(2,1)} %query_hbm.1, ...), custom_call_target="tpu_custom_call" | custom-call | tf_op jit(solution)/shard_map/stage/pallas_call | solution.py:171
  15.6 0.0 collective-permute-done.3.refs_3_
  15.6 0.0 collective-permute-done.2.refs_2_
  15.6 0.0 collective-permute-done.1.refs_1_
  15.7 0.1 collective-permute-start.7
  15.8 0.0 collective-permute-done.6.refs_3_
  15.8 0.1 collective-permute-done.4.refs_1_
  15.9 0.4 %collective-permute-start.8 = (bf16[512,256]{1,0:T(8,128)(2,1)S(1)}, bf16[512,256]{1,0:T(8,128)(2,1)S(1)}, u32[]{:S(2)}, u32[]{:S(2)}) collective-permute-start(bf16[512,256]{1,0:T(8,128)(2,1)S(1)} %far.1.far_ref), channel_id=1, source_target_pairs={{0,1},{1,0},{2,3},{3,2},{4,5},{5,4},{6,7},{7,6},{8,9},{9,8},{10,11... | collective-permute-start | bytes 786440 | tf_op jit(solution)/shard_map/ppermute | solution.py:138
  16.4 1.3 %mine.1 = (f32[1024,512]{1,0:T(8,128)S(1)}, f32[1024,512]{1,0:T(8,128)S(1)}, f32[1024,512]{1,0:T(8,128)S(1)}, bf16[1,3,3,256,256]{4,3,2,1,0:T(8,128)(2,1)S(1)}) custom-call(bf16[528,256]{1,0:T(8,128)(2,1)S(1)} %near.1.near_ref, bf16[512,256]{1,0:T(8,128)(2,1)S(1)} %far.1.far_ref, bf16[512,512]{1,0:T(8,128)(2,1)S(1)} %get-tuple-element.23.query_ref, ...), custom_call_target="tpu_custom_call" | custom-call | tf_op jit(solution)/shard_map/mine/pallas_call | solution.py:416
  17.6 0.0 collective-permute-done.7.other_near_ref
  17.7 0.0 collective-permute-done.8.other_far_ref
  17.7 3.4 %block.1 = (bf16[2,1,64,256]{3,2,1,0:T(8,128)(2,1)S(1)}, bf16[3,6,64,256]{3,2,1,0:T(8,128)(2,1)S(1)}, bf16[128,256]{1,0:T(8,128)(2,1)S(1)}) custom-call(bf16[528,256]{1,0:T(8,128)(2,1)S(1)} %near.1.near_ref, bf16[512,256]{1,0:T(8,128)(2,1)S(1)} %far.1.far_ref, bf16[528,256]{1,0:T(8,128)(2,1)S(1)} %collective-permute-done.7.other_near_ref, ...), custom_call_target="tpu_custom_call" | custom-call | tf_op jit(solution)/shard_map/block/pallas_call | solution.py:426
  21.1 1.4 %collective-permute-start.9 = (bf16[128,256]{1,0:T(8,128)(2,1)S(1)}, bf16[128,256]{1,0:T(8,128)(2,1)S(1)}, u32[]{:S(2)}, u32[]{:S(2)}) collective-permute-start(bf16[128,256]{1,0:T(8,128)(2,1)S(1)} %get-tuple-element.37), channel_id=1, source_target_pairs={{0,2},{2,0},{1,3},{3,1},{4,6},{6,4},{5,7},{7,5},{8,10},{10,8},{9,1... | collective-permute-start | bytes 196616 | tf_op jit(solution)/shard_map/ppermute | solution.py:138
  22.5 0.7 %own.1 = (bf16[2,1,64,256]{3,2,1,0:T(8,128)(2,1)}, f32[128,256]{1,0:T(8,128)S(1)}) custom-call(bf16[3,6,64,256]{3,2,1,0:T(8,128)(2,1)S(1)} %get-tuple-element.33.activated, bf16[2,3,3,256,256]{4,3,2,1,0:T(8,128)(2,1)S(1)} %get-tuple-element.31.early_taps, bf16[1,3,3,256,256]{4,3,2,1,0:T(8,128)(2,1)S(1)} %get-tuple-element.32.last_tap, ...), custom_call_target="tpu_custom_call" | custom-call | tf_op jit(solution)/shard_map/own/pallas_call | solution.py:443
  23.2 2.2 %collective-permute-done.9 = bf16[128,256]{1,0:T(8,128)(2,1)S(1)} collective-permute-done((bf16[128,256]{1,0:T(8,128)(2,1)S(1)}, bf16[128,256]{1,0:T(8,128)(2,1)S(1)}, u32[]{:S(2)}, u32[]{:S(2)}) %collective-permute-start.9) | collective-permute-done | bytes 65568 | tf_op jit(solution)/shard_map/ppermute | solution.py:138
  25.4 0.6 %add_convert_fusion = bf16[128,256]{1,0:T(8,128)(2,1)} fusion(f32[128,256]{1,0:T(8,128)S(1)} %get-tuple-element.36, bf16[128,256]{1,0:T(8,128)(2,1)S(1)} %collective-permute-done.9), kind=kLoop, calls=%fused_computation | loop fusion | flops 98304 | bytes 262144 | tf_op jit(solution)/shard_map/convert_element_type | solution.py:456
  (2 shorter events, 0.1 us)
Async XLA Ops:
  0.6 8.6 %collective-permute-start.5 = (bf16[128,256]{1,0:T(8,128)(2,1)}, bf16[128,256]{1,0:T(8,128)(2,1)S(1)}, u32[]{:S(2)}, u32[]{:S(2)}) collective-permute-start(bf16[128,256]{1,0:T(8,128)(2,1)} %bitcast.6), channel_id=1, source_target_pairs={{0,12},{4,8},{8,4},{12,0},{1,13},{5,9},{9,5},{13,1},{2,14},{6,10},... | collective-permute-start | bytes 196616 | tf_op jit(solution)/shard_map/ppermute | solution.py:138
  5.7 5.9 %collective-permute-start = (bf16[128,256]{1,0:T(8,128)(2,1)}, bf16[128,256]{1,0:T(8,128)(2,1)S(1)}, u32[]{:S(2)}, u32[]{:S(2)}) collective-permute-start(bf16[128,256]{1,0:T(8,128)(2,1)} %bitcast.7), channel_id=1, source_target_pairs={{0,8},{4,12},{8,0},{12,4},{1,9},{5,13},{9,1},{13,5},{2,10},{6,14},... | collective-permute-start | bytes 196616 | tf_op jit(solution)/shard_map/ppermute | solution.py:138
  5.8 9.9 %collective-permute-start.3 = (bf16[128,256]{1,0:T(8,128)(2,1)}, bf16[128,256]{1,0:T(8,128)(2,1)S(1)}, u32[]{:S(2)}, u32[]{:S(2)}) collective-permute-start(bf16[128,256]{1,0:T(8,128)(2,1)} %bitcast.8), channel_id=1, source_target_pairs={{0,6},{2,4},{4,2},{6,0},{8,14},{10,12},{12,10},{14,8},{1,7},{3,5},... | collective-permute-start | bytes 196616 | tf_op jit(solution)/shard_map/ppermute | solution.py:138
  7.5 8.2 %collective-permute-start.2 = (bf16[128,256]{1,0:T(8,128)(2,1)}, bf16[128,256]{1,0:T(8,128)(2,1)S(1)}, u32[]{:S(2)}, u32[]{:S(2)}) collective-permute-start(bf16[128,256]{1,0:T(8,128)(2,1)} %bitcast.9), channel_id=1, source_target_pairs={{0,4},{4,0},{8,12},{12,8},{1,5},{5,1},{9,13},{13,9},{2,6},{6,2},{1... | collective-permute-start | bytes 196616 | tf_op jit(solution)/shard_map/ppermute | solution.py:138
  8.7 6.9 %collective-permute-start.1 = (bf16[128,256]{1,0:T(8,128)(2,1)}, bf16[128,256]{1,0:T(8,128)(2,1)S(1)}, u32[]{:S(2)}, u32[]{:S(2)}) collective-permute-start(bf16[128,256]{1,0:T(8,128)(2,1)} %bitcast.10), channel_id=1, source_target_pairs={{0,2},{2,0},{1,3},{3,1},{4,6},{6,4},{5,7},{7,5},{8,10},{10,8},{9,1... | collective-permute-start | bytes 196616 | tf_op jit(solution)/shard_map/ppermute | solution.py:138
  9.2 6.5 %collective-permute-start.6 = (bf16[128,256]{1,0:T(8,128)(2,1)S(1)}, bf16[128,256]{1,0:T(8,128)(2,1)S(1)}, u32[]{:S(2)}, u32[]{:S(2)}) collective-permute-start(bf16[128,256]{1,0:T(8,128)(2,1)S(1)} %collective-permute-done.5.refs_2_), channel_id=1, source_target_pairs={{0,2},{2,0},{1,3},{3,1},{4,6},{6,4},{5,7},{7,5},{8,10},{10,8},{9,1... | collective-permute-start | bytes 196616 | tf_op jit(solution)/shard_map/ppermute | solution.py:138
  11.7 4.3 %collective-permute-start.4 = (bf16[128,256]{1,0:T(8,128)(2,1)S(1)}, bf16[128,256]{1,0:T(8,128)(2,1)S(1)}, u32[]{:S(2)}, u32[]{:S(2)}) collective-permute-start(bf16[128,256]{1,0:T(8,128)(2,1)S(1)} %collective-permute-done._.refs_0_), channel_id=1, source_target_pairs={{0,2},{2,0},{1,3},{3,1},{4,6},{6,4},{5,7},{7,5},{8,10},{10,8},{9,1... | collective-permute-start | bytes 196616 | tf_op jit(solution)/shard_map/ppermute | solution.py:138
  15.7 2.0 %collective-permute-start.7 = (bf16[528,256]{1,0:T(8,128)(2,1)S(1)}, bf16[528,256]{1,0:T(8,128)(2,1)S(1)}, u32[]{:S(2)}, u32[]{:S(2)}) collective-permute-start(bf16[528,256]{1,0:T(8,128)(2,1)S(1)} %near.1.near_ref), channel_id=1, source_target_pairs={{0,1},{1,0},{2,3},{3,2},{4,5},{5,4},{6,7},{7,6},{8,9},{9,8},{10,11... | collective-permute-start | bytes 811016 | tf_op jit(solution)/shard_map/ppermute | solution.py:138
  15.9 1.7 %collective-permute-start.8 = (bf16[512,256]{1,0:T(8,128)(2,1)S(1)}, bf16[512,256]{1,0:T(8,128)(2,1)S(1)}, u32[]{:S(2)}, u32[]{:S(2)}) collective-permute-start(bf16[512,256]{1,0:T(8,128)(2,1)S(1)} %far.1.far_ref), channel_id=1, source_target_pairs={{0,1},{1,0},{2,3},{3,2},{4,5},{5,4},{6,7},{7,6},{8,9},{9,8},{10,11... | collective-permute-start | bytes 786440 | tf_op jit(solution)/shard_map/ppermute | solution.py:138
  21.1 4.3 %collective-permute-start.9 = (bf16[128,256]{1,0:T(8,128)(2,1)S(1)}, bf16[128,256]{1,0:T(8,128)(2,1)S(1)}, u32[]{:S(2)}, u32[]{:S(2)}) collective-permute-start(bf16[128,256]{1,0:T(8,128)(2,1)S(1)} %get-tuple-element.37), channel_id=1, source_target_pairs={{0,2},{2,0},{1,3},{3,1},{4,6},{6,4},{5,7},{7,5},{8,10},{10,8},{9,1... | collective-permute-start | bytes 196616 | tf_op jit(solution)/shard_map/ppermute | solution.py:138

commit v6 on v5

--- a/solution.py
+++ b/solution.py
@@ -296,12 +296,12 @@
 
 def main_kernel(
     near_ref, far_ref, other_near_ref, other_far_ref, query_ref, key_ref, value_ref, begun_query, begun_key, begun_value,
-    in_out_ref, own_out_ref, early_taps, last_tap,
-    attended_ref, activated, send_ref,
+    in_out_ref, early_taps, last_tap,
+    own_mixed, activated, send_ref,
     normed, queries, keyed, valued, mixed, resid, projected,
 ):
-    own_frames, _, cols, channels = attended_ref.shape
-    frames, rows = resid.shape[:2]
+    frames, rows, cols, channels = resid.shape
+    own_frames = own_mixed.shape[0] // cols
     tokens = frames * rows * cols
     frame_tokens = rows * cols
     space = lax.axis_index("space")
@@ -315,19 +315,19 @@
     layout = (own_frames, cols, rows, blocks)
     mine, other = core_chunks(near_ref, far_ref, layout), core_chunks(other_near_ref, other_far_ref, layout)
     norm_chunks(other, core_gain(other_near_ref, 0), normed)
-    for weight_ref, begun_ref, target in zip(
-        (query_ref, key_ref, value_ref), (begun_query, begun_key, begun_value), (queries, keyed, valued)
-    ):
-        term = jnp.dot(normed[...], weight_ref[channels:, :], preferred_element_type=jnp.float32)
-        target[...] = (begun_ref[...] + term).astype(jnp.bfloat16)
-
     in_channels = early_taps.shape[3]
     mine_in = block == half
     spans = [slice(frame * frame_tokens, (frame + 1) * frame_tokens) for frame in range(frames)]
+    for weight_ref, begun_ref, target in ((query_ref, begun_query, queries), (key_ref, begun_key, keyed)):
+        term = jnp.dot(normed[...], weight_ref[channels:, :], preferred_element_type=jnp.float32)
+        target[...] = (begun_ref[...] + term).astype(jnp.bfloat16)
     scores = [
         lax.dot_general(queries[at, :], keyed[at, :], (((1,), (1,)), ((), ())), preferred_element_type=jnp.float32)
         for at in spans
     ]
+    for weight_ref, begun_ref, target in ((value_ref, begun_value, valued),):
+        term = jnp.dot(normed[...], weight_ref[channels:, :], preferred_element_type=jnp.float32)
+        target[...] = (begun_ref[...] + term).astype(jnp.bfloat16)
     for at, score in zip(spans, scores):
         peak = jnp.max(score, axis=1, keepdims=True)
         weights = jnp.exp((score - peak) * (D ** (-0.5)))
@@ -341,10 +341,9 @@
         total = source + projected[chunk * cols : (chunk + 1) * cols, :].astype(jnp.float32)
         resid[chunk // rows, chunk % rows] = total
         totals = add_chunk(totals, total)
-    own_mixed = jnp.concatenate([mixed[at.start : at.start + cols, :] for at in spans[:own_frames]], axis=0)
-    attended_ref[...] = jnp.dot(
-        own_mixed, own_out_ref[...], preferred_element_type=jnp.float32
-    ).astype(jnp.bfloat16).reshape(own_frames, 1, cols, channels)
+    size = own_mixed.shape[0] // own_frames
+    for frame, at in enumerate(spans[:own_frames]):
+        own_mixed[frame * size : (frame + 1) * size, :] = mixed[at.start : at.start + size, :]
 
     centre, scale = chunk_statistics(totals, count)
     scale = 0.5 * scale * jnp.where(mine_in, core_gain(near_ref, 1), core_gain(other_near_ref, 1))
@@ -370,10 +369,14 @@
     for col_tap in range(3):
         total = None
         for time_tap in range(3):
-            for row_tap in range(3):
-                window = activated[row_tap, pl.ds(block * frames + time_tap, frames)].reshape(tokens, in_channels)
-                term = jnp.dot(window, taps[time_tap][row_tap, col_tap], preferred_element_type=jnp.float32)
-                total = term if total is None else total + term
+            start = block * frames + time_tap
+            windows = [activated[row_tap, pl.ds(start, frames)].reshape(tokens, in_channels) for row_tap in range(3)]
+            term = jnp.dot(
+                jnp.concatenate(windows, axis=1),
+                taps[time_tap][:, col_tap].reshape(3 * in_channels, -1),
+                preferred_element_type=jnp.float32,
+            )
+            total = term if total is None else total + term
         columns.append(total)
     place = lax.broadcasted_iota(jnp.int32, columns[0].shape, 0) % cols
     left = jnp.where(place == 0, 0.0, pltpu.roll(columns[0], 1, 0))
@@ -381,7 +384,10 @@
     return columns[1] + left + right
 
 
-def own_kernel(activated, early_taps, last_tap, attended_ref, attended_hbm, keep_ref, sent):
+def own_kernel(activated, early_taps, last_tap, own_mixed, own_out_ref, attended_hbm, keep_ref, attended_ref, sent):
+    attended_ref[...] = jnp.dot(
+        own_mixed[...], own_out_ref[...], preferred_element_type=jnp.float32
+    ).astype(jnp.bfloat16).reshape(attended_ref.shape)
     copy = pltpu.make_async_copy(attended_ref, attended_hbm, sent)
     copy.start()
     keep_ref[...] = partial_conv(activated, early_taps, last_tap, lax.axis_index("tm"), attended_ref.shape[0])
@@ -423,14 +429,14 @@
         compiler_params=pltpu.CompilerParams(vmem_limit_bytes=8 * 1024 * 1024),
         name="mine",
     )(near_mine, far_mine, *weights, in_hbm(conv_kernel))
-    attended, activated, send = pl.pallas_call(
+    own_mixed, activated, send = pl.pallas_call(
         main_kernel,
         out_shape=(
-            jax.ShapeDtypeStruct((frames, 1, cols, channels), jnp.bfloat16),
+            jax.ShapeDtypeStruct((frames * cols, D), jnp.bfloat16),
             jax.ShapeDtypeStruct((3, blocks * frames + 2, cols, in_channels), jnp.bfloat16),
             jax.ShapeDtypeStruct((frames * cols, out_channels), jnp.bfloat16),
         ),
-        in_specs=[in_vmem] * 14,
+        in_specs=[in_vmem] * 13,
         out_specs=(in_vmem,) * 3,
         scratch_shapes=[pltpu.VMEM((tokens, channels), jnp.bfloat16)]
         + [pltpu.VMEM((tokens, D), jnp.bfloat16)] * 4
@@ -438,20 +444,20 @@
         + [pltpu.VMEM((tokens, in_channels), jnp.bfloat16)],
         compiler_params=pltpu.CompilerParams(vmem_limit_bytes=24 * 1024 * 1024),
         name="block",
-    )(near_mine, far_mine, near_other, far_other, *weights, *begun, in_out, own_out, early_taps, last_tap)
+    )(near_mine, far_mine, near_other, far_other, *weights, *begun, in_out, early_taps, last_tap)
     received = exchange(send, "tm", 1)
     attended, keep = pl.pallas_call(
         own_kernel,
         out_shape=(
-            jax.ShapeDtypeStruct(attended.shape, attended.dtype),
+            jax.ShapeDtypeStruct((frames, 1, cols, channels), jnp.bfloat16),
             jax.ShapeDtypeStruct((frames * cols, out_channels), jnp.float32),
         ),
-        in_specs=[in_vmem] * 4,
+        in_specs=[in_vmem] * 5,
         out_specs=(pl.BlockSpec(memory_space=pl.ANY), in_vmem),
-        scratch_shapes=[pltpu.SemaphoreType.DMA],
+        scratch_shapes=[pltpu.VMEM((frames, 1, cols, channels), jnp.bfloat16), pltpu.SemaphoreType.DMA],
         compiler_params=pltpu.CompilerParams(vmem_limit_bytes=4 * 1024 * 1024),
         name="own",
-    )(activated, early_taps, last_tap, attended)
+    )(activated, early_taps, last_tap, own_mixed, own_out)
     total = keep + received.astype(jnp.float32)
     return attended, total.astype(jnp.bfloat16).reshape(frames, 1, cols, out_channels)
 

time: 26.2 us -> 26.1 us (level)
  waiting for transfers between devices: 3.34 us -> 2.82 us
  Pallas kernels: 7.82 us -> 8.27 us
    ppermute x10, waiting for transfers between devices: 3.34 us -> 2.82 us  [exchange(): return lax.ppermute(x, axes, [(i, i ^ step) for i in range(peers)])]
    pallas_call x2, Pallas kernels: 4.03 us -> 4.48 us  [the longest x1 3.3 us: gathered_plan(): pl.pallas_call(main_kernel, out_shape=(jax.ShapeDtypeStruct((frames * col...]
  transfers between devices with their start and end apart: 10 -> 10, of which waited for: 3 -> 3; matrix products, arithmetic and copies ran while one was open for 0% -> 0% of each run, Pallas kernels for 17% -> 19%
where the time goes in v6:
time: 26.1 us; the launch traced here: 26 us
  starting transfers between devices  13.5 us (52%)
  Pallas kernels  8.27 us (32%)
  waiting for transfers between devices  2.82 us (11%)
  between operations  0.73 us (3%)
  other arithmetic  0.65 us (2%)
    ppermute x10, starting transfers between devices, exchange(): return lax.ppermute(x, axes, [(i, i ^ step) for i in range(peers)])  13.5 us
    pallas_call x1, Pallas kernels, gathered_plan(): pl.pallas_call(main_kernel, out_shape=(jax.ShapeDtypeStruct((frames * col...  3.3 us
    ppermute x10, waiting for transfers between devices, exchange(): return lax.ppermute(x, axes, [(i, i ^ step) for i in range(peers)])  2.82 us
    pallas_call x1, Pallas kernels, stage(): pl.pallas_call(stage_kernel, out_shape=tuple(shapes), in_specs=[pl.BlockS...  2.45 us
    pallas_call x1, Pallas kernels, gathered_plan(): pl.pallas_call(functools.partial(mine_kernel, layout=(frames, cols, rows,...  1.28 us
    pallas_call x1, Pallas kernels, gathered_plan(): pl.pallas_call(own_kernel, out_shape=(jax.ShapeDtypeStruct((frames, 1, co...  1.18 us
    convert_element_type x1, other arithmetic, gathered_plan(): total.astype(jnp.bfloat16).reshape(frames, 1, cols, out_channels)  0.65 us
  transfers between devices with their start and end apart: 10, of which 3 were waited for; matrix products, arithmetic and copies ran while one was open for 0% of the time, Pallas kernels for 19%

profile of v6, /device:TPU:0, one launch (start us, length us, event | category | flops | bytes accessed | tf_op | source)
XLA Modules:
  0.0 26.0 jit_solution(9502182420612766248)
XLA Ops:
  0.6 5.1 %collective-permute-start.5 = (bf16[128,256]{1,0:T(8,128)(2,1)}, bf16[128,256]{1,0:T(8,128)(2,1)S(1)}, u32[]{:S(2)}, u32[]{:S(2)}) collective-permute-start(bf16[128,256]{1,0:T(8,128)(2,1)} %bitcast.6), channel_id=1, source_target_pairs={{0,12},{4,8},{8,4},{12,0},{1,13},{5,9},{9,5},{13,1},{2,14},{6,10},... | collective-permute-start | bytes 196616 | tf_op jit(solution)/shard_map/ppermute | solution.py:138
  5.7 0.0 collective-permute-start
  5.7 1.7 %collective-permute-start.3 = (bf16[128,256]{1,0:T(8,128)(2,1)}, bf16[128,256]{1,0:T(8,128)(2,1)S(1)}, u32[]{:S(2)}, u32[]{:S(2)}) collective-permute-start(bf16[128,256]{1,0:T(8,128)(2,1)} %bitcast.8), channel_id=1, source_target_pairs={{0,6},{2,4},{4,2},{6,0},{8,14},{10,12},{12,10},{14,8},{1,7},{3,5},... | collective-permute-start | bytes 196616 | tf_op jit(solution)/shard_map/ppermute | solution.py:138
  7.5 1.2 %collective-permute-start.2 = (bf16[128,256]{1,0:T(8,128)(2,1)}, bf16[128,256]{1,0:T(8,128)(2,1)S(1)}, u32[]{:S(2)}, u32[]{:S(2)}) collective-permute-start(bf16[128,256]{1,0:T(8,128)(2,1)} %bitcast.9), channel_id=1, source_target_pairs={{0,4},{4,0},{8,12},{12,8},{1,5},{5,1},{9,13},{13,9},{2,6},{6,2},{1... | collective-permute-start | bytes 196616 | tf_op jit(solution)/shard_map/ppermute | solution.py:138
  8.7 0.5 %collective-permute-start.1 = (bf16[128,256]{1,0:T(8,128)(2,1)}, bf16[128,256]{1,0:T(8,128)(2,1)S(1)}, u32[]{:S(2)}, u32[]{:S(2)}) collective-permute-start(bf16[128,256]{1,0:T(8,128)(2,1)} %bitcast.10), channel_id=1, source_target_pairs={{0,2},{2,0},{1,3},{3,1},{4,6},{6,4},{5,7},{7,5},{8,10},{10,8},{9,1... | collective-permute-start | bytes 196616 | tf_op jit(solution)/shard_map/ppermute | solution.py:138
  9.2 0.0 collective-permute-done.5.refs_2_
  9.2 1.5 %collective-permute-start.6 = (bf16[128,256]{1,0:T(8,128)(2,1)S(1)}, bf16[128,256]{1,0:T(8,128)(2,1)S(1)}, u32[]{:S(2)}, u32[]{:S(2)}) collective-permute-start(bf16[128,256]{1,0:T(8,128)(2,1)S(1)} %collective-permute-done.5.refs_2_), channel_id=1, source_target_pairs={{0,2},{2,0},{1,3},{3,1},{4,6},{6,4},{5,7},{7,5},{8,10},{10,8},{9,1... | collective-permute-start | bytes 196616 | tf_op jit(solution)/shard_map/ppermute | solution.py:138
  10.7 0.9 %collective-permute-done._.refs_0_ = bf16[128,256]{1,0:T(8,128)(2,1)S(1)} collective-permute-done((bf16[128,256]{1,0:T(8,128)(2,1)}, bf16[128,256]{1,0:T(8,128)(2,1)S(1)}, u32[]{:S(2)}, u32[]{:S(2)}) %collective-permute-start) | collective-permute-done | bytes 65568 | tf_op jit(solution)/shard_map/ppermute | solution.py:138
  11.7 1.5 %collective-permute-start.4 = (bf16[128,256]{1,0:T(8,128)(2,1)S(1)}, bf16[128,256]{1,0:T(8,128)(2,1)S(1)}, u32[]{:S(2)}, u32[]{:S(2)}) collective-permute-start(bf16[128,256]{1,0:T(8,128)(2,1)S(1)} %collective-permute-done._.refs_0_), channel_id=1, source_target_pairs={{0,2},{2,0},{1,3},{3,1},{4,6},{6,4},{5,7},{7,5},{8,10},{10,8},{9,1... | collective-permute-start | bytes 196616 | tf_op jit(solution)/shard_map/ppermute | solution.py:138
  13.2 2.4 %stage.1 = (bf16[512,512]{1,0:T(8,128)(2,1)S(1)}, bf16[512,512]{1,0:T(8,128)(2,1)S(1)}, bf16[512,512]{1,0:T(8,128)(2,1)S(1)}, bf16[512,256]{1,0:T(8,128)(2,1)S(1...) custom-call(bf16[512,512]{1,0:T(8,128)(2,1)} %query_hbm.1, ...), custom_call_target="tpu_custom_call" | custom-call | tf_op jit(solution)/shard_map/stage/pallas_call | solution.py:171
  15.6 0.0 collective-permute-done.3.refs_3_
  15.6 0.0 collective-permute-done.2.refs_2_
  15.6 0.0 collective-permute-done.1.refs_1_
  15.7 0.1 collective-permute-start.7
  15.8 0.0 collective-permute-done.6.refs_3_
  15.8 0.1 collective-permute-done.4.refs_1_
  15.9 0.4 %collective-permute-start.8 = (bf16[512,256]{1,0:T(8,128)(2,1)S(1)}, bf16[512,256]{1,0:T(8,128)(2,1)S(1)}, u32[]{:S(2)}, u32[]{:S(2)}) collective-permute-start(bf16[512,256]{1,0:T(8,128)(2,1)S(1)} %far.1.far_ref), channel_id=1, source_target_pairs={{0,1},{1,0},{2,3},{3,2},{4,5},{5,4},{6,7},{7,6},{8,9},{9,8},{10,11... | collective-permute-start | bytes 786440 | tf_op jit(solution)/shard_map/ppermute | solution.py:138
  16.4 1.3 %mine.1 = (f32[1024,512]{1,0:T(8,128)S(1)}, f32[1024,512]{1,0:T(8,128)S(1)}, f32[1024,512]{1,0:T(8,128)S(1)}, bf16[1,3,3,256,256]{4,3,2,1,0:T(8,128)(2,1)S(1)}) custom-call(bf16[528,256]{1,0:T(8,128)(2,1)S(1)} %near.1.near_ref, bf16[512,256]{1,0:T(8,128)(2,1)S(1)} %far.1.far_ref, bf16[512,512]{1,0:T(8,128)(2,1)S(1)} %get-tuple-element.23.query_ref, ...), custom_call_target="tpu_custom_call" | custom-call | tf_op jit(solution)/shard_map/mine/pallas_call | solution.py:422
  17.6 0.0 collective-permute-done.7.other_near_ref
  17.7 0.0 collective-permute-done.8.other_far_ref
  17.7 3.3 %block.1 = (bf16[128,512]{1,0:T(8,128)(2,1)S(1)}, bf16[3,6,64,256]{3,2,1,0:T(8,128)(2,1)S(1)}, bf16[128,256]{1,0:T(8,128)(2,1)S(1)}) custom-call(bf16[528,256]{1,0:T(8,128)(2,1)S(1)} %near.1.near_ref, bf16[512,256]{1,0:T(8,128)(2,1)S(1)} %far.1.far_ref, bf16[528,256]{1,0:T(8,128)(2,1)S(1)} %collective-permute-done.7.other_near_ref, ...), custom_call_target="tpu_custom_call" | custom-call | tf_op jit(solution)/shard_map/block/pallas_call | solution.py:432
  21.0 1.4 %collective-permute-start.9 = (bf16[128,256]{1,0:T(8,128)(2,1)S(1)}, bf16[128,256]{1,0:T(8,128)(2,1)S(1)}, u32[]{:S(2)}, u32[]{:S(2)}) collective-permute-start(bf16[128,256]{1,0:T(8,128)(2,1)S(1)} %get-tuple-element.37), channel_id=1, source_target_pairs={{0,2},{2,0},{1,3},{3,1},{4,6},{6,4},{5,7},{7,5},{8,10},{10,8},{9,1... | collective-permute-start | bytes 196616 | tf_op jit(solution)/shard_map/ppermute | solution.py:138
  22.4 1.2 %own.1 = (bf16[2,1,64,256]{3,2,1,0:T(8,128)(2,1)}, f32[128,256]{1,0:T(8,128)S(1)}) custom-call(bf16[3,6,64,256]{3,2,1,0:T(8,128)(2,1)S(1)} %get-tuple-element.32.activated, bf16[2,3,3,256,256]{4,3,2,1,0:T(8,128)(2,1)S(1)} %get-tuple-element.30.early_taps, bf16[1,3,3,256,256]{4,3,2,1,0:T(8,128)(2,1)S(1)} %get-tuple-element.31.last_tap, ...), custom_call_target="tpu_custom_call" | custom-call | tf_op jit(solution)/shard_map/own/pallas_call | solution.py:449
  23.6 1.7 %collective-permute-done.9 = bf16[128,256]{1,0:T(8,128)(2,1)S(1)} collective-permute-done((bf16[128,256]{1,0:T(8,128)(2,1)S(1)}, bf16[128,256]{1,0:T(8,128)(2,1)S(1)}, u32[]{:S(2)}, u32[]{:S(2)}) %collective-permute-start.9) | collective-permute-done | bytes 65568 | tf_op jit(solution)/shard_map/ppermute | solution.py:138
  25.3 0.6 %add_convert_fusion = bf16[128,256]{1,0:T(8,128)(2,1)} fusion(f32[128,256]{1,0:T(8,128)S(1)} %get-tuple-element.36, bf16[128,256]{1,0:T(8,128)(2,1)S(1)} %collective-permute-done.9), kind=kLoop, calls=%fused_computation | loop fusion | flops 98304 | bytes 262144 | tf_op jit(solution)/shard_map/convert_element_type | solution.py:462
  (2 shorter events, 0.1 us)
Async XLA Ops:
  0.6 8.6 %collective-permute-start.5 = (bf16[128,256]{1,0:T(8,128)(2,1)}, bf16[128,256]{1,0:T(8,128)(2,1)S(1)}, u32[]{:S(2)}, u32[]{:S(2)}) collective-permute-start(bf16[128,256]{1,0:T(8,128)(2,1)} %bitcast.6), channel_id=1, source_target_pairs={{0,12},{4,8},{8,4},{12,0},{1,13},{5,9},{9,5},{13,1},{2,14},{6,10},... | collective-permute-start | bytes 196616 | tf_op jit(solution)/shard_map/ppermute | solution.py:138
  5.7 5.9 %collective-permute-start = (bf16[128,256]{1,0:T(8,128)(2,1)}, bf16[128,256]{1,0:T(8,128)(2,1)S(1)}, u32[]{:S(2)}, u32[]{:S(2)}) collective-permute-start(bf16[128,256]{1,0:T(8,128)(2,1)} %bitcast.7), channel_id=1, source_target_pairs={{0,8},{4,12},{8,0},{12,4},{1,9},{5,13},{9,1},{13,5},{2,10},{6,14},... | collective-permute-start | bytes 196616 | tf_op jit(solution)/shard_map/ppermute | solution.py:138
  5.7 9.9 %collective-permute-start.3 = (bf16[128,256]{1,0:T(8,128)(2,1)}, bf16[128,256]{1,0:T(8,128)(2,1)S(1)}, u32[]{:S(2)}, u32[]{:S(2)}) collective-permute-start(bf16[128,256]{1,0:T(8,128)(2,1)} %bitcast.8), channel_id=1, source_target_pairs={{0,6},{2,4},{4,2},{6,0},{8,14},{10,12},{12,10},{14,8},{1,7},{3,5},... | collective-permute-start | bytes 196616 | tf_op jit(solution)/shard_map/ppermute | solution.py:138
  7.5 8.2 %collective-permute-start.2 = (bf16[128,256]{1,0:T(8,128)(2,1)}, bf16[128,256]{1,0:T(8,128)(2,1)S(1)}, u32[]{:S(2)}, u32[]{:S(2)}) collective-permute-start(bf16[128,256]{1,0:T(8,128)(2,1)} %bitcast.9), channel_id=1, source_target_pairs={{0,4},{4,0},{8,12},{12,8},{1,5},{5,1},{9,13},{13,9},{2,6},{6,2},{1... | collective-permute-start | bytes 196616 | tf_op jit(solution)/shard_map/ppermute | solution.py:138
  8.7 6.9 %collective-permute-start.1 = (bf16[128,256]{1,0:T(8,128)(2,1)}, bf16[128,256]{1,0:T(8,128)(2,1)S(1)}, u32[]{:S(2)}, u32[]{:S(2)}) collective-permute-start(bf16[128,256]{1,0:T(8,128)(2,1)} %bitcast.10), channel_id=1, source_target_pairs={{0,2},{2,0},{1,3},{3,1},{4,6},{6,4},{5,7},{7,5},{8,10},{10,8},{9,1... | collective-permute-start | bytes 196616 | tf_op jit(solution)/shard_map/ppermute | solution.py:138
  9.2 6.5 %collective-permute-start.6 = (bf16[128,256]{1,0:T(8,128)(2,1)S(1)}, bf16[128,256]{1,0:T(8,128)(2,1)S(1)}, u32[]{:S(2)}, u32[]{:S(2)}) collective-permute-start(bf16[128,256]{1,0:T(8,128)(2,1)S(1)} %collective-permute-done.5.refs_2_), channel_id=1, source_target_pairs={{0,2},{2,0},{1,3},{3,1},{4,6},{6,4},{5,7},{7,5},{8,10},{10,8},{9,1... | collective-permute-start | bytes 196616 | tf_op jit(solution)/shard_map/ppermute | solution.py:138
  11.7 4.3 %collective-permute-start.4 = (bf16[128,256]{1,0:T(8,128)(2,1)S(1)}, bf16[128,256]{1,0:T(8,128)(2,1)S(1)}, u32[]{:S(2)}, u32[]{:S(2)}) collective-permute-start(bf16[128,256]{1,0:T(8,128)(2,1)S(1)} %collective-permute-done._.refs_0_), channel_id=1, source_target_pairs={{0,2},{2,0},{1,3},{3,1},{4,6},{6,4},{5,7},{7,5},{8,10},{10,8},{9,1... | collective-permute-start | bytes 196616 | tf_op jit(solution)/shard_map/ppermute | solution.py:138
  15.7 2.0 %collective-permute-start.7 = (bf16[528,256]{1,0:T(8,128)(2,1)S(1)}, bf16[528,256]{1,0:T(8,128)(2,1)S(1)}, u32[]{:S(2)}, u32[]{:S(2)}) collective-permute-start(bf16[528,256]{1,0:T(8,128)(2,1)S(1)} %near.1.near_ref), channel_id=1, source_target_pairs={{0,1},{1,0},{2,3},{3,2},{4,5},{5,4},{6,7},{7,6},{8,9},{9,8},{10,11... | collective-permute-start | bytes 811016 | tf_op jit(solution)/shard_map/ppermute | solution.py:138
  15.9 1.7 %collective-permute-start.8 = (bf16[512,256]{1,0:T(8,128)(2,1)S(1)}, bf16[512,256]{1,0:T(8,128)(2,1)S(1)}, u32[]{:S(2)}, u32[]{:S(2)}) collective-permute-start(bf16[512,256]{1,0:T(8,128)(2,1)S(1)} %far.1.far_ref), channel_id=1, source_target_pairs={{0,1},{1,0},{2,3},{3,2},{4,5},{5,4},{6,7},{7,6},{8,9},{9,8},{10,11... | collective-permute-start | bytes 786440 | tf_op jit(solution)/shard_map/ppermute | solution.py:138
  21.0 4.3 %collective-permute-start.9 = (bf16[128,256]{1,0:T(8,128)(2,1)S(1)}, bf16[128,256]{1,0:T(8,128)(2,1)S(1)}, u32[]{:S(2)}, u32[]{:S(2)}) collective-permute-start(bf16[128,256]{1,0:T(8,128)(2,1)S(1)} %get-tuple-element.37), channel_id=1, source_target_pairs={{0,2},{2,0},{1,3},{3,1},{4,6},{6,4},{5,7},{7,5},{8,10},{10,8},{9,1... | collective-permute-start | bytes 196616 | tf_op jit(solution)/shard_map/ppermute | solution.py:138

commit v7 on v6

--- a/solution.py
+++ b/solution.py
@@ -407,7 +407,7 @@
     for row in range(1, rows // 2):
         onward[row] = exchange(own, ("space", "tm"), row * blocks + 1)
     staged = (query_weight, key_weight, value_weight, out_weight, own, *gains, conv_kernel)
-    *weights, in_out, own_out, own_staged, first_gain, second_gain, early_taps = stage(staged, by_row[rows // 2])
+    *weights, in_out, own_out, own_staged, first_gain, second_gain, early_taps = stage(staged, by_row[rows - 1])
     near = [own_staged, first]
     for row in range(1, rows // 2):
         near += [by_row[row], onward[row]]

time: 26.1 us -> 26.1 us (level)
  waiting for transfers between devices: 2.82 us -> 2.4 us
  starting transfers between devices: 13.5 us -> 13.9 us
    ppermute x10, starting transfers between devices: 13.5 us -> 13.9 us  [exchange(): return lax.ppermute(x, axes, [(i, i ^ step) for i in range(peers)])]
    ppermute x10, waiting for transfers between devices: 2.82 us -> 2.4 us  [exchange(): return lax.ppermute(x, axes, [(i, i ^ step) for i in range(peers)])]
where the time goes in v7:
time: 26.1 us; the launch traced here: 26 us
  starting transfers between devices  13.9 us (53%)
  Pallas kernels  8.27 us (32%)
  waiting for transfers between devices  2.4 us (9%)
  between operations  0.73 us (3%)
  other arithmetic  0.65 us (2%)
    ppermute x10, starting transfers between devices, exchange(): return lax.ppermute(x, axes, [(i, i ^ step) for i in range(peers)])  13.9 us
    pallas_call x1, Pallas kernels, gathered_plan(): pl.pallas_call(main_kernel, out_shape=(jax.ShapeDtypeStruct((frames * col...  3.3 us
    pallas_call x1, Pallas kernels, stage(): pl.pallas_call(stage_kernel, out_shape=tuple(shapes), in_specs=[pl.BlockS...  2.45 us
    ppermute x10, waiting for transfers between devices, exchange(): return lax.ppermute(x, axes, [(i, i ^ step) for i in range(peers)])  2.4 us
    pallas_call x1, Pallas kernels, gathered_plan(): pl.pallas_call(functools.partial(mine_kernel, layout=(frames, cols, rows,...  1.28 us
    pallas_call x1, Pallas kernels, gathered_plan(): pl.pallas_call(own_kernel, out_shape=(jax.ShapeDtypeStruct((frames, 1, co...  1.18 us
    convert_element_type x1, other arithmetic, gathered_plan(): total.astype(jnp.bfloat16).reshape(frames, 1, cols, out_channels)  0.65 us
  transfers between devices with their start and end apart: 10, of which 3 were waited for; matrix products, arithmetic and copies ran while one was open for 0% of the time, Pallas kernels for 19%

profile of v7, /device:TPU:0, one launch (start us, length us, event | category | flops | bytes accessed | tf_op | source)
XLA Modules:
  0.0 26.0 jit_solution(15822874505578225024)
XLA Ops:
  0.6 4.1 %collective-permute-start.4 = (bf16[128,256]{1,0:T(8,128)(2,1)}, bf16[128,256]{1,0:T(8,128)(2,1)S(1)}, u32[]{:S(2)}, u32[]{:S(2)}) collective-permute-start(bf16[128,256]{1,0:T(8,128)(2,1)} %bitcast.6), channel_id=1, source_target_pairs={{0,8},{4,12},{8,0},{12,4},{1,9},{5,13},{9,1},{13,5},{2,10},{6,14},... | collective-permute-start | bytes 196616 | tf_op jit(solution)/shard_map/ppermute | solution.py:138
  4.7 1.3 %collective-permute-start = (bf16[128,256]{1,0:T(8,128)(2,1)}, bf16[128,256]{1,0:T(8,128)(2,1)S(1)}, u32[]{:S(2)}, u32[]{:S(2)}) collective-permute-start(bf16[128,256]{1,0:T(8,128)(2,1)} %bitcast.7), channel_id=1, source_target_pairs={{0,12},{4,8},{8,4},{12,0},{1,13},{5,9},{9,5},{13,1},{2,14},{6,10},... | collective-permute-start | bytes 196616 | tf_op jit(solution)/shard_map/ppermute | solution.py:138
  6.1 1.2 %collective-permute-start.3 = (bf16[128,256]{1,0:T(8,128)(2,1)}, bf16[128,256]{1,0:T(8,128)(2,1)S(1)}, u32[]{:S(2)}, u32[]{:S(2)}) collective-permute-start(bf16[128,256]{1,0:T(8,128)(2,1)} %bitcast.8), channel_id=1, source_target_pairs={{0,6},{2,4},{4,2},{6,0},{8,14},{10,12},{12,10},{14,8},{1,7},{3,5},... | collective-permute-start | bytes 196616 | tf_op jit(solution)/shard_map/ppermute | solution.py:138
  7.2 1.8 %collective-permute-start.2 = (bf16[128,256]{1,0:T(8,128)(2,1)}, bf16[128,256]{1,0:T(8,128)(2,1)S(1)}, u32[]{:S(2)}, u32[]{:S(2)}) collective-permute-start(bf16[128,256]{1,0:T(8,128)(2,1)} %bitcast.9), channel_id=1, source_target_pairs={{0,4},{4,0},{8,12},{12,8},{1,5},{5,1},{9,13},{13,9},{2,6},{6,2},{1... | collective-permute-start | bytes 196616 | tf_op jit(solution)/shard_map/ppermute | solution.py:138
  9.0 0.5 %collective-permute-start.1 = (bf16[128,256]{1,0:T(8,128)(2,1)}, bf16[128,256]{1,0:T(8,128)(2,1)S(1)}, u32[]{:S(2)}, u32[]{:S(2)}) collective-permute-start(bf16[128,256]{1,0:T(8,128)(2,1)} %bitcast.10), channel_id=1, source_target_pairs={{0,2},{2,0},{1,3},{3,1},{4,6},{6,4},{5,7},{7,5},{8,10},{10,8},{9,1... | collective-permute-start | bytes 196616 | tf_op jit(solution)/shard_map/ppermute | solution.py:138
  9.6 0.0 collective-permute-done.4.refs_0_
  9.6 1.7 %collective-permute-start.5 = (bf16[128,256]{1,0:T(8,128)(2,1)S(1)}, bf16[128,256]{1,0:T(8,128)(2,1)S(1)}, u32[]{:S(2)}, u32[]{:S(2)}) collective-permute-start(bf16[128,256]{1,0:T(8,128)(2,1)S(1)} %collective-permute-done.4.refs_0_), channel_id=1, source_target_pairs={{0,2},{2,0},{1,3},{3,1},{4,6},{6,4},{5,7},{7,5},{8,10},{10,8},{9,1... | collective-permute-start | bytes 196616 | tf_op jit(solution)/shard_map/ppermute | solution.py:138
  11.2 0.5 %collective-permute-done._.refs_2_ = bf16[128,256]{1,0:T(8,128)(2,1)S(1)} collective-permute-done((bf16[128,256]{1,0:T(8,128)(2,1)}, bf16[128,256]{1,0:T(8,128)(2,1)S(1)}, u32[]{:S(2)}, u32[]{:S(2)}) %collective-permute-start) | collective-permute-done | bytes 65568 | tf_op jit(solution)/shard_map/ppermute | solution.py:138
  11.7 1.5 %collective-permute-start.6 = (bf16[128,256]{1,0:T(8,128)(2,1)S(1)}, bf16[128,256]{1,0:T(8,128)(2,1)S(1)}, u32[]{:S(2)}, u32[]{:S(2)}) collective-permute-start(bf16[128,256]{1,0:T(8,128)(2,1)S(1)} %collective-permute-done._.refs_2_), channel_id=1, source_target_pairs={{0,2},{2,0},{1,3},{3,1},{4,6},{6,4},{5,7},{7,5},{8,10},{10,8},{9,1... | collective-permute-start | bytes 196616 | tf_op jit(solution)/shard_map/ppermute | solution.py:138
  13.2 2.4 %stage.1 = (bf16[512,512]{1,0:T(8,128)(2,1)S(1)}, bf16[512,512]{1,0:T(8,128)(2,1)S(1)}, bf16[512,512]{1,0:T(8,128)(2,1)S(1)}, bf16[512,256]{1,0:T(8,128)(2,1)S(1...) custom-call(bf16[512,512]{1,0:T(8,128)(2,1)} %query_hbm.1, ...), custom_call_target="tpu_custom_call" | custom-call | tf_op jit(solution)/shard_map/stage/pallas_call | solution.py:171
  15.6 0.0 collective-permute-done.3.refs_3_
  15.6 0.0 collective-permute-done.2.refs_2_
  15.7 0.0 collective-permute-done.1.refs_1_
  15.7 0.1 collective-permute-start.7
  15.8 0.0 collective-permute-done.5.refs_1_
  15.8 0.2 collective-permute-done.6.refs_3_
  16.0 0.4 %collective-permute-start.8 = (bf16[512,256]{1,0:T(8,128)(2,1)S(1)}, bf16[512,256]{1,0:T(8,128)(2,1)S(1)}, u32[]{:S(2)}, u32[]{:S(2)}) collective-permute-start(bf16[512,256]{1,0:T(8,128)(2,1)S(1)} %far.1.far_ref), channel_id=1, source_target_pairs={{0,1},{1,0},{2,3},{3,2},{4,5},{5,4},{6,7},{7,6},{8,9},{9,8},{10,11... | collective-permute-start | bytes 786440 | tf_op jit(solution)/shard_map/ppermute | solution.py:138
  16.4 1.3 %mine.1 = (f32[1024,512]{1,0:T(8,128)S(1)}, f32[1024,512]{1,0:T(8,128)S(1)}, f32[1024,512]{1,0:T(8,128)S(1)}, bf16[1,3,3,256,256]{4,3,2,1,0:T(8,128)(2,1)S(1)}) custom-call(bf16[528,256]{1,0:T(8,128)(2,1)S(1)} %near.1.near_ref, bf16[512,256]{1,0:T(8,128)(2,1)S(1)} %far.1.far_ref, bf16[512,512]{1,0:T(8,128)(2,1)S(1)} %get-tuple-element.23.query_ref, ...), custom_call_target="tpu_custom_call" | custom-call | tf_op jit(solution)/shard_map/mine/pallas_call | solution.py:422
  17.7 0.0 collective-permute-done.7.other_near_ref
  17.7 0.0 collective-permute-done.8.other_far_ref
  17.7 3.3 %block.1 = (bf16[128,512]{1,0:T(8,128)(2,1)S(1)}, bf16[3,6,64,256]{3,2,1,0:T(8,128)(2,1)S(1)}, bf16[128,256]{1,0:T(8,128)(2,1)S(1)}) custom-call(bf16[528,256]{1,0:T(8,128)(2,1)S(1)} %near.1.near_ref, bf16[512,256]{1,0:T(8,128)(2,1)S(1)} %far.1.far_ref, bf16[528,256]{1,0:T(8,128)(2,1)S(1)} %collective-permute-done.7.other_near_ref, ...), custom_call_target="tpu_custom_call" | custom-call | tf_op jit(solution)/shard_map/block/pallas_call | solution.py:432
  21.0 1.4 %collective-permute-start.9 = (bf16[128,256]{1,0:T(8,128)(2,1)S(1)}, bf16[128,256]{1,0:T(8,128)(2,1)S(1)}, u32[]{:S(2)}, u32[]{:S(2)}) collective-permute-start(bf16[128,256]{1,0:T(8,128)(2,1)S(1)} %get-tuple-element.37), channel_id=1, source_target_pairs={{0,2},{2,0},{1,3},{3,1},{4,6},{6,4},{5,7},{7,5},{8,10},{10,8},{9,1... | collective-permute-start | bytes 196616 | tf_op jit(solution)/shard_map/ppermute | solution.py:138
  22.4 1.2 %own.1 = (bf16[2,1,64,256]{3,2,1,0:T(8,128)(2,1)}, f32[128,256]{1,0:T(8,128)S(1)}) custom-call(bf16[3,6,64,256]{3,2,1,0:T(8,128)(2,1)S(1)} %get-tuple-element.32.activated, bf16[2,3,3,256,256]{4,3,2,1,0:T(8,128)(2,1)S(1)} %get-tuple-element.30.early_taps, bf16[1,3,3,256,256]{4,3,2,1,0:T(8,128)(2,1)S(1)} %get-tuple-element.31.last_tap, ...), custom_call_target="tpu_custom_call" | custom-call | tf_op jit(solution)/shard_map/own/pallas_call | solution.py:449
  23.6 1.7 %collective-permute-done.9 = bf16[128,256]{1,0:T(8,128)(2,1)S(1)} collective-permute-done((bf16[128,256]{1,0:T(8,128)(2,1)S(1)}, bf16[128,256]{1,0:T(8,128)(2,1)S(1)}, u32[]{:S(2)}, u32[]{:S(2)}) %collective-permute-start.9) | collective-permute-done | bytes 65568 | tf_op jit(solution)/shard_map/ppermute | solution.py:138
  25.3 0.6 %add_convert_fusion = bf16[128,256]{1,0:T(8,128)(2,1)} fusion(f32[128,256]{1,0:T(8,128)S(1)} %get-tuple-element.36, bf16[128,256]{1,0:T(8,128)(2,1)S(1)} %collective-permute-done.9), kind=kLoop, calls=%fused_computation | loop fusion | flops 98304 | bytes 262144 | tf_op jit(solution)/shard_map/convert_element_type | solution.py:462
  (2 shorter events, 0.1 us)
Async XLA Ops:
  0.6 8.9 %collective-permute-start.4 = (bf16[128,256]{1,0:T(8,128)(2,1)}, bf16[128,256]{1,0:T(8,128)(2,1)S(1)}, u32[]{:S(2)}, u32[]{:S(2)}) collective-permute-start(bf16[128,256]{1,0:T(8,128)(2,1)} %bitcast.6), channel_id=1, source_target_pairs={{0,8},{4,12},{8,0},{12,4},{1,9},{5,13},{9,1},{13,5},{2,10},{6,14},... | collective-permute-start | bytes 196616 | tf_op jit(solution)/shard_map/ppermute | solution.py:138
  4.7 7.0 %collective-permute-start = (bf16[128,256]{1,0:T(8,128)(2,1)}, bf16[128,256]{1,0:T(8,128)(2,1)S(1)}, u32[]{:S(2)}, u32[]{:S(2)}) collective-permute-start(bf16[128,256]{1,0:T(8,128)(2,1)} %bitcast.7), channel_id=1, source_target_pairs={{0,12},{4,8},{8,4},{12,0},{1,13},{5,9},{9,5},{13,1},{2,14},{6,10},... | collective-permute-start | bytes 196616 | tf_op jit(solution)/shard_map/ppermute | solution.py:138
  6.1 9.6 %collective-permute-start.3 = (bf16[128,256]{1,0:T(8,128)(2,1)}, bf16[128,256]{1,0:T(8,128)(2,1)S(1)}, u32[]{:S(2)}, u32[]{:S(2)}) collective-permute-start(bf16[128,256]{1,0:T(8,128)(2,1)} %bitcast.8), channel_id=1, source_target_pairs={{0,6},{2,4},{4,2},{6,0},{8,14},{10,12},{12,10},{14,8},{1,7},{3,5},... | collective-permute-start | bytes 196616 | tf_op jit(solution)/shard_map/ppermute | solution.py:138
  7.2 8.4 %collective-permute-start.2 = (bf16[128,256]{1,0:T(8,128)(2,1)}, bf16[128,256]{1,0:T(8,128)(2,1)S(1)}, u32[]{:S(2)}, u32[]{:S(2)}) collective-permute-start(bf16[128,256]{1,0:T(8,128)(2,1)} %bitcast.9), channel_id=1, source_target_pairs={{0,4},{4,0},{8,12},{12,8},{1,5},{5,1},{9,13},{13,9},{2,6},{6,2},{1... | collective-permute-start | bytes 196616 | tf_op jit(solution)/shard_map/ppermute | solution.py:138
  9.0 6.6 %collective-permute-start.1 = (bf16[128,256]{1,0:T(8,128)(2,1)}, bf16[128,256]{1,0:T(8,128)(2,1)S(1)}, u32[]{:S(2)}, u32[]{:S(2)}) collective-permute-start(bf16[128,256]{1,0:T(8,128)(2,1)} %bitcast.10), channel_id=1, source_target_pairs={{0,2},{2,0},{1,3},{3,1},{4,6},{6,4},{5,7},{7,5},{8,10},{10,8},{9,1... | collective-permute-start | bytes 196616 | tf_op jit(solution)/shard_map/ppermute | solution.py:138
  9.6 6.2 %collective-permute-start.5 = (bf16[128,256]{1,0:T(8,128)(2,1)S(1)}, bf16[128,256]{1,0:T(8,128)(2,1)S(1)}, u32[]{:S(2)}, u32[]{:S(2)}) collective-permute-start(bf16[128,256]{1,0:T(8,128)(2,1)S(1)} %collective-permute-done.4.refs_0_), channel_id=1, source_target_pairs={{0,2},{2,0},{1,3},{3,1},{4,6},{6,4},{5,7},{7,5},{8,10},{10,8},{9,1... | collective-permute-start | bytes 196616 | tf_op jit(solution)/shard_map/ppermute | solution.py:138
  11.7 4.3 %collective-permute-start.6 = (bf16[128,256]{1,0:T(8,128)(2,1)S(1)}, bf16[128,256]{1,0:T(8,128)(2,1)S(1)}, u32[]{:S(2)}, u32[]{:S(2)}) collective-permute-start(bf16[128,256]{1,0:T(8,128)(2,1)S(1)} %collective-permute-done._.refs_2_), channel_id=1, source_target_pairs={{0,2},{2,0},{1,3},{3,1},{4,6},{6,4},{5,7},{7,5},{8,10},{10,8},{9,1... | collective-permute-start | bytes 196616 | tf_op jit(solution)/shard_map/ppermute | solution.py:138
  15.7 2.0 %collective-permute-start.7 = (bf16[528,256]{1,0:T(8,128)(2,1)S(1)}, bf16[528,256]{1,0:T(8,128)(2,1)S(1)}, u32[]{:S(2)}, u32[]{:S(2)}) collective-permute-start(bf16[528,256]{1,0:T(8,128)(2,1)S(1)} %near.1.near_ref), channel_id=1, source_target_pairs={{0,1},{1,0},{2,3},{3,2},{4,5},{5,4},{6,7},{7,6},{8,9},{9,8},{10,11... | collective-permute-start | bytes 811016 | tf_op jit(solution)/shard_map/ppermute | solution.py:138
  16.0 1.7 %collective-permute-start.8 = (bf16[512,256]{1,0:T(8,128)(2,1)S(1)}, bf16[512,256]{1,0:T(8,128)(2,1)S(1)}, u32[]{:S(2)}, u32[]{:S(2)}) collective-permute-start(bf16[512,256]{1,0:T(8,128)(2,1)S(1)} %far.1.far_ref), channel_id=1, source_target_pairs={{0,1},{1,0},{2,3},{3,2},{4,5},{5,4},{6,7},{7,6},{8,9},{9,8},{10,11... | collective-permute-start | bytes 786440 | tf_op jit(solution)/shard_map/ppermute | solution.py:138
  21.0 4.3 %collective-permute-start.9 = (bf16[128,256]{1,0:T(8,128)(2,1)S(1)}, bf16[128,256]{1,0:T(8,128)(2,1)S(1)}, u32[]{:S(2)}, u32[]{:S(2)}) collective-permute-start(bf16[128,256]{1,0:T(8,128)(2,1)S(1)} %get-tuple-element.37), channel_id=1, source_target_pairs={{0,2},{2,0},{1,3},{3,1},{4,6},{6,4},{5,7},{7,5},{8,10},{10,8},{9,1... | collective-permute-start | bytes 196616 | tf_op jit(solution)/shard_map/ppermute | solution.py:138

commit v8 on v6

--- a/solution.py
+++ b/solution.py
@@ -12,6 +12,7 @@
 
 
 EPSILON = 1e-06
+LOG2_E = 1.4426950408889634
 
 
 def shifted_2(x, axis, by):
@@ -330,7 +331,7 @@
         target[...] = (begun_ref[...] + term).astype(jnp.bfloat16)
     for at, score in zip(spans, scores):
         peak = jnp.max(score, axis=1, keepdims=True)
-        weights = jnp.exp((score - peak) * (D ** (-0.5)))
+        weights = jnp.exp2((score - peak) * (D ** (-0.5) * LOG2_E))
         mass = jnp.sum(weights, axis=1, keepdims=True)
         blend = jnp.dot(weights.astype(jnp.bfloat16), valued[at, :], preferred_element_type=jnp.float32)
         mixed[at, :] = (blend * (1.0 / mass)).astype(jnp.bfloat16)

time: 26.1 us -> 26.1 us (level)
  no operation moved by 1% of the time
where the time goes in v8:
time: 26.1 us; the launch traced here: 25.9 us
  starting transfers between devices  13.5 us (52%)
  Pallas kernels  8.25 us (32%)
  waiting for transfers between devices  2.82 us (11%)
  between operations  0.73 us (3%)
  other arithmetic  0.65 us (2%)
    ppermute x10, starting transfers between devices, exchange(): return lax.ppermute(x, axes, [(i, i ^ step) for i in range(peers)])  13.5 us
    pallas_call x1, Pallas kernels, gathered_plan(): pl.pallas_call(main_kernel, out_shape=(jax.ShapeDtypeStruct((frames * col...  3.28 us
    ppermute x10, waiting for transfers between devices, exchange(): return lax.ppermute(x, axes, [(i, i ^ step) for i in range(peers)])  2.82 us
    pallas_call x1, Pallas kernels, stage(): pl.pallas_call(stage_kernel, out_shape=tuple(shapes), in_specs=[pl.BlockS...  2.45 us
    pallas_call x1, Pallas kernels, gathered_plan(): pl.pallas_call(functools.partial(mine_kernel, layout=(frames, cols, rows,...  1.28 us
    pallas_call x1, Pallas kernels, gathered_plan(): pl.pallas_call(own_kernel, out_shape=(jax.ShapeDtypeStruct((frames, 1, co...  1.18 us
    convert_element_type x1, other arithmetic, gathered_plan(): total.astype(jnp.bfloat16).reshape(frames, 1, cols, out_channels)  0.65 us
  transfers between devices with their start and end apart: 10, of which 3 were waited for; matrix products, arithmetic and copies ran while one was open for 0% of the time, Pallas kernels for 19%

profile of v8, /device:TPU:0, one launch (start us, length us, event | category | flops | bytes accessed | tf_op | source)
XLA Modules:
  0.0 25.9 jit_solution(11394245019372333685)
XLA Ops:
  0.6 5.1 %collective-permute-start.5 = (bf16[128,256]{1,0:T(8,128)(2,1)}, bf16[128,256]{1,0:T(8,128)(2,1)S(1)}, u32[]{:S(2)}, u32[]{:S(2)}) collective-permute-start(bf16[128,256]{1,0:T(8,128)(2,1)} %bitcast.6), channel_id=1, source_target_pairs={{0,12},{4,8},{8,4},{12,0},{1,13},{5,9},{9,5},{13,1},{2,14},{6,10},... | collective-permute-start | bytes 196616 | tf_op jit(solution)/shard_map/ppermute | solution.py:139
  5.7 0.0 collective-permute-start
  5.7 1.7 %collective-permute-start.3 = (bf16[128,256]{1,0:T(8,128)(2,1)}, bf16[128,256]{1,0:T(8,128)(2,1)S(1)}, u32[]{:S(2)}, u32[]{:S(2)}) collective-permute-start(bf16[128,256]{1,0:T(8,128)(2,1)} %bitcast.8), channel_id=1, source_target_pairs={{0,6},{2,4},{4,2},{6,0},{8,14},{10,12},{12,10},{14,8},{1,7},{3,5},... | collective-permute-start | bytes 196616 | tf_op jit(solution)/shard_map/ppermute | solution.py:139
  7.5 1.2 %collective-permute-start.2 = (bf16[128,256]{1,0:T(8,128)(2,1)}, bf16[128,256]{1,0:T(8,128)(2,1)S(1)}, u32[]{:S(2)}, u32[]{:S(2)}) collective-permute-start(bf16[128,256]{1,0:T(8,128)(2,1)} %bitcast.9), channel_id=1, source_target_pairs={{0,4},{4,0},{8,12},{12,8},{1,5},{5,1},{9,13},{13,9},{2,6},{6,2},{1... | collective-permute-start | bytes 196616 | tf_op jit(solution)/shard_map/ppermute | solution.py:139
  8.7 0.5 %collective-permute-start.1 = (bf16[128,256]{1,0:T(8,128)(2,1)}, bf16[128,256]{1,0:T(8,128)(2,1)S(1)}, u32[]{:S(2)}, u32[]{:S(2)}) collective-permute-start(bf16[128,256]{1,0:T(8,128)(2,1)} %bitcast.10), channel_id=1, source_target_pairs={{0,2},{2,0},{1,3},{3,1},{4,6},{6,4},{5,7},{7,5},{8,10},{10,8},{9,1... | collective-permute-start | bytes 196616 | tf_op jit(solution)/shard_map/ppermute | solution.py:139
  9.2 0.0 collective-permute-done.5.refs_2_
  9.2 1.5 %collective-permute-start.6 = (bf16[128,256]{1,0:T(8,128)(2,1)S(1)}, bf16[128,256]{1,0:T(8,128)(2,1)S(1)}, u32[]{:S(2)}, u32[]{:S(2)}) collective-permute-start(bf16[128,256]{1,0:T(8,128)(2,1)S(1)} %collective-permute-done.5.refs_2_), channel_id=1, source_target_pairs={{0,2},{2,0},{1,3},{3,1},{4,6},{6,4},{5,7},{7,5},{8,10},{10,8},{9,1... | collective-permute-start | bytes 196616 | tf_op jit(solution)/shard_map/ppermute | solution.py:139
  10.7 0.9 %collective-permute-done._.refs_0_ = bf16[128,256]{1,0:T(8,128)(2,1)S(1)} collective-permute-done((bf16[128,256]{1,0:T(8,128)(2,1)}, bf16[128,256]{1,0:T(8,128)(2,1)S(1)}, u32[]{:S(2)}, u32[]{:S(2)}) %collective-permute-start) | collective-permute-done | bytes 65568 | tf_op jit(solution)/shard_map/ppermute | solution.py:139
  11.7 1.5 %collective-permute-start.4 = (bf16[128,256]{1,0:T(8,128)(2,1)S(1)}, bf16[128,256]{1,0:T(8,128)(2,1)S(1)}, u32[]{:S(2)}, u32[]{:S(2)}) collective-permute-start(bf16[128,256]{1,0:T(8,128)(2,1)S(1)} %collective-permute-done._.refs_0_), channel_id=1, source_target_pairs={{0,2},{2,0},{1,3},{3,1},{4,6},{6,4},{5,7},{7,5},{8,10},{10,8},{9,1... | collective-permute-start | bytes 196616 | tf_op jit(solution)/shard_map/ppermute | solution.py:139
  13.2 2.4 %stage.1 = (bf16[512,512]{1,0:T(8,128)(2,1)S(1)}, bf16[512,512]{1,0:T(8,128)(2,1)S(1)}, bf16[512,512]{1,0:T(8,128)(2,1)S(1)}, bf16[512,256]{1,0:T(8,128)(2,1)S(1...) custom-call(bf16[512,512]{1,0:T(8,128)(2,1)} %query_hbm.1, ...), custom_call_target="tpu_custom_call" | custom-call | tf_op jit(solution)/shard_map/stage/pallas_call | solution.py:172
  15.6 0.0 collective-permute-done.3.refs_3_
  15.6 0.0 collective-permute-done.2.refs_2_
  15.6 0.0 collective-permute-done.1.refs_1_
  15.7 0.1 collective-permute-start.7
  15.8 0.0 collective-permute-done.6.refs_3_
  15.8 0.1 collective-permute-done.4.refs_1_
  15.9 0.4 %collective-permute-start.8 = (bf16[512,256]{1,0:T(8,128)(2,1)S(1)}, bf16[512,256]{1,0:T(8,128)(2,1)S(1)}, u32[]{:S(2)}, u32[]{:S(2)}) collective-permute-start(bf16[512,256]{1,0:T(8,128)(2,1)S(1)} %far.1.far_ref), channel_id=1, source_target_pairs={{0,1},{1,0},{2,3},{3,2},{4,5},{5,4},{6,7},{7,6},{8,9},{9,8},{10,11... | collective-permute-start | bytes 786440 | tf_op jit(solution)/shard_map/ppermute | solution.py:139
  16.4 1.3 %mine.1 = (f32[1024,512]{1,0:T(8,128)S(1)}, f32[1024,512]{1,0:T(8,128)S(1)}, f32[1024,512]{1,0:T(8,128)S(1)}, bf16[1,3,3,256,256]{4,3,2,1,0:T(8,128)(2,1)S(1)}) custom-call(bf16[528,256]{1,0:T(8,128)(2,1)S(1)} %near.1.near_ref, bf16[512,256]{1,0:T(8,128)(2,1)S(1)} %far.1.far_ref, bf16[512,512]{1,0:T(8,128)(2,1)S(1)} %get-tuple-element.23.query_ref, ...), custom_call_target="tpu_custom_call" | custom-call | tf_op jit(solution)/shard_map/mine/pallas_call | solution.py:423
  17.6 0.0 collective-permute-done.7.other_near_ref
  17.7 0.0 collective-permute-done.8.other_far_ref
  17.7 3.3 %block.1 = (bf16[128,512]{1,0:T(8,128)(2,1)S(1)}, bf16[3,6,64,256]{3,2,1,0:T(8,128)(2,1)S(1)}, bf16[128,256]{1,0:T(8,128)(2,1)S(1)}) custom-call(bf16[528,256]{1,0:T(8,128)(2,1)S(1)} %near.1.near_ref, bf16[512,256]{1,0:T(8,128)(2,1)S(1)} %far.1.far_ref, bf16[528,256]{1,0:T(8,128)(2,1)S(1)} %collective-permute-done.7.other_near_ref, ...), custom_call_target="tpu_custom_call" | custom-call | tf_op jit(solution)/shard_map/block/pallas_call | solution.py:433
  21.0 1.4 %collective-permute-start.9 = (bf16[128,256]{1,0:T(8,128)(2,1)S(1)}, bf16[128,256]{1,0:T(8,128)(2,1)S(1)}, u32[]{:S(2)}, u32[]{:S(2)}) collective-permute-start(bf16[128,256]{1,0:T(8,128)(2,1)S(1)} %get-tuple-element.37), channel_id=1, source_target_pairs={{0,2},{2,0},{1,3},{3,1},{4,6},{6,4},{5,7},{7,5},{8,10},{10,8},{9,1... | collective-permute-start | bytes 196616 | tf_op jit(solution)/shard_map/ppermute | solution.py:139
  22.4 1.2 %own.1 = (bf16[2,1,64,256]{3,2,1,0:T(8,128)(2,1)}, f32[128,256]{1,0:T(8,128)S(1)}) custom-call(bf16[3,6,64,256]{3,2,1,0:T(8,128)(2,1)S(1)} %get-tuple-element.32.activated, bf16[2,3,3,256,256]{4,3,2,1,0:T(8,128)(2,1)S(1)} %get-tuple-element.30.early_taps, bf16[1,3,3,256,256]{4,3,2,1,0:T(8,128)(2,1)S(1)} %get-tuple-element.31.last_tap, ...), custom_call_target="tpu_custom_call" | custom-call | tf_op jit(solution)/shard_map/own/pallas_call | solution.py:450
  23.6 1.7 %collective-permute-done.9 = bf16[128,256]{1,0:T(8,128)(2,1)S(1)} collective-permute-done((bf16[128,256]{1,0:T(8,128)(2,1)S(1)}, bf16[128,256]{1,0:T(8,128)(2,1)S(1)}, u32[]{:S(2)}, u32[]{:S(2)}) %collective-permute-start.9) | collective-permute-done | bytes 65568 | tf_op jit(solution)/shard_map/ppermute | solution.py:139
  25.3 0.6 %add_convert_fusion = bf16[128,256]{1,0:T(8,128)(2,1)} fusion(f32[128,256]{1,0:T(8,128)S(1)} %get-tuple-element.36, bf16[128,256]{1,0:T(8,128)(2,1)S(1)} %collective-permute-done.9), kind=kLoop, calls=%fused_computation | loop fusion | flops 98304 | bytes 262144 | tf_op jit(solution)/shard_map/convert_element_type | solution.py:463
  (2 shorter events, 0.1 us)
Async XLA Ops:
  0.6 8.6 %collective-permute-start.5 = (bf16[128,256]{1,0:T(8,128)(2,1)}, bf16[128,256]{1,0:T(8,128)(2,1)S(1)}, u32[]{:S(2)}, u32[]{:S(2)}) collective-permute-start(bf16[128,256]{1,0:T(8,128)(2,1)} %bitcast.6), channel_id=1, source_target_pairs={{0,12},{4,8},{8,4},{12,0},{1,13},{5,9},{9,5},{13,1},{2,14},{6,10},... | collective-permute-start | bytes 196616 | tf_op jit(solution)/shard_map/ppermute | solution.py:139
  5.7 5.9 %collective-permute-start = (bf16[128,256]{1,0:T(8,128)(2,1)}, bf16[128,256]{1,0:T(8,128)(2,1)S(1)}, u32[]{:S(2)}, u32[]{:S(2)}) collective-permute-start(bf16[128,256]{1,0:T(8,128)(2,1)} %bitcast.7), channel_id=1, source_target_pairs={{0,8},{4,12},{8,0},{12,4},{1,9},{5,13},{9,1},{13,5},{2,10},{6,14},... | collective-permute-start | bytes 196616 | tf_op jit(solution)/shard_map/ppermute | solution.py:139
  5.7 9.9 %collective-permute-start.3 = (bf16[128,256]{1,0:T(8,128)(2,1)}, bf16[128,256]{1,0:T(8,128)(2,1)S(1)}, u32[]{:S(2)}, u32[]{:S(2)}) collective-permute-start(bf16[128,256]{1,0:T(8,128)(2,1)} %bitcast.8), channel_id=1, source_target_pairs={{0,6},{2,4},{4,2},{6,0},{8,14},{10,12},{12,10},{14,8},{1,7},{3,5},... | collective-permute-start | bytes 196616 | tf_op jit(solution)/shard_map/ppermute | solution.py:139
  7.5 8.2 %collective-permute-start.2 = (bf16[128,256]{1,0:T(8,128)(2,1)}, bf16[128,256]{1,0:T(8,128)(2,1)S(1)}, u32[]{:S(2)}, u32[]{:S(2)}) collective-permute-start(bf16[128,256]{1,0:T(8,128)(2,1)} %bitcast.9), channel_id=1, source_target_pairs={{0,4},{4,0},{8,12},{12,8},{1,5},{5,1},{9,13},{13,9},{2,6},{6,2},{1... | collective-permute-start | bytes 196616 | tf_op jit(solution)/shard_map/ppermute | solution.py:139
  8.7 6.9 %collective-permute-start.1 = (bf16[128,256]{1,0:T(8,128)(2,1)}, bf16[128,256]{1,0:T(8,128)(2,1)S(1)}, u32[]{:S(2)}, u32[]{:S(2)}) collective-permute-start(bf16[128,256]{1,0:T(8,128)(2,1)} %bitcast.10), channel_id=1, source_target_pairs={{0,2},{2,0},{1,3},{3,1},{4,6},{6,4},{5,7},{7,5},{8,10},{10,8},{9,1... | collective-permute-start | bytes 196616 | tf_op jit(solution)/shard_map/ppermute | solution.py:139
  9.2 6.5 %collective-permute-start.6 = (bf16[128,256]{1,0:T(8,128)(2,1)S(1)}, bf16[128,256]{1,0:T(8,128)(2,1)S(1)}, u32[]{:S(2)}, u32[]{:S(2)}) collective-permute-start(bf16[128,256]{1,0:T(8,128)(2,1)S(1)} %collective-permute-done.5.refs_2_), channel_id=1, source_target_pairs={{0,2},{2,0},{1,3},{3,1},{4,6},{6,4},{5,7},{7,5},{8,10},{10,8},{9,1... | collective-permute-start | bytes 196616 | tf_op jit(solution)/shard_map/ppermute | solution.py:139
  11.7 4.3 %collective-permute-start.4 = (bf16[128,256]{1,0:T(8,128)(2,1)S(1)}, bf16[128,256]{1,0:T(8,128)(2,1)S(1)}, u32[]{:S(2)}, u32[]{:S(2)}) collective-permute-start(bf16[128,256]{1,0:T(8,128)(2,1)S(1)} %collective-permute-done._.refs_0_), channel_id=1, source_target_pairs={{0,2},{2,0},{1,3},{3,1},{4,6},{6,4},{5,7},{7,5},{8,10},{10,8},{9,1... | collective-permute-start | bytes 196616 | tf_op jit(solution)/shard_map/ppermute | solution.py:139
  15.7 2.0 %collective-permute-start.7 = (bf16[528,256]{1,0:T(8,128)(2,1)S(1)}, bf16[528,256]{1,0:T(8,128)(2,1)S(1)}, u32[]{:S(2)}, u32[]{:S(2)}) collective-permute-start(bf16[528,256]{1,0:T(8,128)(2,1)S(1)} %near.1.near_ref), channel_id=1, source_target_pairs={{0,1},{1,0},{2,3},{3,2},{4,5},{5,4},{6,7},{7,6},{8,9},{9,8},{10,11... | collective-permute-start | bytes 811016 | tf_op jit(solution)/shard_map/ppermute | solution.py:139
  15.9 1.7 %collective-permute-start.8 = (bf16[512,256]{1,0:T(8,128)(2,1)S(1)}, bf16[512,256]{1,0:T(8,128)(2,1)S(1)}, u32[]{:S(2)}, u32[]{:S(2)}) collective-permute-start(bf16[512,256]{1,0:T(8,128)(2,1)S(1)} %far.1.far_ref), channel_id=1, source_target_pairs={{0,1},{1,0},{2,3},{3,2},{4,5},{5,4},{6,7},{7,6},{8,9},{9,8},{10,11... | collective-permute-start | bytes 786440 | tf_op jit(solution)/shard_map/ppermute | solution.py:139
  21.0 4.3 %collective-permute-start.9 = (bf16[128,256]{1,0:T(8,128)(2,1)S(1)}, bf16[128,256]{1,0:T(8,128)(2,1)S(1)}, u32[]{:S(2)}, u32[]{:S(2)}) collective-permute-start(bf16[128,256]{1,0:T(8,128)(2,1)S(1)} %get-tuple-element.37), channel_id=1, source_target_pairs={{0,2},{2,0},{1,3},{3,1},{4,6},{6,4},{5,7},{7,5},{8,10},{10,8},{9,1... | collective-permute-start | bytes 196616 | tf_op jit(solution)/shard_map/ppermute | solution.py:139
